TPU v7x, 32 devices: a whole 2x2x4 slice. The times are simulated.
32 devices in a mesh: expert: 8 (over z, x), shard: 4 (over y, core).
Axes of the slice: x: 2, y: 2, z: 4, core: 2. Of those that a mesh axis runs over, the one named last changes fastest.
Arguments:
- tokens: bfloat16 [192, 197, 768], P(('expert', 'shard')), may hold values from -6 to 6
- ln1_gain: bfloat16 [768], P('shard'), may hold values from 0.5 to 1.5
- ln1_bias: bfloat16 [768], P('shard'), may hold values from -1.796875 to 1.796875
- qkv_weight: bfloat16 [768, 2304], P('shard'), may hold values from -0.3125 to 0.3125
- out_weight: bfloat16 [768, 768], P('shard'), may hold values from -1.25 to 1.25
- ln2_gain: bfloat16 [768], P('shard'), may hold values from 0.5 to 1.5
- ln2_bias: bfloat16 [768], P('shard'), may hold values from -1.796875 to 1.796875
- router_weight: bfloat16 [768, 8], P('shard'), may hold values from -0.15625 to 0.15625
- up_weight: bfloat16 [3072, 8, 768], P('shard', 'expert'), may hold values from -0.21875 to 0.21875
- down_weight: bfloat16 [3072, 8, 768], P('shard', 'expert'), may hold values from -0.4375 to 0.4375
- routes: int32 [192, 197, 2], P(('expert', 'shard')), may hold values from 0 to 7, as said below
- slots: int32 [192, 197, 2], P(('expert', 'shard')), may hold values from 0 to 368, as said below
- keep: int32 [192, 197, 2], P(('expert', 'shard')), may hold values from 0 to 1, as said below
- cotangent: bfloat16 [192, 197, 768], P(('expert', 'shard')), may hold values from -6 to 6
Outputs:
- block_out: bfloat16 [192, 197, 768], P(('expert', 'shard'))
- tokens_grad: bfloat16 [192, 197, 768], P(('expert', 'shard'))
- ln1_gain_grad: float32 [768], P('shard')
- ln1_bias_grad: float32 [768], P('shard')
- qkv_grad: float32 [768, 2304], P('shard')
- out_grad: float32 [768, 768], P('shard')
- ln2_gain_grad: float32 [768], P('shard')
- ln2_bias_grad: float32 [768], P('shard')
- router_grad: float32 [768, 8], P('shard')
- up_grad: float32 [3072, 8, 768], P('shard', 'expert')
- down_grad: float32 [3072, 8, 768], P('shard', 'expert')
Inputs may be any that keep to these rules, and one draw needn't show every extreme that they name: `routes`: each token names two different experts. Of the assignments (in order of token, then choice) that the tokens of one device make to one expert, the first 369 have keep 1 and slots 0, 1, 2, ... in that order; the later ones have keep 0 and slot 368. In every draw some expert receives 369 kept assignments from every device. `keep`: 1 exactly for the kept assignments described for slots.
All inputs are finite; a program needn't handle non-finite values.
Results may differ from a plain program's by a relative error of at most 0.014.
Values may be sent and summed in bfloat16 or wider, within the bound.
No kernel may reach another device: no remote copies, remote signals or barrier semaphores. Data moves between devices by JAX's collectives and lax.ppermute only.
A program may use at most 320 MiB of HBM per device.

v0:
```python
import jax
import jax.numpy as jnp
from jax import lax
from jax.sharding import PartitionSpec as P

HEADS = 12


EPSILON = 1e-06
HIGH = lax.Precision.HIGHEST


def layer_norm(value, gain, shift):
    mean = jnp.mean(value, -1, keepdims=True)
    centered = value - mean
    spread = jnp.mean(centered * centered, -1, keepdims=True)
    return centered * lax.rsqrt(spread + EPSILON) * gain + shift


def shards(
    tokens,
    ln1_gain,
    ln1_bias,
    qkv_weight,
    out_weight,
    ln2_gain,
    ln2_bias,
    router_weight,
    up_weight,
    down_weight,
    routes,
    slots,
    keep,
    cotangent,
):
    images, length, width = tokens.shape
    head_dim = width // HEADS
    rows = images * length
    experts_here = up_weight.shape[1]
    owners = lax.axis_size("expert")
    all_experts = experts_here * owners
    capacity = max(4, 5 * rows // (2 * all_experts))
    spread = owners * capacity
    empty_slot = experts_here * spread
    scale = head_dim ** (-0.5)
    flat = tokens.reshape(rows, width).astype(jnp.float32)
    gain1, bias1, w_qkv, w_out, gain2, bias2, w_router = (
        lax.all_gather(ln1_gain, "shard", axis=0, tiled=True),
        lax.all_gather(ln1_bias, "shard", axis=0, tiled=True),
        lax.all_gather(qkv_weight, "shard", axis=0, tiled=True),
        lax.all_gather(out_weight, "shard", axis=0, tiled=True),
        lax.all_gather(ln2_gain, "shard", axis=0, tiled=True),
        lax.all_gather(ln2_bias, "shard", axis=0, tiled=True),
        lax.all_gather(router_weight, "shard", axis=0, tiled=True),
    )
    normed1, norm1_back = jax.vjp(
        layer_norm, flat, gain1.astype(jnp.float32), bias1.astype(jnp.float32)
    )
    first_in = normed1.astype(jnp.bfloat16)
    qkv = jnp.dot(first_in, w_qkv, preferred_element_type=jnp.float32).astype(jnp.bfloat16)
    split = qkv.reshape(images, length, 3, HEADS, head_dim)
    query, key_part, value_part = (split[:, :, 0], split[:, :, 1], split[:, :, 2])
    scores = (
        jnp.einsum("iqhc,ikhc->ihqk", query, key_part, preferred_element_type=jnp.float32) * scale
    )
    highest = jnp.max(scores, -1, keepdims=True)
    raised = jnp.exp(scores - highest)
    total = jnp.sum(raised, -1, keepdims=True)
    log_total = highest + jnp.log(total)
    probs_low = (raised / total).astype(jnp.bfloat16)
    mixed = jnp.einsum("ihqk,ikhc->iqhc", probs_low, value_part, preferred_element_type=jnp.float32)
    mixed_low = mixed.reshape(rows, width).astype(jnp.bfloat16)
    attended = flat + jnp.dot(mixed_low, w_out, preferred_element_type=jnp.float32)
    normed2, norm2_back = jax.vjp(
        layer_norm, attended, gain2.astype(jnp.float32), bias2.astype(jnp.float32)
    )
    second_in = normed2.astype(jnp.bfloat16)
    logits = jnp.dot(second_in, w_router, preferred_element_type=jnp.float32)
    route_rows = routes.reshape(rows, 2)
    slot_rows = slots.reshape(rows, 2)
    keep_rows = keep.reshape(rows, 2).astype(jnp.float32)
    table = (
        route_rows[:, :, None] == jnp.arange(all_experts, dtype=jnp.int32)[None, None, :]
    ).astype(jnp.float32)

    def gating(values):
        return jnp.sum(jax.nn.softmax(values, -1)[:, None, :] * table, -1) * keep_rows

    gates, gate_back = jax.vjp(gating, logits)
    position = (
        route_rows % experts_here * spread + route_rows // experts_here * capacity + slot_rows
    )
    position = jnp.where(keep_rows > 0, position, empty_slot).reshape(-1)

    def to_slots(values):
        filled = (
            jnp.zeros((empty_slot + 1, width), jnp.bfloat16)
            .at[position]
            .set(values.reshape(rows * 2, width))
        )
        return filled[:empty_slot].reshape(experts_here, spread, width)

    def from_slots(values):
        padded = jnp.concatenate(
            [values.reshape(empty_slot, width), jnp.zeros((1, width), values.dtype)], 0
        )
        return padded[position].reshape(rows, 2, width)

    arrived = lax.all_to_all(
        to_slots(jnp.broadcast_to(second_in[:, None, :], (rows, 2, width))),
        "expert",
        split_axis=1,
        concat_axis=1,
        tiled=True,
    )
    w_up, w_down = (
        lax.all_gather(up_weight, "shard", axis=0, tiled=True),
        lax.all_gather(down_weight, "shard", axis=0, tiled=True),
    )
    part = w_up.shape[0] // 4
    produced = jnp.zeros((experts_here, spread, width), jnp.float32)
    for block in range(4):
        up_part = w_up[block * part : (block + 1) * part]
        down_part = w_down[block * part : (block + 1) * part]
        before = jnp.einsum("erd,fed->erf", arrived, up_part, preferred_element_type=jnp.float32)
        active = jax.nn.gelu(before).astype(jnp.bfloat16)
        produced = produced + jnp.einsum(
            "erf,fed->erd", active, down_part, preferred_element_type=jnp.float32
        )
    returned = lax.all_to_all(
        produced.astype(jnp.bfloat16), "expert", split_axis=1, concat_axis=1, tiled=True
    )
    picked = from_slots(returned).astype(jnp.float32)
    output = attended + jnp.sum(gates[:, :, None] * picked, 1)
    block_out = output.astype(jnp.bfloat16).reshape(images, length, width)
    grad_out = cotangent.reshape(rows, width).astype(jnp.float32)
    gate_grad = jnp.sum(grad_out[:, None, :] * picked, -1)
    (logit_grad,) = gate_back(gate_grad)
    back_rows = (gates[:, :, None] * grad_out[:, None, :]).astype(jnp.bfloat16)
    arrived_grad = lax.all_to_all(
        to_slots(back_rows), "expert", split_axis=1, concat_axis=1, tiled=True
    )
    w_up, w_down = (
        lax.all_gather(up_weight, "shard", axis=0, tiled=True),
        lax.all_gather(down_weight, "shard", axis=0, tiled=True),
    )
    up_blocks = []
    down_blocks = []
    input_grad = jnp.zeros((experts_here, spread, width), jnp.float32)
    for block in range(4):
        up_part = w_up[block * part : (block + 1) * part]
        down_part = w_down[block * part : (block + 1) * part]
        before = jnp.einsum("erd,fed->erf", arrived, up_part, preferred_element_type=jnp.float32)
        active, slope = jax.vjp(jax.nn.gelu, before)
        active_grad = jnp.einsum(
            "erd,fed->erf", arrived_grad, down_part, preferred_element_type=jnp.float32
        )
        (before_grad,) = slope(active_grad)
        before_low = before_grad.astype(jnp.bfloat16)
        down_blocks.append(
            jnp.einsum(
                "erf,erd->fed",
                active.astype(jnp.bfloat16),
                arrived_grad,
                preferred_element_type=jnp.float32,
            )
        )
        up_blocks.append(
            jnp.einsum("erf,erd->fed", before_low, arrived, preferred_element_type=jnp.float32)
        )
        input_grad = input_grad + jnp.einsum(
            "erf,fed->erd", before_low, up_part, preferred_element_type=jnp.float32
        )
    up_grad, down_grad = (
        lax.psum_scatter(jnp.concatenate(up_blocks, 0), "shard", scatter_dimension=0, tiled=True),
        lax.psum_scatter(jnp.concatenate(down_blocks, 0), "shard", scatter_dimension=0, tiled=True),
    )
    returned_grad = lax.all_to_all(
        input_grad.astype(jnp.bfloat16), "expert", split_axis=1, concat_axis=1, tiled=True
    )
    router_f32 = w_router.astype(jnp.float32)
    second_grad = jnp.sum(from_slots(returned_grad).astype(jnp.float32), 1) + jnp.dot(
        logit_grad, router_f32.T, precision=HIGH
    )
    router_grad_full = jnp.dot(second_in.astype(jnp.float32).T, logit_grad, precision=HIGH)
    attended_part, gain2_grad, bias2_grad = norm2_back(second_grad)
    attended_grad = grad_out + attended_part
    branch_grad = attended_grad.astype(jnp.bfloat16)
    out_grad_full = jnp.dot(mixed_low.T, branch_grad, preferred_element_type=jnp.float32)
    mixed_grad = (
        jnp.dot(branch_grad, w_out.T, preferred_element_type=jnp.float32)
        .astype(jnp.bfloat16)
        .reshape(images, length, HEADS, head_dim)
    )
    scores = (
        jnp.einsum("iqhc,ikhc->ihqk", query, key_part, preferred_element_type=jnp.float32) * scale
    )
    probs = jnp.exp(scores - log_total)
    value_grad = jnp.einsum(
        "ihqk,iqhc->ikhc",
        probs.astype(jnp.bfloat16),
        mixed_grad,
        preferred_element_type=jnp.float32,
    )
    prob_grad = jnp.einsum(
        "iqhc,ikhc->ihqk", mixed_grad, value_part, preferred_element_type=jnp.float32
    )
    score_grad = (probs * (prob_grad - jnp.sum(probs * prob_grad, -1, keepdims=True))).astype(
        jnp.bfloat16
    )
    query_grad = (
        jnp.einsum("ihqk,ikhc->iqhc", score_grad, key_part, preferred_element_type=jnp.float32)
        * scale
    )
    key_grad = (
        jnp.einsum("ihqk,iqhc->ikhc", score_grad, query, preferred_element_type=jnp.float32) * scale
    )
    qkv_rows_grad = (
        jnp.stack([query_grad, key_grad, value_grad], 2)
        .reshape(rows, 3 * width)
        .astype(jnp.bfloat16)
    )
    qkv_grad_full = jnp.dot(first_in.T, qkv_rows_grad, preferred_element_type=jnp.float32)
    first_grad = jnp.dot(qkv_rows_grad, w_qkv.T, preferred_element_type=jnp.float32)
    token_part, gain1_grad, bias1_grad = norm1_back(first_grad)
    tokens_grad = (attended_grad + token_part).astype(jnp.bfloat16).reshape(images, length, width)
    layer_grads = (
        gain1_grad,
        bias1_grad,
        qkv_grad_full,
        out_grad_full,
        gain2_grad,
        bias2_grad,
        router_grad_full,
    )
    summed = lax.psum(
        (
            layer_grads[0],
            layer_grads[1],
            layer_grads[2],
            layer_grads[3],
            layer_grads[4],
            layer_grads[5],
            layer_grads[6],
        ),
        "expert",
    )
    shares = (
        lax.psum_scatter(summed[0], "shard", scatter_dimension=0, tiled=True),
        lax.psum_scatter(summed[1], "shard", scatter_dimension=0, tiled=True),
        lax.psum_scatter(summed[2], "shard", scatter_dimension=0, tiled=True),
        lax.psum_scatter(summed[3], "shard", scatter_dimension=0, tiled=True),
        lax.psum_scatter(summed[4], "shard", scatter_dimension=0, tiled=True),
        lax.psum_scatter(summed[5], "shard", scatter_dimension=0, tiled=True),
        lax.psum_scatter(summed[6], "shard", scatter_dimension=0, tiled=True),
    )
    return (
        block_out,
        tokens_grad,
        shares[0],
        shares[1],
        shares[2],
        shares[3],
        shares[4],
        shares[5],
        shares[6],
        up_grad,
        down_grad,
    )


def solution(mesh):
    placed = (
        P(("expert", "shard"), None, None),
        P("shard"),
        P("shard"),
        P("shard", None),
        P("shard", None),
        P("shard"),
        P("shard"),
        P("shard", None),
        P("shard", "expert", None),
        P("shard", "expert", None),
        P(("expert", "shard"), None, None),
        P(("expert", "shard"), None, None),
        P(("expert", "shard"), None, None),
        P(("expert", "shard"), None, None),
    )
    return jax.shard_map(
        shards,
        mesh=mesh,
        in_specs=placed,
        out_specs=(
            P(("expert", "shard"), None, None),
            P(("expert", "shard"), None, None),
            P("shard"),
            P("shard"),
            P("shard", None),
            P("shard", None),
            P("shard"),
            P("shard"),
            P("shard", None),
            P("shard", "expert", None),
            P("shard", "expert", None),
        ),
        check_vma=False,
    )
```

profile of v0, /device:TPU:0, one launch (start us, length us, event | category | flops | bytes accessed | tf_op | source)
XLA Modules:
  0.0 1409.4 jit_solution(14446444412430654195)
XLA Ops:
  17.4 8.9 all-reduce.13
  37.7 7.3 mul.504
  45.0 10.0 mul.505
  55.0 10.3 convolution_convert_fusion
  65.3 17.4 %reshape.586 = bf16[6,197,3,12,64]{4,3,2,1,0:T(8,128)(2,1)} reshape(bf16[1182,2304]{1,0:T(8,128)(2,1)} %convolution_convert_fusion) | data formatting | bytes 10893312 | tf_op jit(solution)/shard_map/reshape | solution.py:61
  82.7 11.4 fusion.148
  94.1 6.7 copy.189
  106.5 7.5 copy.188
  114.0 9.0 multiply_reduce_fusion.1
  123.0 8.9 fusion
  132.0 8.6 convert_bitcast_fusion
  155.5 24.3 %scatter_custom_fusion.1 = bf16[2953,768]{1,0:T(8,128)(2,1)} fusion(s32[2364]{0:T(1024)S(1)} %fusion.140, f32[2364,768]{1,0:T(8,128)} %mul.505, f32[2364]{0:T(1024)S(1)} %mul.502, bf16[]{:T(256)} %constant.63.clone.1), kind=kCustom, calls=%fused_computation.111 | custom fusion | flops 3631104 | bytes 11810306 | tf_op jit(solution)/shard_map/scatter | solution.py:99
  182.4 27.4 %copy.200 = bf16[1,2952,768]{2,0,1:T(2,128)(2,1)} copy(bf16[1,2952,768]{2,1,0:T(8,128)(2,1)S(1)} %slice_bitcast_fusion) | data formatting | bytes 9068544 | tf_op jit(solution)/shard_map/reshape | solution.py:101
  210.4 29.0 %reduce.9 = bf16[2952,768]{1,0:T(8,128)(2,1)} reduce(bf16[2952,1,768]{2,1,0:T(2,128)(2,1)} %bitcast.232, bf16[]{:T(256)} %broadcast.428), dimensions={1}, to_apply=%bitcast.229.reduce_sub_computation | reduce | bytes 9068546
  251.4 8.6 broadcast_in_dim.18
  260.1 8.8 reshape.546
  268.9 16.7 %scatter_custom_fusion = bf16[2953,768]{1,0:T(8,128)(2,1)} fusion(s32[2364]{0:T(1024)S(1)} %fusion.140, bf16[2364,768]{1,0:T(8,128)(2,1)} %reshape.546, bf16[]{:T(256)} %constant.63.clone.1), kind=kCustom, calls=%fused_computation.138 | custom fusion | bytes 4536320 | tf_op jit(solution)/shard_map/scatter | solution.py:99
  288.2 27.3 %copy.202 = bf16[1,2952,768]{2,0,1:T(2,128)(2,1)} copy(bf16[1,2952,768]{2,1,0:T(8,128)(2,1)S(1)} %slice_bitcast_fusion.1) | data formatting | bytes 9068544 | tf_op jit(solution)/shard_map/reshape | solution.py:101
  315.5 29.0 %reduce.8 = bf16[2952,768]{1,0:T(8,128)(2,1)} reduce(bf16[2952,1,768]{2,1,0:T(2,128)(2,1)} %bitcast.234, bf16[]{:T(256)} %broadcast.428), dimensions={1}, to_apply=%bitcast.231.reduce_sub_computation | reduce | bytes 9068546
  356.9 15.6 %reshape.598 = bf16[2952,1,768]{2,1,0:T(2,128)(2,1)} reshape(bf16[8,2,141696]{2,1,0:T(2,128)(2,1)} %all-to-all-done.2) | data formatting | bytes 9068544
  372.5 6.6 copy.186
  379.2 77.2 %all-to-all-done = bf16[8,2,141696]{2,1,0:T(2,128)(2,1)} async-done(((bf16[8,2,141696]{2,1,0:T(2,128)(2,1)}), bf16[8,2,141696]{2,1,0:T(2,128)(2,1)}, u32[]{:S(2)}, u32[]{:S(2)}) %all-to-all-start) | async-done | bytes 4534304 | tf_op jit(solution)/shard_map/all_to_all | solution.py:109
  456.4 15.6 %reshape.594 = bf16[2952,1,768]{2,1,0:T(2,128)(2,1)} reshape(bf16[8,2,141696]{2,1,0:T(2,128)(2,1)} %all-to-all-done) | data formatting | bytes 9068544
  478.5 10.0 fusion.65
  507.0 12.9 fusion.130
  519.9 12.7 fusion.132
  532.7 7.9 fusion.134
  540.6 14.9 %fusion.67 = bf16[1,2952,768]{2,1,0:T(8,128)(2,1)S(1)} fusion(f32[2952,768]{1,0:T(8,128)} %fusion.134, f32[2952,768]{1,0:T(8,128)} %fusion.130, f32[2952,768]{1,0:T(8,128)} %fusion.132, bf16[3072,1,768]{2,0,1:T(8,128)(2,1)} %all-gather.12.cloned.1.call-done, f32[2952,768]{1,0:T(8,128)} %fusion.59), kind=kOutput, calls=%fused_computation.105 | convolution fusion | flops 3511793664 | bytes 41988096 | tf_op jit(solution)/shard_map/erf,fed->erd/dot_general | solution.py:127
  555.5 27.3 %copy.201 = bf16[1,2952,768]{2,0,1:T(2,128)(2,1)} copy(bf16[1,2952,768]{2,1,0:T(8,128)(2,1)S(1)} %fusion.67) | data formatting | bytes 9068544 | tf_op jit(solution)/shard_map/convert_element_type | solution.py:131
  582.8 29.0 %reduce.11 = bf16[2952,768]{1,0:T(8,128)(2,1)} reduce(bf16[2952,1,768]{2,1,0:T(2,128)(2,1)} %bitcast.237, bf16[]{:T(256)} %broadcast.428), dimensions={1}, to_apply=%bitcast.230.reduce_sub_computation | reduce | bytes 9068546
  622.5 11.7 fusion.15
  634.3 12.0 fusion.8
  658.5 11.7 fusion.22
  670.2 9.6 fusion.133
  679.8 9.9 fusion.29
  689.7 14.6 %fusion.68 = bf16[1,2952,768]{2,1,0:T(8,128)(2,1)S(1)} fusion(bf16[2952,768]{1,0:T(8,128)(2,1)} %fusion.29, f32[2952,768]{1,0:T(8,128)} %fusion.133, f32[2952,768]{1,0:T(8,128)} %fusion.129, f32[2952,768]{1,0:T(8,128)} %fusion.131, bf16[3072,1,768]{2,0,1:T(8,128)(2,1)} %all-gather.10.cloned.1.call-done), kind=kOutput, calls=%fused_computation.106 | convolution fusion | flops 3491389440 | bytes 37453824 | tf_op jit(solution)/shard_map/erf,fed->erd/dot_general | solution.py:171
  704.2 27.3 %copy.199 = bf16[1,2952,768]{2,0,1:T(2,128)(2,1)} copy(bf16[1,2952,768]{2,1,0:T(8,128)(2,1)S(1)} %fusion.68) | data formatting | bytes 9068544 | tf_op jit(solution)/shard_map/convert_element_type | solution.py:179
  731.5 29.0 %reduce.10 = bf16[2952,768]{1,0:T(8,128)(2,1)} reduce(bf16[2952,1,768]{2,1,0:T(2,128)(2,1)} %bitcast.233, bf16[]{:T(256)} %broadcast.428), dimensions={1}, to_apply=%bitcast.228.reduce_sub_computation | reduce | bytes 9068546
  778.0 16.0 %reshape.596 = bf16[2952,1,768]{2,1,0:T(2,128)(2,1)} reshape(bf16[8,2,141696]{2,1,0:T(2,128)(2,1)} %all-to-all-done.1) | data formatting | bytes 9068544
  800.7 13.1 gather_fusion
  813.8 9.1 reshape.523
  822.9 19.5 %multiply_reduce_fusion.2 = (f32[1182,2]{1,0:T(8,128)S(1)}, f32[1182,768]{1,0:T(8,128)}) fusion(f32[1182,2,768]{2,1,0:T(2,128)} %reshape.523, f32[1182,768]{1,0:T(8,128)} %reshape.524, f32[1182,2]{1,0:T(8,128)S(1)} %copy.156), kind=kLoop, calls=%fused_computation.63 | loop fusion | flops 6352068 | bytes 14543328 | tf_op jit(solution)/shard_map/reduce_sum | solution.py:137
  842.7 28.7 %all-to-all-done.3 = bf16[8,2,141696]{2,1,0:T(2,128)(2,1)} async-done(((bf16[8,2,141696]{2,1,0:T(2,128)(2,1)}), bf16[8,2,141696]{2,1,0:T(2,128)(2,1)}, u32[]{:S(2)}, u32[]{:S(2)}) %all-to-all-start.3) | async-done | bytes 4534304 | tf_op jit(solution)/shard_map/all_to_all | solution.py:178
  871.4 15.8 %reshape.600 = bf16[2952,1,768]{2,1,0:T(2,128)(2,1)} reshape(bf16[8,2,141696]{2,1,0:T(2,128)(2,1)} %all-to-all-done.3) | data formatting | bytes 9068544
  893.8 13.1 gather_fusion.1
  906.9 9.1 reshape.525
  916.0 11.7 reduce_sum.203
  957.5 12.6 multiply_reduce_fusion
  970.1 11.2 multiply_convert_fusion
  986.7 8.0 fusion.89
  1000.8 12.3 copy.171
  1013.2 14.7 %convert_element_type.226 = bf16[1182,2304]{0,1:T(8,128)(2,1)} reshape(bf16[6,197,3,12,64]{1,0,4,3,2:T(8,128)(2,1)} %copy.171) | data formatting | bytes 10893312 | tf_op jit(solution)/shard_map/convert_element_type | solution.py:221
  1027.9 9.7 fusion.153
  1037.7 10.0 fusion.117
  1047.7 12.3 fusion.120
  1075.5 7.4 pad_maximum_fusion.1
  1083.0 7.5 fusion.108
  1090.5 7.7 fusion.105
  1112.0 12.4 multiply_reduce_fusion.6
  1124.4 10.1 all-reduce.12
  1149.1 36.0 %all-reduce.10 = (f32[192]{0:T(256)}, f32[192]{0:T(256)}, f32[192]{0:T(256)}, f32[192]{0:T(256)}, f32[192,8]{0,1:T(8,128)}) all-reduce(f32[192]{0:T(256)S(1)} %dynamic-slice.5, f32[192]{0:T(256)S(1)} %dynamic-slice.7, f32[192]{0:T(256)S(1)} %dynamic-slice.9, ...), channel_id=1, replica_groups=mesh['expert'=8,'shard'=4] {'expert'}, use_global_device_ids=true, to_apply=%region_22.23 | all-reduce | flops 2304 | bytes 18432 | tf_op jit(solution)/shard_map/psum | solution.py:236
  1185.1 19.0 %reduce-scatter.10.cloned.1.call-done = f32[768,1,768]{2,0,1:T(8,128)} async-done(((f32[3072,1,768]{2,0,1:T(8,128)}), f32[768,1,768]{2,0,1:T(8,128)}) %reduce-scatter.10.cloned.1.call-update) | async-done | bytes 2359312 | tf_op jit(solution)/shard_map/reduce_scatter | solution.py:176
  1209.6 75.5 %reduce-scatter.8.cloned.1.call-done = f32[768,1,768]{2,0,1:T(8,128)} async-done(((f32[3072,1,768]{2,0,1:T(8,128)}), f32[768,1,768]{2,0,1:T(8,128)}) %reduce-scatter.8.cloned.1.call-update) | async-done | bytes 2359312 | tf_op jit(solution)/shard_map/reduce_scatter | solution.py:175
  1290.6 107.1 %all-reduce.16.cloned.1.call-done = (f32[192,2304]{1,0:T(8,128)}, f32[192,768]{1,0:T(8,128)}) async-done(((f32[192,2304]{1,0:T(8,128)}, f32[192,768]{1,0:T(8,128)}), (f32[192,2304]{1,0:T(8,128)}, f32[192,768]{1,0:T(8,128)})) %all-reduce.16.cloned.1.call-update) | async-done | bytes 2359312 | tf_op jit(solution)/shard_map/psum | solution.py:236
  (358 shorter events, 249.5 us)
Async XLA Ops:
  7.2 47.8 %all-gather.6.cloned.1.call-start = ((), (), s32[]{:S(2)}) async-start(), calls=%async_computation.9 | async-start | bytes 4423680 | tf_op jit(solution)/shard_map/all_gather | solution.py:50
  7.9 138.4 %all-gather.8.cloned.1.call-start = ((), (), s32[]{:S(2)}) async-start(), calls=%async_computation.10 | async-start | bytes 1474560 | tf_op jit(solution)/shard_map/all_gather | solution.py:51
  8.7 18.3 %copy-start.66 = (bf16[192,8]{0,1:T(8,128)(2,1)S(1)}, bf16[192,8]{0,1:T(8,128)(2,1)}, u32[]{:S(2)}) copy-start(bf16[192,8]{0,1:T(8,128)(2,1)} %param.21) | copy-start | bytes 9220
  8.8 23.8 %copy-start.51 = (s32[6,197,2]{1,2,0:T(2,128)S(1)}, s32[6,197,2]{1,2,0:T(2,128)}, u32[]{:S(2)}) copy-start(s32[6,197,2]{1,2,0:T(2,128)} %param.24) | copy-start | bytes 28372
  8.8 23.9 %copy-start.64 = (s32[6,197,2]{1,2,0:T(2,128)S(1)}, s32[6,197,2]{1,2,0:T(2,128)}, u32[]{:S(2)}) copy-start(s32[6,197,2]{1,2,0:T(2,128)} %param.26) | copy-start | bytes 28372
  8.8 23.9 %copy-start.65 = (s32[6,197,2]{1,2,0:T(2,128)S(1)}, s32[6,197,2]{1,2,0:T(2,128)}, u32[]{:S(2)}) copy-start(s32[6,197,2]{1,2,0:T(2,128)} %param.25) | copy-start | bytes 28372
  10.7 22.9 %copy-start.33 = (f32[6,197]{1,0:T(8,128)}, f32[6,197]{1,0:T(8,128)S(1)}, u32[]{:S(2)}) copy-start(f32[6,197]{1,0:T(8,128)S(1)} %broadcast_multiply_fusion.1) | copy-start | bytes 14188
  13.0 42.1 %copy-start.56 = (f32[1182]{0:T(1024)}, f32[1182]{0:T(1024)S(1)}, u32[]{:S(2)}) copy-start(f32[1182]{0:T(1024)S(1)} %div.73) | copy-start | bytes 14188
  26.3 28.8 %copy-start.52 = (f32[768]{0:T(1024)}, f32[768]{0:T(1024)S(1)}, u32[]{:S(2)}) copy-start(f32[768]{0:T(1024)S(1)} %convert_element_type.187) | copy-start | bytes 9220
  26.3 28.7 %copy-start.60 = (f32[768]{0:T(1024)}, f32[768]{0:T(1024)S(1)}, u32[]{:S(2)}) copy-start(f32[768]{0:T(1024)S(1)} %convert_element_type.188) | copy-start | bytes 9220
  27.0 28.0 %copy-start.58 = (f32[1182]{0:T(1024)}, f32[1182]{0:T(1024)S(1)}, u32[]{:S(2)}) copy-start(f32[1182]{0:T(1024)S(1)} %rsqrt.23) | copy-start | bytes 14188
  27.0 125.9 %copy-start.47 = (f32[768]{0:T(1024)}, f32[768]{0:T(1024)S(1)}, u32[]{:S(2)}) copy-start(f32[768]{0:T(1024)S(1)} %convert_element_type.195) | copy-start | bytes 9220
  32.6 121.0 %copy-start.35 = (bf16[768,8]{0,1:T(8,128)(2,1)}, bf16[768,8]{0,1:T(8,128)(2,1)S(1)}, u32[]{:S(2)}) copy-start(bf16[768,8]{0,1:T(8,128)(2,1)S(1)} %reshape.571) | copy-start | bytes 36868
  32.7 121.7 %copy-start.39 = (s32[1182,2]{0,1:T(2,128)}, s32[1182,2]{0,1:T(2,128)S(1)}, u32[]{:S(2)}) copy-start(s32[1182,2]{0,1:T(2,128)S(1)} %eq.17) | copy-start | bytes 28372
  32.7 12.2 copy-start.37
  33.9 234.9 %copy-start.49 = (s32[2364]{0:T(1024)}, s32[2364]{0:T(1024)S(1)}, u32[]{:S(2)}) copy-start(s32[2364]{0:T(1024)S(1)} %fusion.140) | copy-start | bytes 28372
  106.4 16.6 %copy-start.7 = (bf16[6,197,1,12,64]{1,4,3,0,2:T(8,128)(2,1)}, bf16[6,197,1,12,64]{1,4,3,0,2:T(8,128)(2,1)S(1)}, u32[]{:S(2)}) copy-start(bf16[6,197,1,12,64]{1,4,3,0,2:T(8,128)(2,1)S(1)} %copy.190) | copy-start | bytes 5446660
  153.6 97.8 %copy-start.5 = (bf16[1182,768]{1,0:T(8,128)(2,1)}, bf16[1182,768]{1,0:T(8,128)(2,1)S(1)}, u32[]{:S(2)}) copy-start(bf16[1182,768]{1,0:T(8,128)(2,1)S(1)} %add_convert_fusion.5) | copy-start | bytes 5446660
  154.9 24.9 %copy-start.41 = (f32[1182,2]{0,1:T(2,128)}, f32[1182,2]{0,1:T(2,128)S(1)}, u32[]{:S(2)}) copy-start(f32[1182,2]{0,1:T(2,128)S(1)} %select_reduce_fusion.1) | copy-start | bytes 28372
  244.9 106.8 %all-to-all-start.2 = ((bf16[8,2,141696]{2,1,0:T(2,128)(2,1)}), bf16[8,2,141696]{2,1,0:T(2,128)(2,1)}, u32[]{:S(2)}, u32[]{:S(2)}) async-start(bf16[8,2,141696]{2,1,0:T(2,128)(2,1)} %reshape.597), calls=%async_computation.2 | async-start | bytes 9068544 | tf_op jit(solution)/shard_map/all_to_all | solution.py:140
  250.7 227.8 %all-gather.10.cloned.1.call-start = ((), (), s32[]{:S(2)}) async-start(), calls=%async_computation.11 | async-start | bytes 5898240 | tf_op jit(solution)/shard_map/all_gather | solution.py:117
  351.7 104.7 %all-to-all-start = ((bf16[8,2,141696]{2,1,0:T(2,128)(2,1)}), bf16[8,2,141696]{2,1,0:T(2,128)(2,1)}, u32[]{:S(2)}, u32[]{:S(2)}) async-start(bf16[8,2,141696]{2,1,0:T(2,128)(2,1)} %reshape.593), calls=%async_computation | async-start | bytes 9068544 | tf_op jit(solution)/shard_map/all_to_all | solution.py:109
  356.3 150.6 %all-gather.12.cloned.1.call-start = ((), (), s32[]{:S(2)}) async-start(), calls=%async_computation.12 | async-start | bytes 5898240 | tf_op jit(solution)/shard_map/all_gather | solution.py:118
  507.0 13.0 copy-start.68
  507.0 25.7 %slice-start.18 = ((s8[9068544]{0:T(1024)(128)(4,1)}), s8[4194304]{0:T(1024)(128)(4,1)S(1)}, s32[]{:S(2)}) async-start(s8[9068544]{0:T(1024)(128)(4,1)} %bitcast.259), calls=%async_computation.37 | async-start | bytes 8388608
  507.0 25.7 %slice-start.19 = ((s8[9068544]{0:T(1024)(128)(4,1)}), s8[4194304]{0:T(1024)(128)(4,1)S(1)}, s32[]{:S(2)}) async-start(s8[9068544]{0:T(1024)(128)(4,1)} %bitcast.259), calls=%async_computation.38 | async-start | bytes 8388608
  519.9 12.7 slice-start.20
  617.3 17.0 %slice-start.2 = ((s8[4534272]{0:T(1024)(128)(4,1)}), s8[339968]{0:T(1024)(128)(4,1)S(1)}, s32[]{:S(2)}) async-start(s8[4534272]{0:T(1024)(128)(4,1)} %bitcast.244), calls=%async_computation.21 | async-start | bytes 679936
  617.3 148.7 %all-to-all-start.1 = ((bf16[8,2,141696]{2,1,0:T(2,128)(2,1)}), bf16[8,2,141696]{2,1,0:T(2,128)(2,1)}, u32[]{:S(2)}, u32[]{:S(2)}) async-start(bf16[8,2,141696]{2,1,0:T(2,128)(2,1)} %reshape.595), calls=%async_computation.1 | async-start | bytes 9068544 | tf_op jit(solution)/shard_map/all_to_all | solution.py:130
  622.5 11.8 slice-start.3
  622.5 23.9 %slice-start.8 = ((s8[4718592]{0:T(1024)(128)(4,1)}), s8[4194304]{0:T(1024)(128)(4,1)S(1)}, s32[]{:S(2)}) async-start(s8[4718592]{0:T(1024)(128)(4,1)} %bitcast.250), calls=%async_computation.27 | async-start | bytes 8388608
  634.3 12.1 copy-start.74
  634.3 12.1 slice-start.9
  646.4 12.1 slice-start.10
  652.4 27.3 %slice-start.12 = ((s8[9068544]{0:T(1024)(128)(4,1)}), s8[4194304]{0:T(1024)(128)(4,1)S(1)}, s32[]{:S(2)}) async-start(s8[9068544]{0:T(1024)(128)(4,1)} %bitcast.255), calls=%async_computation.31 | async-start | bytes 8388608
  658.4 21.3 %slice-start.13 = ((s8[9068544]{0:T(1024)(128)(4,1)}), s8[4194304]{0:T(1024)(128)(4,1)S(1)}, s32[]{:S(2)}) async-start(s8[9068544]{0:T(1024)(128)(4,1)} %bitcast.255), calls=%async_computation.32 | async-start | bytes 8388608
  658.4 21.3 %slice-start.14 = ((s8[9068544]{0:T(1024)(128)(4,1)}), s8[679936]{0:T(1024)(128)(4,1)S(1)}, s32[]{:S(2)}) async-start(s8[9068544]{0:T(1024)(128)(4,1)} %bitcast.255), calls=%async_computation.33 | async-start | bytes 1359872
  766.0 105.4 %all-to-all-start.3 = ((bf16[8,2,141696]{2,1,0:T(2,128)(2,1)}), bf16[8,2,141696]{2,1,0:T(2,128)(2,1)}, u32[]{:S(2)}, u32[]{:S(2)}) async-start(bf16[8,2,141696]{2,1,0:T(2,128)(2,1)} %reshape.599), calls=%async_computation.3 | async-start | bytes 9068544 | tf_op jit(solution)/shard_map/all_to_all | solution.py:178
  772.2 339.7 %reduce-scatter.14.cloned.1.call-start = ((), (), s32[]{:S(2)}) async-start(), calls=%async_computation.16 | async-start | bytes 2949120 | tf_op jit(solution)/shard_map/reduce_scatter | solution.py:252
  822.8 19.8 %copy-start.40 = (s32[1182,2]{0,1:T(2,128)S(1)}, s32[1182,2]{0,1:T(2,128)}, u32[]{:S(2)}) copy-start(s32[1182,2]{0,1:T(2,128)} %copy-done.39) | copy-start | bytes 28372
  822.8 19.8 %copy-start.19 = (f32[1182,8]{0,1:T(8,128)S(1)}, f32[1182,8]{0,1:T(8,128)}, u32[]{:S(2)}) copy-start(f32[1182,8]{0,1:T(8,128)} %copy-done.18) | copy-start | bytes 113476
  822.8 19.8 %copy-start.25 = (f32[1182]{0:T(1024)S(1)}, f32[1182]{0:T(1024)}, u32[]{:S(2)}) copy-start(f32[1182]{0:T(1024)} %copy-done.24) | copy-start | bytes 14188
  916.0 11.7 copy-start.32
  916.0 11.7 copy-start.36
  916.0 11.7 copy-start.48
  957.5 154.4 %reduce-scatter.12.cloned.1.call-start = ((), (), s32[]{:S(2)}) async-start(), calls=%async_computation.15 | async-start | bytes 8847360 | tf_op jit(solution)/shard_map/reduce_scatter | solution.py:251
  1013.2 14.7 %copy-start.17 = (bf16[1182,768]{1,0:T(8,128)(2,1)S(1)}, bf16[1182,768]{1,0:T(8,128)(2,1)}, u32[]{:S(2)}) copy-start(bf16[1182,768]{1,0:T(8,128)(2,1)} %convert_element_type.229) | copy-start | bytes 5446660
  1037.6 110.5 %reduce-scatter.16.cloned.1.call-start = ((), (), s32[]{:S(2)}) async-start(), calls=%async_computation.17 | async-start | bytes 491520
  1037.7 22.4 %slice-start.4 = ((s8[4534272]{0:T(1024)(128)(4,1)}), s8[4194304]{0:T(1024)(128)(4,1)S(1)}, s32[]{:S(2)}) async-start(s8[4534272]{0:T(1024)(128)(4,1)} %bitcast.246), calls=%async_computation.23 | async-start | bytes 8388608
  1037.7 22.4 %slice-start.21 = ((s8[9068544]{0:T(1024)(128)(4,1)}), s8[4194304]{0:T(1024)(128)(4,1)S(1)}, s32[]{:S(2)}) async-start(s8[9068544]{0:T(1024)(128)(4,1)} %bitcast.261), calls=%async_computation.40 | async-start | bytes 8388608
  1037.7 22.4 %slice-start.22 = ((s8[9068544]{0:T(1024)(128)(4,1)}), s8[4194304]{0:T(1024)(128)(4,1)S(1)}, s32[]{:S(2)}) async-start(s8[9068544]{0:T(1024)(128)(4,1)} %bitcast.261), calls=%async_computation.41 | async-start | bytes 8388608
  1047.7 12.4 slice-start.5
  1047.7 12.4 slice-start.23
  1047.7 18.5 %slice-start.15 = ((s8[9068544]{0:T(1024)(128)(4,1)}), s8[4194304]{0:T(1024)(128)(4,1)S(1)}, s32[]{:S(2)}) async-start(s8[9068544]{0:T(1024)(128)(4,1)} %bitcast.257), calls=%async_computation.34 | async-start | bytes 8388608
  1047.7 18.5 %slice-start.16 = ((s8[9068544]{0:T(1024)(128)(4,1)}), s8[4194304]{0:T(1024)(128)(4,1)S(1)}, s32[]{:S(2)}) async-start(s8[9068544]{0:T(1024)(128)(4,1)} %bitcast.257), calls=%async_computation.35 | async-start | bytes 8388608
  1075.4 128.7 %reduce-scatter.10.cloned.1.call-start = ((), (), s32[]{:S(2)}) async-start(), calls=%async_computation.14 | async-start | bytes 11796480 | tf_op jit(solution)/shard_map/reduce_scatter | solution.py:176
  1082.9 202.2 %reduce-scatter.8.cloned.1.call-start = ((), (), s32[]{:S(2)}) async-start(), calls=%async_computation.13 | async-start | bytes 11796480 | tf_op jit(solution)/shard_map/reduce_scatter | solution.py:175
  1082.9 15.3 %slice-start = ((s8[4534272]{0:T(1024)(128)(4,1)}), s8[4194304]{0:T(1024)(128)(4,1)S(1)}, s32[]{:S(2)}) async-start(s8[4534272]{0:T(1024)(128)(4,1)} %bitcast.242), calls=%async_computation.19 | async-start | bytes 8388608
  1082.9 15.3 %slice-start.24 = ((s8[4534272]{0:T(1024)(128)(4,1)}), s8[4194304]{0:T(1024)(128)(4,1)S(1)}, s32[]{:S(2)}) async-start(s8[4534272]{0:T(1024)(128)(4,1)} %bitcast.263), calls=%async_computation.43 | async-start | bytes 8388608
  1090.5 12.1 slice-start.6
  1111.0 286.7 %all-reduce.16.cloned.1.call-start = ((), (), s32[]{:S(2)}) async-start(), calls=%async_computation.18 | async-start | bytes 4718592 | tf_op jit(solution)/shard_map/psum | solution.py:236
  1112.0 12.4 copy-start.62
  1112.0 12.4 copy-start.63
  1112.0 22.8 %copy-start.46 = (f32[1182]{0:T(1024)S(1)}, f32[1182]{0:T(1024)}, u32[]{:S(2)}) copy-start(f32[1182]{0:T(1024)} %copy-done.45) | copy-start | bytes 14188
  (51 other events, 283.8 us)
Sparse Core Ops, SparseCore 0:
  9.6 33.8 all-gather.5
  45.1 17.4 all-gather.7
  253.1 37.9 all-gather.9
  358.4 37.8 all-gather.11
  957.6 31.1 reduce-scatter.13
  1037.7 61.3 reduce-scatter.11
  1102.2 20.8 reduce-scatter.15
  1125.7 78.4 reduce-scatter.9
  1206.7 78.3 reduce-scatter.7
  1288.5 109.0 all-reduce.15
where the time goes:
time: 1420 us; the launch traced here: 1410 us
  local copies, waits for them, and re-layouts  454 us (32%)
  matrix products  315 us (22%)
  waiting for transfers between devices  312 us (22%)
  other arithmetic  228 us (16%)
  blocking collectives  60.4 us (4%)
  starting transfers between devices  22.3 us (2%)
  between operations  17.4 us (1%)
    unnamed x238, local copies, waits for them, and re-layouts  150 us
    unnamed x15, other arithmetic  116 us
    psum x1, waiting for transfers between devices, shards(): lax.psum((layer_grads[0], layer_grads[1], layer_grads[2], layer_grads[3],...  107 us
    all_to_all x1, waiting for transfers between devices, shards(): lax.all_to_all(to_slots(jnp.broadcast_to(second_in[:, None, :], (rows, 2,...  77.2 us
    reduce_scatter x1, waiting for transfers between devices, shards(): lax.psum_scatter(jnp.concatenate(up_blocks, 0), 'shard', scatter_dimensio...  75.5 us
    reshape x4, local copies, waits for them, and re-layouts, to_slots(): return filled[:empty_slot].reshape(experts_here, spread, width)  59.9 us
    dot_general x4, matrix products, shards(): jnp.einsum('erf,fed->erd', active, down_part, preferred_element_type=jnp....  48.5 us
    dot_general x4, matrix products, shards(): jnp.einsum('erd,fed->erf', arrived_grad, down_part, preferred_element_typ...  45.4 us
  transfers between devices with their start and end apart: 14, of which 6 were waited for; matrix products, arithmetic and copies ran while one was open for 49% of the time, Pallas kernels for 0%

commit v1 on v0

v1 whole, which is shorter than its diff:
```python
import functools

import jax
import jax.numpy as jnp
from jax import lax
from jax.experimental import pallas as pl
from jax.experimental.pallas import tpu as pltpu
from jax.sharding import PartitionSpec as P

HEADS = 12
EPSILON = 1e-06
CHUNKS = 2
LANES = 128
MIB = 1024 * 1024
BF16 = jnp.bfloat16
F32 = jnp.float32
NN = (((1,), (0,)), ((), ()))
NT = (((1,), (1,)), ((), ()))
TN = (((0,), (0,)), ((), ()))


def dot(a, b, dims=NN):
    return lax.dot_general(a, b, dims, preferred_element_type=F32)


def whole(shape):
    return pl.BlockSpec(shape, lambda *_: (0,) * len(shape), pipeline_mode=pl.Buffered(1))


def call(kernel, grid, in_specs, out_specs, out_shape, scratch, limit):
    return pl.pallas_call(
        kernel,
        grid=grid,
        in_specs=in_specs,
        out_specs=out_specs,
        out_shape=out_shape,
        scratch_shapes=scratch,
        compiler_params=pltpu.CompilerParams(
            vmem_limit_bytes=limit * MIB,
            dimension_semantics=("arbitrary",) * len(grid),
        ),
    )


def normal(value):
    centered = value - jnp.mean(value, -1, keepdims=True)
    inverse = lax.rsqrt(jnp.mean(centered * centered, -1, keepdims=True) + EPSILON)
    return centered * inverse, inverse


def norm_back(grad, gain, unit, inverse):
    scaled = grad * gain
    return inverse * (
        scaled
        - jnp.mean(scaled, -1, keepdims=True)
        - unit * jnp.mean(scaled * unit, -1, keepdims=True)
    )


def one_hot(equal):
    return jnp.where(equal, 1.0, 0.0).astype(BF16)


def padded_rows(source, buffer):
    length = source.shape[1]
    buffer[...] = jnp.zeros_like(buffer)
    buffer[0:length, :] = source[0].astype(buffer.dtype)
    return buffer[...]


def send_images_kernel(codes_ref, source_ref, out_ref, rows):
    images, length, _ = source_ref.shape
    padded = rows.shape[0] // images
    step = pl.program_id(0)

    @pl.when(step == 0)
    def _():
        rows[...] = jnp.zeros_like(rows)
        for image in range(images):
            rows[image * padded : image * padded + length, :] = source_ref[image].astype(F32)

    pick_rows(codes_ref, rows[...].astype(BF16), out_ref, step)


def send_rows_kernel(codes_ref, source_ref, out_ref):
    pick_rows(codes_ref, source_ref[...], out_ref, pl.program_id(0))


def pick_rows(codes_ref, rows, out_ref, step):
    count = out_ref.shape[1]
    tokens = rows.shape[0]
    slot = lax.broadcasted_iota(jnp.int32, (count, tokens), 0) + step * count
    hot = one_hot((slot == codes_ref[0:1, :]) | (slot == codes_ref[1:2, :]))
    out_ref[0] = dot(hot, rows).astype(BF16)


def send(source, codes, experts, count, width):
    tokens = codes.shape[1]
    if source.ndim == 3:
        kernel, scratch = send_images_kernel, [pltpu.VMEM((tokens, width), F32)]
    else:
        kernel, scratch = send_rows_kernel, []
    return call(
        kernel,
        (experts,),
        [whole(codes.shape), whole(source.shape)],
        pl.BlockSpec((1, count, width), lambda e: (e, 0, 0)),
        jax.ShapeDtypeStruct((experts, count, width), BF16),
        scratch,
        40,
    )(codes, source)


def gather_rows(codes, arrays):
    total = None
    for chunk, array in enumerate(arrays):
        slot = lax.broadcasted_iota(jnp.int32, (codes.shape[0], array.shape[0]), 1)
        first = codes[:, 2 * chunk : 2 * chunk + 1]
        second = codes[:, 2 * chunk + 1 : 2 * chunk + 2]
        part = dot(one_hot((slot == first) | (slot == second)), array[...])
        total = part if total is None else total + part
    return total


def attend_kernel(
    tokens_ref, qkv_weight_ref, out_weight_ref, vector_ref,
    qkv_ref, mixed_ref, attended_ref, first_ref, second_ref, buffer,
):
    length = tokens_ref.shape[1]
    padded, width = buffer.shape
    value = padded_rows(tokens_ref, buffer)
    unit, _ = normal(value)
    first = (unit * vector_ref[0:1, :] + vector_ref[1:2, :]).astype(BF16)
    first_ref[0] = first
    qkv_ref[0] = dot(first, qkv_weight_ref[...]).astype(BF16)
    scale = (width // HEADS) ** (-0.5)
    per_tile = LANES * HEADS // width
    lane = lax.broadcasted_iota(jnp.int32, (padded, LANES), 1) // (width // HEADS)
    real = lax.broadcasted_iota(jnp.int32, (padded, padded), 1) < length
    for tile in range(width // LANES):
        at = tile * LANES
        query = qkv_ref[0, :, at : at + LANES]
        keys = qkv_ref[0, :, width + at : width + at + LANES]
        values = qkv_ref[0, :, 2 * width + at : 2 * width + at + LANES]
        result = None
        for head in range(per_tile):
            chosen = jnp.where(lane == head, query.astype(F32) * scale, 0.0).astype(BF16)
            scores = jnp.where(real, dot(chosen, keys, NT), -1e30)
            raised = jnp.exp(scores - jnp.max(scores, -1, keepdims=True))
            probs = raised * (1.0 / jnp.sum(raised, -1, keepdims=True))
            part = dot(probs.astype(BF16), values)
            result = part if result is None else jnp.where(lane == head, part, result)
        mixed_ref[0, :, at : at + LANES] = result.astype(BF16)
    attended = value + dot(mixed_ref[0], out_weight_ref[...])
    attended_ref[0] = attended
    unit, _ = normal(attended)
    second_ref[0] = (unit * vector_ref[2:3, :] + vector_ref[3:4, :]).astype(BF16)


def attend(tokens, weights, vectors, padded):
    images, length, width = tokens.shape
    image = lambda cols: pl.BlockSpec((1, padded, cols), lambda i: (i, 0, 0))
    shape = lambda cols, kind: jax.ShapeDtypeStruct((images, padded, cols), kind)
    return call(
        attend_kernel,
        (images,),
        [
            pl.BlockSpec((1, length, width), lambda i: (i, 0, 0)),
            pl.BlockSpec((width, 3 * width), lambda i: (0, 0), pipeline_mode=pl.Buffered(1)),
            pl.BlockSpec((width, width), lambda i: (0, 3), pipeline_mode=pl.Buffered(1)),
            whole(vectors.shape),
        ],
        [image(3 * width), image(width), image(width), image(width), image(width)],
        [
            shape(3 * width, BF16), shape(width, BF16), shape(width, F32),
            shape(width, BF16), shape(width, BF16),
        ],
        [pltpu.VMEM((padded, width), F32)],
        40,
    )(tokens, weights, weights, vectors)


def gelu_pair(value):
    root = 0.7978845608028654
    cubic = 0.044715
    square = value * value
    bent = jnp.tanh(root * value * (1.0 + cubic * square))
    half = 0.5 * (1.0 + bent)
    slope = half + 0.5 * value * (1.0 - bent * bent) * (root * (1.0 + 3.0 * cubic * square))
    return value * half, slope


def expert_kernel(
    experts, block,
    mine_ref, x_ref, g_ref, up_ref, down_ref, router_ref,
    active_ref, before_ref, scaled_ref, out_ref, back_ref, logit_ref,
    out_sum, back_sum, probs_ref,
):
    step = pl.program_id(0)
    blocks = x_ref.shape[0] // block
    mine = mine_ref[0:1, :]

    def rows_of(index):
        return pl.ds(pl.multiple_of(index * block, block), block)

    @pl.when(step == 0)
    def _():
        def start(index, _):
            rows = rows_of(index)
            logits = dot(x_ref[rows, :], router_ref[...])
            column = lax.broadcasted_iota(jnp.int32, logits.shape, 1)
            logits = jnp.where(column < experts, logits, -1e30)
            raised = jnp.exp(logits - jnp.max(logits, -1, keepdims=True))
            probs = raised / jnp.sum(raised, -1, keepdims=True)
            probs_ref[rows, :] = probs
            gate = jnp.sum(probs * mine, -1, keepdims=True)
            scaled_ref[rows, :] = (gate * g_ref[rows, :].astype(F32)).astype(BF16)
            out_sum[rows, :] = jnp.zeros((block, out_sum.shape[1]), F32)
            back_sum[rows, :] = jnp.zeros((block, back_sum.shape[1]), F32)
            return 0

        lax.fori_loop(0, blocks, start, 0)

    def work(index, _):
        rows = rows_of(index)
        before = dot(x_ref[rows, :], up_ref[...], NT)
        active_grad = dot(scaled_ref[rows, :], down_ref[...], NT)
        active, slope = gelu_pair(before)
        active = active.astype(BF16)
        before_grad = (active_grad * slope).astype(BF16)
        active_ref[rows, :] = active
        before_ref[rows, :] = before_grad
        out_sum[rows, :] += dot(active, down_ref[...])
        back_sum[rows, :] += dot(before_grad, up_ref[...])
        return 0

    lax.fori_loop(0, blocks, work, 0)

    @pl.when(step == pl.num_programs(0) - 1)
    def _():
        def finish(index, _):
            rows = rows_of(index)
            made = out_sum[rows, :].astype(BF16).astype(F32)
            probs = probs_ref[rows, :]
            gate = jnp.sum(probs * mine, -1, keepdims=True)
            gate_grad = jnp.sum(made * g_ref[rows, :].astype(F32), -1, keepdims=True)
            logit = (gate_grad * gate * (mine - probs)).astype(BF16)
            logit_ref[rows, :] = logit
            out_ref[rows, :] = (gate * made).astype(BF16)
            back_ref[rows, :] = (back_sum[rows, :] + dot(logit, router_ref[...], NT)).astype(BF16)
            return 0

        lax.fori_loop(0, blocks, finish, 0)


def run_expert(mine, x, g, up, down, weights, experts):
    rows, width = x.shape
    hidden = up.shape[0]
    part = 512
    block = 256
    last = weights.shape[1] // LANES - 1
    wide = pl.BlockSpec((rows, part), lambda f: (0, f))
    weight = pl.BlockSpec((part, width), lambda f: (f, 0))
    return call(
        functools.partial(expert_kernel, experts, block),
        (hidden // part,),
        [
            whole(mine.shape), whole(x.shape), whole(g.shape), weight, weight,
            pl.BlockSpec((width, LANES), lambda f: (0, last), pipeline_mode=pl.Buffered(1)),
        ],
        [wide, wide, whole((rows, width)), whole((rows, width)), whole((rows, width)), whole((rows, LANES))],
        [
            jax.ShapeDtypeStruct((rows, hidden), BF16), jax.ShapeDtypeStruct((rows, hidden), BF16),
            jax.ShapeDtypeStruct((rows, width), BF16), jax.ShapeDtypeStruct((rows, width), BF16),
            jax.ShapeDtypeStruct((rows, width), BF16), jax.ShapeDtypeStruct((rows, LANES), BF16),
        ],
        [pltpu.VMEM((rows, width), F32), pltpu.VMEM((rows, width), F32), pltpu.VMEM((rows, LANES), F32)],
        52,
    )(mine, x, g, up, down, weights)


def attend_back_kernel(*refs):
    codes_ref, *refs = refs
    returned, refs = refs[:CHUNKS], refs[CHUNKS:]
    (
        cotangent_ref, tokens_ref, attended_ref, qkv_ref,
        qkv_weight_ref, out_weight_ref, vector_ref,
        tokens_grad_ref, branch_ref, rows_grad_ref, sums_ref, buffer,
    ) = refs
    length = tokens_ref.shape[1]
    padded, width = buffer.shape

    @pl.when(pl.program_id(0) == 0)
    def _():
        sums_ref[...] = jnp.zeros_like(sums_ref)

    second_grad = gather_rows(codes_ref[0], returned)
    unit, inverse = normal(attended_ref[0])
    sums_ref[2:3, :] += jnp.sum(second_grad * unit, 0, keepdims=True)
    sums_ref[3:4, :] += jnp.sum(second_grad, 0, keepdims=True)
    attended_grad = padded_rows(cotangent_ref, buffer) + norm_back(
        second_grad, vector_ref[2:3, :], unit, inverse
    )
    branch = attended_grad.astype(BF16)
    branch_ref[0] = branch
    mixed_grad = dot(branch, out_weight_ref[...], NT).astype(BF16)
    scale = (width // HEADS) ** (-0.5)
    per_tile = LANES * HEADS // width
    lane = lax.broadcasted_iota(jnp.int32, (padded, LANES), 1) // (width // HEADS)
    real = lax.broadcasted_iota(jnp.int32, (padded, padded), 0) < length
    for tile in range(width // LANES):
        at = tile * LANES
        query = qkv_ref[0, :, at : at + LANES].astype(F32) * scale
        keys = qkv_ref[0, :, width + at : width + at + LANES]
        values = qkv_ref[0, :, 2 * width + at : 2 * width + at + LANES]
        keys_scaled = keys.astype(F32) * scale
        result = mixed_grad[:, at : at + LANES].astype(F32)
        grads = [None, None, None]
        for head in range(per_tile):
            own = lane == head
            own_query = jnp.where(own, query, 0.0).astype(BF16)
            own_keys = jnp.where(own, keys_scaled, 0.0).astype(BF16)
            own_result = jnp.where(own, result, 0.0).astype(BF16)
            scores = jnp.where(real, dot(keys, own_query, NT), -1e30)
            raised = jnp.exp(scores - jnp.max(scores, 0, keepdims=True))
            probs = raised * (1.0 / jnp.sum(raised, 0, keepdims=True))
            prob_grad = dot(values, own_result, NT)
            score_grad = (
                probs * (prob_grad - jnp.sum(probs * prob_grad, 0, keepdims=True))
            ).astype(BF16)
            parts = (
                dot(score_grad, own_keys, TN),
                dot(score_grad, own_query),
                dot(probs.astype(BF16), own_result),
            )
            grads = [part if old is None else old + part for old, part in zip(grads, parts)]
        for index, grad in enumerate(grads):
            start = index * width + at
            rows_grad_ref[0, :, start : start + LANES] = grad.astype(BF16)
    first_grad = dot(rows_grad_ref[0], qkv_weight_ref[...], NT)
    unit, inverse = normal(padded_rows(tokens_ref, buffer))
    sums_ref[0:1, :] += jnp.sum(first_grad * unit, 0, keepdims=True)
    sums_ref[1:2, :] += jnp.sum(first_grad, 0, keepdims=True)
    tokens_grad = attended_grad + norm_back(first_grad, vector_ref[0:1, :], unit, inverse)
    tokens_grad_ref[0] = tokens_grad[0:length, :].astype(BF16)


def attend_back(codes, returned, cotangent, tokens, attended, qkv, weights, vectors):
    images, length, width = tokens.shape
    padded = attended.shape[1]
    image = lambda rows, cols: pl.BlockSpec((1, rows, cols), lambda i: (i, 0, 0))
    return call(
        attend_back_kernel,
        (images,),
        [image(padded, codes.shape[2])]
        + [whole(array.shape) for array in returned]
        + [
            image(length, width), image(length, width), image(padded, width), image(padded, 3 * width),
            pl.BlockSpec((width, 3 * width), lambda i: (0, 0), pipeline_mode=pl.Buffered(1)),
            pl.BlockSpec((width, width), lambda i: (0, 3), pipeline_mode=pl.Buffered(1)),
            whole(vectors.shape),
        ],
        [image(length, width), image(padded, width), image(padded, 3 * width), whole((8, width))],
        [
            jax.ShapeDtypeStruct((images, length, width), BF16),
            jax.ShapeDtypeStruct((images, padded, width), BF16),
            jax.ShapeDtypeStruct((images, padded, 3 * width), BF16),
            jax.ShapeDtypeStruct((8, width), F32),
        ],
        [pltpu.VMEM((padded, width), F32)],
        48,
    )(codes, *returned, cotangent, tokens, attended, qkv, weights, weights, vectors)


def combine_kernel(codes_ref, *refs):
    returned, (attended_ref, out_ref) = refs[:CHUNKS], refs[CHUNKS:]
    total = attended_ref[0] + gather_rows(codes_ref[0], returned)
    out_ref[0] = total[0 : out_ref.shape[1], :].astype(BF16)


def combine(codes, returned, attended, length):
    images, padded, width = attended.shape
    image = lambda rows, cols: pl.BlockSpec((1, rows, cols), lambda i: (i, 0, 0))
    return call(
        combine_kernel,
        (images,),
        [image(padded, codes.shape[2])]
        + [whole(array.shape) for array in returned]
        + [image(padded, width)],
        image(length, width),
        jax.ShapeDtypeStruct((images, length, width), BF16),
        [],
        40,
    )(codes, *returned, attended)


def exchange(array):
    return lax.all_to_all(array, "expert", split_axis=0, concat_axis=0, tiled=True)


def shards(
    tokens,
    ln1_gain,
    ln1_bias,
    qkv_weight,
    out_weight,
    ln2_gain,
    ln2_bias,
    router_weight,
    up_weight,
    down_weight,
    routes,
    slots,
    keep,
    cotangent,
):
    images, length, width = tokens.shape
    rows = images * length
    experts = lax.axis_size("expert")
    assert up_weight.shape[1] == 1 and router_weight.shape[1] == experts
    capacity = max(4, 5 * rows // (2 * experts))
    count = -(-capacity // (16 * CHUNKS)) * 16
    padded = -(-length // 16) * 16

    columns = experts + 4
    spare = -columns % LANES
    small = jnp.concatenate(
        [router_weight, jnp.stack([ln1_gain, ln1_bias, ln2_gain, ln2_bias], 1)], 1
    )
    packed = jnp.concatenate(
        [qkv_weight, out_weight, jnp.pad(small, ((0, 0), (0, spare)))], 1
    )
    weights = lax.all_gather(packed, "shard", axis=0, tiled=True)
    vectors = jnp.pad(
        weights[:, 4 * width + experts : 4 * width + columns].T.astype(F32), ((0, 4), (0, 0))
    )

    chunk_codes = []
    for chunk in range(CHUNKS):
        place = slots - chunk * count
        here = (keep > 0) & (place >= 0) & (place < count)
        chunk_codes.append(jnp.where(here, routes * count + place, -1))
    codes = jnp.pad(
        jnp.concatenate(chunk_codes, -1),
        ((0, 0), (0, padded - length), (0, 0)),
        constant_values=-1,
    )
    flat_codes = codes.reshape(images * padded, 2 * CHUNKS).T
    row_codes = [flat_codes[2 * chunk : 2 * chunk + 2] for chunk in range(CHUNKS)]

    g_sent = [send(cotangent, code, experts, count, width) for code in row_codes]
    g_sent, tokens_in = lax.optimization_barrier((g_sent, tokens))
    g_here = [exchange(array).reshape(experts * count, width) for array in g_sent]

    up = lax.all_gather(up_weight.reshape(-1, width), "shard", axis=0, tiled=True)
    down = lax.all_gather(down_weight.reshape(-1, width), "shard", axis=0, tiled=True)

    qkv, mixed, attended, first, second = attend(tokens_in, weights, vectors, padded)
    flat_second = second.reshape(images * padded, width)
    mine = (
        lax.broadcasted_iota(jnp.int32, (8, LANES), 1) == lax.axis_index("expert")
    ).astype(F32)

    back_here, out_here, wide = [], [], []
    for chunk in range(CHUNKS):
        x = exchange(send(flat_second, row_codes[chunk], experts, count, width))
        x = x.reshape(experts * count, width)
        active, before_grad, scaled, out, back, logit = run_expert(
            mine, x, g_here[chunk], up, down, weights, experts
        )
        wide.append((active, before_grad, scaled, x, logit))
        back_here.append(back.reshape(experts, count, width))
        out_here.append(out.reshape(experts, count, width))

    returned = [exchange(array).reshape(experts * count, width) for array in back_here]
    out_here, returned = lax.optimization_barrier((out_here, returned))
    out_returned = [exchange(array).reshape(experts * count, width) for array in out_here]

    down_full = sum(dot(part[0], part[2], TN) for part in wide)
    up_full = sum(dot(part[1], part[3], TN) for part in wide)
    router_full = sum(dot(part[3], part[4], TN) for part in wide)
    down_grad = lax.psum_scatter(down_full.astype(BF16), "shard", scatter_dimension=0, tiled=True)
    up_grad = lax.psum_scatter(up_full.astype(BF16), "shard", scatter_dimension=0, tiled=True)

    tokens_grad, branch, rows_grad, sums = attend_back(
        codes, returned, cotangent, tokens, attended, qkv, weights, vectors
    )
    flat = lambda array: array.reshape(images * padded, -1)
    qkv_full = dot(flat(first), flat(rows_grad), TN)
    out_full = dot(flat(mixed), flat(branch), TN)
    small_full = jnp.concatenate([router_full[:, :experts], sums[0:4].T], 1)
    layer = jnp.concatenate(
        [qkv_full, out_full, jnp.pad(small_full, ((0, 0), (0, spare)))], 1
    ).astype(BF16)
    layer = lax.psum_scatter(layer, "shard", scatter_dimension=0, tiled=True)
    layer = lax.psum(layer, "expert").astype(F32)
    block_out = combine(codes, out_returned, attended, length)
    tail = 4 * width + experts
    return (
        block_out,
        tokens_grad,
        layer[:, tail],
        layer[:, tail + 1],
        layer[:, : 3 * width],
        layer[:, 3 * width : 4 * width],
        layer[:, tail + 2],
        layer[:, tail + 3],
        layer[:, 4 * width : tail],
        up_grad.astype(F32)[:, None, :],
        down_grad.astype(F32)[:, None, :],
    )


def solution(mesh):
    placed = (
        P(("expert", "shard"), None, None),
        P("shard"),
        P("shard"),
        P("shard", None),
        P("shard", None),
        P("shard"),
        P("shard"),
        P("shard", None),
        P("shard", "expert", None),
        P("shard", "expert", None),
        P(("expert", "shard"), None, None),
        P(("expert", "shard"), None, None),
        P(("expert", "shard"), None, None),
        P(("expert", "shard"), None, None),
    )
    return jax.shard_map(
        shards,
        mesh=mesh,
        in_specs=placed,
        out_specs=(
            P(("expert", "shard"), None, None),
            P(("expert", "shard"), None, None),
            P("shard"),
            P("shard"),
            P("shard", None),
            P("shard", None),
            P("shard"),
            P("shard"),
            P("shard", None),
            P("shard", "expert", None),
            P("shard", "expert", None),
        ),
        check_vma=False,
    )
```

time: 1420 us -> 706 us (0.50)
  local copies, waits for them, and re-layouts: 454 us -> 38 us
  matrix products: 315 us -> 62.2 us
  other arithmetic: 228 us -> 9.45 us
  Pallas kernels: 0 us -> 210 us
  waiting for transfers between devices: 312 us -> 266 us
  starting transfers between devices: 22.3 us -> 38.1 us
    dot_general x38 -> x8, matrix products: 312 us -> 62.2 us  [dot(): return lax.dot_general(a, b, dims, preferred_element_type=F32)]
    pallas_call x0 -> x9, Pallas kernels: none -> 210 us  [the longest x2 110 us: run_expert(): call(functools.partial(expert_kernel, experts, block), (hidden // part,),...]
    unnamed x238 -> x46, local copies, waits for them, and re-layouts: 150 us -> 28.8 us
    all_to_all x4 -> x7, waiting for transfers between devices: 108 us -> 227 us  [exchange(): lax.all_to_all(array, 'expert', split_axis=0, concat_axis=0, tiled=True)]
    unnamed x15 -> x0, other arithmetic: 116 us -> none
    convert_element_type x15 -> x0, local copies, waits for them, and re-layouts: 115 us -> none  [the longest x1 27.3 us: shards(): produced.astype(jnp.bfloat16)]
    reshape x10 -> x1, local copies, waits for them, and re-layouts: 102 us -> 0.22 us  [shards(): flat_codes = codes.reshape(images * padded, 2 * CHUNKS).T]
    reduce_scatter x4 -> x3, waiting for transfers between devices: 94.5 us -> 0.02 us  [the longest x1 0.02 us: shards(): layer = lax.psum_scatter(layer, 'shard', scatter_dimension=0, tiled=True)]
  transfers between devices with their start and end apart: 14 -> 14, of which waited for: 6 -> 6; matrix products, arithmetic and copies ran while one was open for 49% -> 9% of each run, Pallas kernels for 0% -> 23%
where the time goes in v1:
time: 706 us; the launch traced here: 697 us
  waiting for transfers between devices  266 us (38%)
  Pallas kernels  210 us (30%)
  matrix products  62.2 us (9%)
  blocking collectives  57.8 us (8%)
  starting transfers between devices  38.1 us (5%)
  local copies, waits for them, and re-layouts  38 us (5%)
  between operations  14.8 us (2%)
  other arithmetic  9.45 us (1%)
    all_to_all x7, waiting for transfers between devices, exchange(): lax.all_to_all(array, 'expert', split_axis=0, concat_axis=0, tiled=True)  227 us
    pallas_call x2, Pallas kernels, run_expert(): call(functools.partial(expert_kernel, experts, block), (hidden // part,),...  110 us
    dot_general x8, matrix products, dot(): return lax.dot_general(a, b, dims, preferred_element_type=F32)  62.2 us
    all_to_all x1, blocking collectives, exchange(): lax.all_to_all(array, 'expert', split_axis=0, concat_axis=0, tiled=True)  57.8 us
    pallas_call x1, Pallas kernels, attend_back(): call(attend_back_kernel, (images,), [image(padded, codes.shape[2])] + [wh...  48.2 us
    psum x1, waiting for transfers between devices, shards(): layer = lax.psum(layer, 'expert').astype(F32)  37.6 us
    all_to_all x7, starting transfers between devices, exchange(): lax.all_to_all(array, 'expert', split_axis=0, concat_axis=0, tiled=True)  36.8 us
    unnamed x46, local copies, waits for them, and re-layouts  28.8 us
  transfers between devices with their start and end apart: 14, of which 6 were waited for; matrix products, arithmetic and copies ran while one was open for 9% of the time, Pallas kernels for 23%

profile of v1, /device:TPU:0, one launch (start us, length us, event | category | flops | bytes accessed | tf_op | source)
XLA Modules:
  0.0 696.6 jit_solution(4961890554733031545)
XLA Ops:
  7.3 0.7 stack.12
  7.9 0.7 stack.13
  8.6 0.7 stack.14
  9.9 0.7 concatenate.18
  10.7 2.4 fusion.3
  13.8 0.8 copy-done
  14.6 5.1 shard_map.222
  19.7 1.4 copy-done.3
  21.1 5.1 shard_map.221
  26.2 1.4 copy-done.6
  27.6 7.2 %all-to-all-start.1 = ((bf16[8,192,768]{2,1,0:T(8,128)(2,1)}), bf16[8,192,768]{2,1,0:T(8,128)(2,1)}, u32[]{:S(2)}, u32[]{:S(2)}) async-start(bf16[8,192,768]{2,1,0:T(8,128)(2,1)} %copy-done.6), calls=%async_computation.1 | async-start | bytes 4718592 | tf_op jit(solution)/shard_map/all_to_all | solution.py:398
  34.9 0.7 all-gather.8.cloned.1.call-update
  35.6 53.2 %all-to-all-done.1 = bf16[8,192,768]{2,1,0:T(8,128)(2,1)} async-done(((bf16[8,192,768]{2,1,0:T(8,128)(2,1)}), bf16[8,192,768]{2,1,0:T(8,128)(2,1)}, u32[]{:S(2)}, u32[]{:S(2)}) %all-to-all-start.1) | async-done | bytes 2359328 | tf_op jit(solution)/shard_map/all_to_all | solution.py:398
  88.8 4.4 all-to-all-start.3
  93.2 1.0 slice.52
  94.4 1.5 copy-done.9
  95.9 22.9 %shard_map.223 = (bf16[6,208,2304]{2,1,0:T(8,128)(2,1)}, bf16[6,208,768]{2,1,0:T(8,128)(2,1)S(1)}, f32[6,208,768]{2,1,0:T(8,128)S(1)}, bf16[6,208,768]{2,1,0:T(8,128)(2,1)S(1)}, bf16[6,208,768]{2,1,0:T(8,128)(2,1)S(1)}) custom-call(bf16[6,197,768]{2,1,0:T(8,128)(2,1)S(1)} %copy-done.9, ...), custom_call_target="tpu_custom_call" | custom-call | tf_op jit(solution)/shard_map/pallas_call | solution.py:164
  118.8 1.9 copy-done.1
  120.6 1.3 copy-done.11
  121.9 1.2 copy-done.13
  123.2 4.7 shard_map.224
  127.9 1.4 copy-done.5
  129.3 1.3 copy-done.7
  130.6 15.9 %all-to-all-done.3 = bf16[8,192,768]{2,1,0:T(8,128)(2,1)} async-done(((bf16[8,192,768]{2,1,0:T(8,128)(2,1)}), bf16[8,192,768]{2,1,0:T(8,128)(2,1)}, u32[]{:S(2)}, u32[]{:S(2)}) %all-to-all-start.3) | async-done | bytes 2359328 | tf_op jit(solution)/shard_map/all_to_all | solution.py:398
  146.6 4.4 all-to-all-start
  151.0 0.7 all-gather.10.cloned.1.call-update
  151.7 1.5 copy-done.8
  153.2 4.8 shard_map.226
  158.0 1.4 copy-done.4
  159.4 44.9 %all-to-all-done = bf16[8,192,768]{2,1,0:T(8,128)(2,1)} async-done(((bf16[8,192,768]{2,1,0:T(8,128)(2,1)}), bf16[8,192,768]{2,1,0:T(8,128)(2,1)}, u32[]{:S(2)}, u32[]{:S(2)}) %all-to-all-start) | async-done | bytes 2359328 | tf_op jit(solution)/shard_map/all_to_all | solution.py:398
  204.3 4.4 all-to-all-start.2
  208.8 54.8 %shard_map.225 = (bf16[1536,3072]{1,0:T(8,128)(2,1)}, bf16[1536,3072]{1,0:T(8,128)(2,1)}, bf16[1536,768]{1,0:T(8,128)(2,1)}, bf16[1536,768]{1,0:T(8,128)(2,1)}, ...) custom-call(f32[8,128]{1,0:T(8,128)S(1)} %iota.7.mine_ref, bf16[1536,768]{1,0:T(8,128)(2,1)} %bitcast.4.x_ref, ...), custom_call_target="tpu_custom_call" | custom-call | tf_op jit(solution)/shard_map/pallas_call | solution.py:264
  263.6 5.9 all-to-all-start.4
  269.6 54.8 %shard_map.227 = (bf16[1536,3072]{1,0:T(8,128)(2,1)}, bf16[1536,3072]{1,0:T(8,128)(2,1)}, bf16[1536,768]{1,0:T(8,128)(2,1)}, bf16[1536,768]{1,0:T(8,128)(2,1)}, ...) custom-call(f32[8,128]{1,0:T(8,128)S(1)} %iota.7.mine_ref, bf16[1536,768]{1,0:T(8,128)(2,1)} %bitcast.9.x_ref, ...), custom_call_target="tpu_custom_call" | custom-call | tf_op jit(solution)/shard_map/pallas_call | solution.py:264
  324.4 6.0 all-to-all-start.5
  330.6 2.2 fusion.7
  332.8 2.2 fusion.8
  335.1 47.6 %all-to-all-done.5 = bf16[8,192,768]{2,1,0:T(8,128)(2,1)} async-done(((bf16[8,192,768]{2,1,0:T(8,128)(2,1)}), bf16[8,192,768]{2,1,0:T(8,128)(2,1)}, u32[]{:S(2)}, u32[]{:S(2)}) %all-to-all-start.5) | async-done | bytes 2359328 | tf_op jit(solution)/shard_map/all_to_all | solution.py:398
  382.7 1.5 copy-done.10
  384.2 48.2 %shard_map.229 = (bf16[6,197,768]{2,1,0:T(8,128)(2,1)}, bf16[6,208,768]{2,1,0:T(8,128)(2,1)}, bf16[6,208,2304]{2,1,0:T(8,128)(2,1)}, f32[8,768]{1,0:T(8,128)S(1)}) custom-call(s32[6,208,4]{2,1,0:T(8,128)S(1)} %pad.19.codes_ref.refs_0_, bf16[1536,768]{1,0:T(8,128)(2,1)} %bitcast.13.refs_1_, bf16[1536,768]{1,0:T(8,128)(2,1)} %bitcast.15.refs_2_, ...), custom_call_target="tpu_custom_call" | custom-call | tf_op jit(solution)/shard_map/pallas_call | solution.py:352
  432.6 4.0 bitcast_convert_fusion.1
  436.9 5.2 bitcast_convert_fusion
  442.1 2.6 fusion.1
  445.2 1.2 copy-done.19
  446.4 10.6 %fusion.10 = f32[3072,768]{1,0:T(8,128)S(1)} fusion(bf16[1536,3072]{1,0:T(8,128)(2,1)} %get-tuple-element.63, bf16[1536,768]{1,0:T(8,128)(2,1)S(1)} %copy-done.19), kind=kOutput, calls=%fused_computation.31 | convolution fusion | flops 7247757312 | bytes 21233664 | tf_op jit(solution)/shard_map/dot_general | solution.py:23
  457.0 14.0 %add_convert_fusion = bf16[3072,768]{1,0:T(8,128)(2,1)} fusion(f32[3072,768]{1,0:T(8,128)S(1)} %fusion.10, bf16[1536,3072]{1,0:T(8,128)(2,1)} %get-tuple-element.65, bf16[1536,768]{1,0:T(8,128)(2,1)S(1)} %copy-done.20), kind=kOutput, calls=%fused_computation.2 | convolution fusion | flops 7252475904 | bytes 25952256 | tf_op jit(solution)/shard_map/dot_general | solution.py:23
  471.3 11.3 %fusion.9 = f32[3072,768]{1,0:T(8,128)S(1)} fusion(bf16[1536,3072]{1,0:T(8,128)(2,1)} %get-tuple-element.61, bf16[1536,768]{1,0:T(8,128)(2,1)} %bitcast.4.x_ref), kind=kOutput, calls=%fused_computation.30 | convolution fusion | flops 7247757312 | bytes 21233664 | tf_op jit(solution)/shard_map/dot_general | solution.py:23
  482.5 12.8 %add_convert_fusion.1 = bf16[3072,768]{1,0:T(8,128)(2,1)} fusion(f32[3072,768]{1,0:T(8,128)S(1)} %fusion.9, bf16[1536,3072]{1,0:T(8,128)(2,1)} %get-tuple-element.62, bf16[1536,768]{1,0:T(8,128)(2,1)} %bitcast.9.x_ref), kind=kOutput, calls=%fused_computation.3 | convolution fusion | flops 7252475904 | bytes 25952256 | tf_op jit(solution)/shard_map/dot_general | solution.py:23
  495.3 57.8 %all_to_all.40 = bf16[8,192,768]{2,1,0:T(8,128)(2,1)S(1)} all-to-all(bf16[8,192,768]{2,1,0:T(8,128)(2,1)} %bitcast.55), channel_id=1, replica_groups=mesh['expert'=8,'shard'=4] {'expert'}, dimensions={0} | all-to-all | bytes 4718592 | tf_op jit(solution)/shard_map/all_to_all | solution.py:398
  553.1 4.5 all-to-all-start.7
  558.4 65.0 %all-to-all-done.7 = bf16[8,192,768]{2,1,0:T(8,128)(2,1)} async-done(((bf16[8,192,768]{2,1,0:T(8,128)(2,1)}), bf16[8,192,768]{2,1,0:T(8,128)(2,1)}, u32[]{:S(2)}, u32[]{:S(2)}) %all-to-all-start.7) | async-done | bytes 2359328 | tf_op jit(solution)/shard_map/all_to_all | solution.py:398
  623.3 2.1 copy-done.2
  625.4 9.8 %shard_map.228 = bf16[6,197,768]{2,1,0:T(8,128)(2,1)} custom-call(s32[6,208,4]{2,1,0:T(8,128)S(1)} %pad.19.codes_ref.refs_0_, bf16[1536,768]{1,0:T(8,128)(2,1)S(1)} %bitcast.47, bf16[1536,768]{1,0:T(8,128)(2,1)} %bitcast.17.refs_1_, f32[6,208,768]{2,1,0:T(8,128)S(1)} %copy-done.2), custom_call_target="tpu_custom_call" | custom-call | tf_op jit(solution)/shard_map/pallas_call | solution.py:384
  635.3 1.4 bitcast_convert_fusion.2
  636.7 3.8 copy.117
  640.5 1.4 bitcast_convert_fusion.3
  642.0 3.8 copy.116
  645.8 37.6 %all-reduce.6.cloned.1.call-done = bf16[192,3200]{1,0:T(8,128)(2,1)} async-done(((bf16[192,3200]{1,0:T(8,128)(2,1)}), bf16[192,3200]{1,0:T(8,128)(2,1)}) %all-reduce.6.cloned.1.call-update) | async-done | bytes 1228816 | tf_op jit(solution)/shard_map/psum | solution.py:496
  683.4 0.9 slice.62
  684.3 0.7 copy.115
  685.0 1.4 convert_element_type.27
  686.4 0.9 slice_reduce_fusion
  687.4 0.9 slice.59
  688.2 1.3 slice.58
  (64 shorter events, 4.0 us)
Async XLA Ops:
  7.2 6.0 copy-start.17
  7.2 6.0 copy-start.15
  7.2 6.0 copy-start.16
  7.2 86.0 %all-gather.6.cloned.1.call-start = ((), (), s32[]{:S(2)}) async-start(), calls=%async_computation.11 | async-start | bytes 6144000 | tf_op jit(solution)/shard_map/all_gather | solution.py:433
  13.1 1.5 copy-start
  19.7 1.4 copy-start.3
  26.1 1.4 copy-start.6
  27.6 61.2 %all-to-all-start.1 = ((bf16[8,192,768]{2,1,0:T(8,128)(2,1)}), bf16[8,192,768]{2,1,0:T(8,128)(2,1)}, u32[]{:S(2)}, u32[]{:S(2)}) async-start(bf16[8,192,768]{2,1,0:T(8,128)(2,1)} %copy-done.6), calls=%async_computation.1 | async-start | bytes 4718592 | tf_op jit(solution)/shard_map/all_to_all | solution.py:398
  34.8 174.0 %all-gather.8.cloned.1.call-start = ((), (), s32[]{:S(2)}) async-start(), calls=%async_computation.16 | async-start | bytes 5898240 | tf_op jit(solution)/shard_map/all_gather | solution.py:455
  88.8 57.8 %all-to-all-start.3 = ((bf16[8,192,768]{2,1,0:T(8,128)(2,1)}), bf16[8,192,768]{2,1,0:T(8,128)(2,1)}, u32[]{:S(2)}, u32[]{:S(2)}) async-start(bf16[8,192,768]{2,1,0:T(8,128)(2,1)} %copy-done.3), calls=%async_computation.3 | async-start | bytes 4718592 | tf_op jit(solution)/shard_map/all_to_all | solution.py:398
  94.4 1.5 copy-start.9
  118.8 1.9 copy-start.1
  120.6 1.3 copy-start.11
  121.9 1.2 copy-start.13
  127.9 1.4 copy-start.5
  129.3 1.3 copy-start.7
  146.6 57.8 %all-to-all-start = ((bf16[8,192,768]{2,1,0:T(8,128)(2,1)}), bf16[8,192,768]{2,1,0:T(8,128)(2,1)}, u32[]{:S(2)}, u32[]{:S(2)}) async-start(bf16[8,192,768]{2,1,0:T(8,128)(2,1)} %copy-done.5), calls=%async_computation | async-start | bytes 4718592 | tf_op jit(solution)/shard_map/all_to_all | solution.py:398
  151.0 57.8 %all-gather.10.cloned.1.call-start = ((), (), s32[]{:S(2)}) async-start(), calls=%async_computation.17 | async-start | bytes 5898240 | tf_op jit(solution)/shard_map/all_gather | solution.py:456
  151.7 1.5 copy-start.8
  158.0 1.4 copy-start.4
  204.3 59.3 %all-to-all-start.2 = ((bf16[8,192,768]{2,1,0:T(8,128)(2,1)}), bf16[8,192,768]{2,1,0:T(8,128)(2,1)}, u32[]{:S(2)}, u32[]{:S(2)}) async-start(bf16[8,192,768]{2,1,0:T(8,128)(2,1)} %copy-done.4), calls=%async_computation.2 | async-start | bytes 4718592 | tf_op jit(solution)/shard_map/all_to_all | solution.py:398
  263.6 60.8 %all-to-all-start.4 = ((bf16[8,192,768]{2,1,0:T(8,128)(2,1)}), bf16[8,192,768]{2,1,0:T(8,128)(2,1)}, u32[]{:S(2)}, u32[]{:S(2)}) async-start(bf16[8,192,768]{2,1,0:T(8,128)(2,1)} %bitcast.56), calls=%async_computation.4 | async-start | bytes 4718592 | tf_op jit(solution)/shard_map/all_to_all | solution.py:398
  324.4 58.3 %all-to-all-start.5 = ((bf16[8,192,768]{2,1,0:T(8,128)(2,1)}), bf16[8,192,768]{2,1,0:T(8,128)(2,1)}, u32[]{:S(2)}, u32[]{:S(2)}) async-start(bf16[8,192,768]{2,1,0:T(8,128)(2,1)} %bitcast.57), calls=%async_computation.5 | async-start | bytes 4718592 | tf_op jit(solution)/shard_map/all_to_all | solution.py:398
  330.4 227.5 %reduce-scatter.4.cloned.1.call-start = ((), (), s32[]{:S(2)}) async-start(), calls=%async_computation.12 | async-start | bytes 6144000 | tf_op jit(solution)/shard_map/reduce_scatter | solution.py:495
  382.7 1.5 copy-start.10
  432.6 4.0 copy-start.12
  432.6 4.4 copy-start.18
  444.8 1.7 copy-start.19
  444.8 190.5 %reduce-scatter.8.cloned.1.call-start = ((), (), s32[]{:S(2)}) async-start(), calls=%async_computation.15 | async-start | bytes 5898240 | tf_op jit(solution)/shard_map/reduce_scatter | solution.py:482
  446.4 10.6 %copy-start.20 = (bf16[1536,768]{1,0:T(8,128)(2,1)S(1)}, bf16[1536,768]{1,0:T(8,128)(2,1)}, u32[]{:S(2)}) copy-start(bf16[1536,768]{1,0:T(8,128)(2,1)} %get-tuple-element.66) | copy-start | bytes 7077892
  471.0 169.5 %reduce-scatter.6.cloned.1.call-start = ((), (), s32[]{:S(2)}) async-start(), calls=%async_computation.14 | async-start | bytes 5898240 | tf_op jit(solution)/shard_map/reduce_scatter | solution.py:483
  553.1 70.2 %all-to-all-start.7 = ((bf16[8,192,768]{2,1,0:T(8,128)(2,1)}), bf16[8,192,768]{2,1,0:T(8,128)(2,1)}, u32[]{:S(2)}, u32[]{:S(2)}) async-start(bf16[8,192,768]{2,1,0:T(8,128)(2,1)} %bitcast.54), calls=%async_computation.7 | async-start | bytes 4718592 | tf_op jit(solution)/shard_map/all_to_all | solution.py:398
  557.6 125.8 %all-reduce.6.cloned.1.call-start = ((), (), s32[]{:S(2)}) async-start(), calls=%async_computation.13 | async-start | bytes 2457600 | tf_op jit(solution)/shard_map/psum | solution.py:496
  623.3 2.1 copy-start.2
  683.4 4.0 copy-start.14
Sparse Core Ops, SparseCore 0:
  13.3 41.2 all-gather.5
  56.1 37.4 all-gather.7
  153.3 38.7 all-gather.9
  444.9 48.2 reduce-scatter.3
  495.7 47.8 reduce-scatter.7
  546.0 47.8 reduce-scatter.5
  597.8 85.5 all-reduce.5

commit v2 on v1

--- a/solution.py
+++ b/solution.py
@@ -184,99 +184,114 @@
     root = 0.7978845608028654
     cubic = 0.044715
     square = value * value
-    bent = jnp.tanh(root * value * (1.0 + cubic * square))
-    half = 0.5 * (1.0 + bent)
-    slope = half + 0.5 * value * (1.0 - bent * bent) * (root * (1.0 + 3.0 * cubic * square))
-    return value * half, slope
-
-
-def expert_kernel(
-    experts, block,
-    mine_ref, x_ref, g_ref, up_ref, down_ref, router_ref,
-    active_ref, before_ref, scaled_ref, out_ref, back_ref, logit_ref,
-    out_sum, back_sum, probs_ref,
-):
+    bent = jnp.tanh(value * (root + root * cubic * square))
+    half = 0.5 + 0.5 * bent
+    active = value * half
+    slope = half + active * (1.0 - half) * (2.0 * root + 6.0 * root * cubic * square)
+    return active, slope
+
+
+def expert_kernel(experts, block, kept, mine_ref, x_ref, g_ref, up_ref, down_ref, router_ref, *refs):
+    (
+        active_ref, before_ref, scaled_ref, x_all_ref, logit_ref, out_ref, back_ref,
+        out_sum, back_sum, probs_ref,
+    ) = refs[kept:]
     step = pl.program_id(0)
-    blocks = x_ref.shape[0] // block
+    sources, count, width = x_ref.shape
+    total = sources * count
+    blocks = total // block
     mine = mine_ref[0:1, :]
-
-    def rows_of(index):
-        return pl.ds(pl.multiple_of(index * block, block), block)
 
     @pl.when(step == 0)
     def _():
-        def start(index, _):
-            rows = rows_of(index)
-            logits = dot(x_ref[rows, :], router_ref[...])
+        out_sum[...] = jnp.zeros_like(out_sum)
+        back_sum[...] = jnp.zeros_like(back_sum)
+        for source in range(sources):
+            rows = slice(source * count, (source + 1) * count)
+            x = x_ref[source]
+            x_all_ref[0, rows, :] = x
+            logits = dot(x, router_ref[...])
             column = lax.broadcasted_iota(jnp.int32, logits.shape, 1)
             logits = jnp.where(column < experts, logits, -1e30)
             raised = jnp.exp(logits - jnp.max(logits, -1, keepdims=True))
             probs = raised / jnp.sum(raised, -1, keepdims=True)
             probs_ref[rows, :] = probs
             gate = jnp.sum(probs * mine, -1, keepdims=True)
-            scaled_ref[rows, :] = (gate * g_ref[rows, :].astype(F32)).astype(BF16)
-            out_sum[rows, :] = jnp.zeros((block, out_sum.shape[1]), F32)
-            back_sum[rows, :] = jnp.zeros((block, back_sum.shape[1]), F32)
-            return 0
-
-        lax.fori_loop(0, blocks, start, 0)
-
-    def work(index, _):
-        rows = rows_of(index)
-        before = dot(x_ref[rows, :], up_ref[...], NT)
-        active_grad = dot(scaled_ref[rows, :], down_ref[...], NT)
+            scaled_ref[0, rows, :] = (gate * g_ref[source].astype(F32)).astype(BF16)
+
+    def first_products(index):
+        rows = slice(index * block, (index + 1) * block)
+        before = dot(x_all_ref[0, rows, :], up_ref[...], NT)
+        return before, dot(scaled_ref[0, rows, :], down_ref[...], NT)
+
+    ahead = first_products(0)
+    for index in range(blocks):
+        rows = slice(index * block, (index + 1) * block)
+        before, active_grad = ahead
+        if index + 1 < blocks:
+            ahead = first_products(index + 1)
         active, slope = gelu_pair(before)
         active = active.astype(BF16)
         before_grad = (active_grad * slope).astype(BF16)
-        active_ref[rows, :] = active
-        before_ref[rows, :] = before_grad
+        active_ref[0, rows, :] = active
+        before_ref[0, rows, :] = before_grad
         out_sum[rows, :] += dot(active, down_ref[...])
         back_sum[rows, :] += dot(before_grad, up_ref[...])
-        return 0
-
-    lax.fori_loop(0, blocks, work, 0)
 
     @pl.when(step == pl.num_programs(0) - 1)
     def _():
-        def finish(index, _):
-            rows = rows_of(index)
+        for source in range(sources):
+            rows = slice(source * count, (source + 1) * count)
             made = out_sum[rows, :].astype(BF16).astype(F32)
             probs = probs_ref[rows, :]
             gate = jnp.sum(probs * mine, -1, keepdims=True)
-            gate_grad = jnp.sum(made * g_ref[rows, :].astype(F32), -1, keepdims=True)
+            gate_grad = jnp.sum(made * g_ref[source].astype(F32), -1, keepdims=True)
             logit = (gate_grad * gate * (mine - probs)).astype(BF16)
-            logit_ref[rows, :] = logit
-            out_ref[rows, :] = (gate * made).astype(BF16)
-            back_ref[rows, :] = (back_sum[rows, :] + dot(logit, router_ref[...], NT)).astype(BF16)
-            return 0
-
-        lax.fori_loop(0, blocks, finish, 0)
-
-
-def run_expert(mine, x, g, up, down, weights, experts):
-    rows, width = x.shape
+            logit_ref[0, rows, :] = logit
+            out_ref[source] = (gate * made).astype(BF16)
+            back_ref[source] = (
+                back_sum[rows, :] + dot(logit, router_ref[...], NT)
+            ).astype(BF16)
+
+
+def run_expert(chunk, kept, mine, x, g, up, down, weights, experts):
+    sources, count, width = x.shape
+    rows = sources * count
     hidden = up.shape[0]
-    part = 512
+    part = 768
     block = 256
     last = weights.shape[1] // LANES - 1
-    wide = pl.BlockSpec((rows, part), lambda f: (0, f))
+    chunk_rows = (sources, count, width)
+    wide = pl.BlockSpec((1, rows, part), lambda f: (chunk, 0, f))
     weight = pl.BlockSpec((part, width), lambda f: (f, 0))
-    return call(
-        functools.partial(expert_kernel, experts, block),
-        (hidden // part,),
-        [
-            whole(mine.shape), whole(x.shape), whole(g.shape), weight, weight,
+    slots = pl.BlockSpec(chunk_rows, lambda f: (0, chunk, 0), pipeline_mode=pl.Buffered(1))
+    one = lambda cols: pl.BlockSpec(
+        (1, rows, cols), lambda f: (chunk, 0, 0), pipeline_mode=pl.Buffered(1)
+    )
+    made = lambda cols: jax.ShapeDtypeStruct((CHUNKS, rows, cols), BF16)
+    return pl.pallas_call(
+        functools.partial(expert_kernel, experts, block, len(kept)),
+        grid=(hidden // part,),
+        in_specs=[
+            whole(mine.shape),
+            whole(chunk_rows),
+            slots,
+            weight,
+            weight,
             pl.BlockSpec((width, LANES), lambda f: (0, last), pipeline_mode=pl.Buffered(1)),
+        ]
+        + [pl.BlockSpec(memory_space=pl.ANY)] * len(kept),
+        out_specs=[wide, wide, one(width), one(width), one(LANES), slots, whole(chunk_rows)],
+        out_shape=[made(hidden), made(hidden), made(width), made(width), made(LANES)]
+        + [jax.ShapeDtypeStruct(g.shape, BF16), jax.ShapeDtypeStruct(chunk_rows, BF16)],
+        scratch_shapes=[
+            pltpu.VMEM((rows, width), F32), pltpu.VMEM((rows, width), F32), pltpu.VMEM((rows, LANES), F32)
         ],
-        [wide, wide, whole((rows, width)), whole((rows, width)), whole((rows, width)), whole((rows, LANES))],
-        [
-            jax.ShapeDtypeStruct((rows, hidden), BF16), jax.ShapeDtypeStruct((rows, hidden), BF16),
-            jax.ShapeDtypeStruct((rows, width), BF16), jax.ShapeDtypeStruct((rows, width), BF16),
-            jax.ShapeDtypeStruct((rows, width), BF16), jax.ShapeDtypeStruct((rows, LANES), BF16),
-        ],
-        [pltpu.VMEM((rows, width), F32), pltpu.VMEM((rows, width), F32), pltpu.VMEM((rows, LANES), F32)],
-        52,
-    )(mine, x, g, up, down, weights)
+        input_output_aliases={6 + index: index for index in range(len(kept))},
+        compiler_params=pltpu.CompilerParams(
+            vmem_limit_bytes=56 * MIB, dimension_semantics=("arbitrary",)
+        ),
+    )(mine, x, g, up, down, weights, *kept)
 
 
 def attend_back_kernel(*refs):
@@ -373,7 +388,7 @@
 
 
 def combine_kernel(codes_ref, *refs):
-    returned, (attended_ref, out_ref) = refs[:CHUNKS], refs[CHUNKS:]
+    *returned, attended_ref, out_ref = refs
     total = attended_ref[0] + gather_rows(codes_ref[0], returned)
     out_ref[0] = total[0 : out_ref.shape[1], :].astype(BF16)
 
@@ -392,6 +407,25 @@
         [],
         40,
     )(codes, *returned, attended)
+
+
+def sum_shards(array):
+    size = lax.axis_size("shard")
+    rows, cols = array.shape
+    pairs = size // 2
+    me = lax.axis_index("shard")
+    blocks = array.reshape(pairs, 2, rows // size, cols)
+    take = lambda core: lax.dynamic_index_in_dim(blocks, core, 1, keepdims=False)
+    other = lax.ppermute(take(1 - me % 2), "shard", [(s, s ^ 1) for s in range(size)])
+    halves = take(me % 2).astype(F32) + other.astype(F32)
+    sent = halves.astype(BF16)
+    at = me // 2
+    total = lax.dynamic_index_in_dim(halves, at, 0, keepdims=False)
+    for shift in range(1, pairs):
+        part = lax.dynamic_index_in_dim(sent, (at + shift) % pairs, 0, keepdims=False)
+        moves = [(s, (s // 2 + shift) % pairs * 2 + s % 2) for s in range(size)]
+        total = total + lax.ppermute(part, "shard", moves).astype(F32)
+    return total.astype(BF16)
 
 
 def exchange(array):
@@ -448,9 +482,15 @@
     flat_codes = codes.reshape(images * padded, 2 * CHUNKS).T
     row_codes = [flat_codes[2 * chunk : 2 * chunk + 2] for chunk in range(CHUNKS)]
 
-    g_sent = [send(cotangent, code, experts, count, width) for code in row_codes]
+    all_codes = jnp.pad(
+        jnp.where(keep > 0, routes * (CHUNKS * count) + slots, -1),
+        ((0, 0), (0, padded - length), (0, 0)),
+        constant_values=-1,
+    )
+    g_codes = all_codes.reshape(images * padded, 2).T
+    g_sent = send(cotangent, g_codes, experts, CHUNKS * count, width)
     g_sent, tokens_in = lax.optimization_barrier((g_sent, tokens))
-    g_here = [exchange(array).reshape(experts * count, width) for array in g_sent]
+    g_here = exchange(g_sent)
 
     up = lax.all_gather(up_weight.reshape(-1, width), "shard", axis=0, tiled=True)
     down = lax.all_gather(down_weight.reshape(-1, width), "shard", axis=0, tiled=True)
@@ -461,26 +501,28 @@
         lax.broadcasted_iota(jnp.int32, (8, LANES), 1) == lax.axis_index("expert")
     ).astype(F32)
 
-    back_here, out_here, wide = [], [], []
+    back_here, kept = [], []
     for chunk in range(CHUNKS):
         x = exchange(send(flat_second, row_codes[chunk], experts, count, width))
-        x = x.reshape(experts * count, width)
-        active, before_grad, scaled, out, back, logit = run_expert(
-            mine, x, g_here[chunk], up, down, weights, experts
-        )
-        wide.append((active, before_grad, scaled, x, logit))
-        back_here.append(back.reshape(experts, count, width))
-        out_here.append(out.reshape(experts, count, width))
+        *kept, back = run_expert(chunk, kept, mine, x, g_here, up, down, weights, experts)
+        back_here.append(back)
+    *kept, out_here = kept
+    active, before_grad, scaled, x_all, logit = [
+        array.reshape(CHUNKS * experts * count, -1) for array in kept
+    ]
 
     returned = [exchange(array).reshape(experts * count, width) for array in back_here]
     out_here, returned = lax.optimization_barrier((out_here, returned))
-    out_returned = [exchange(array).reshape(experts * count, width) for array in out_here]
-
-    down_full = sum(dot(part[0], part[2], TN) for part in wide)
-    up_full = sum(dot(part[1], part[3], TN) for part in wide)
-    router_full = sum(dot(part[3], part[4], TN) for part in wide)
-    down_grad = lax.psum_scatter(down_full.astype(BF16), "shard", scatter_dimension=0, tiled=True)
-    up_grad = lax.psum_scatter(up_full.astype(BF16), "shard", scatter_dimension=0, tiled=True)
+    out_returned = exchange(out_here).reshape(experts * CHUNKS * count, width)
+
+    down_full = dot(active, scaled, TN).astype(BF16)
+    up_full = dot(before_grad, x_all, TN).astype(BF16)
+    router_full = dot(x_all, logit, TN)
+    down_full, up_full, router_full, returned = lax.optimization_barrier(
+        (down_full, up_full, router_full, returned)
+    )
+    down_grad = lax.psum_scatter(down_full, "shard", scatter_dimension=0, tiled=True)
+    up_grad = lax.psum_scatter(up_full, "shard", scatter_dimension=0, tiled=True)
 
     tokens_grad, branch, rows_grad, sums = attend_back(
         codes, returned, cotangent, tokens, attended, qkv, weights, vectors
@@ -492,9 +534,10 @@
     layer = jnp.concatenate(
         [qkv_full, out_full, jnp.pad(small_full, ((0, 0), (0, spare)))], 1
     ).astype(BF16)
-    layer = lax.psum_scatter(layer, "shard", scatter_dimension=0, tiled=True)
+    layer = sum_shards(layer)
+    layer, up_grad, down_grad = lax.optimization_barrier((layer, up_grad, down_grad))
     layer = lax.psum(layer, "expert").astype(F32)
-    block_out = combine(codes, out_returned, attended, length)
+    block_out = combine(all_codes, [out_returned], attended, length)
     tail = 4 * width + experts
     return (
         block_out,

time: 706 us -> 660 us (0.935)
  waiting for transfers between devices: 266 us -> 248 us
  Pallas kernels: 210 us -> 195 us
  starting transfers between devices: 38.1 us -> 27.6 us
  matrix products: 62.2 us -> 55 us
    all_to_all x7 -> x5, waiting for transfers between devices: 227 us -> 166 us  [exchange(): lax.all_to_all(array, 'expert', split_axis=0, concat_axis=0, tiled=True)]
    ppermute x0 -> x2, waiting for transfers between devices: none -> 44.4 us  [the longest x1 39.5 us: sum_shards(): total = total + lax.ppermute(part, 'shard', moves).astype(F32)]
    pallas_call x2, Pallas kernels: 110 us -> 90.1 us  [run_expert(): pl.pallas_call(functools.partial(expert_kernel, experts, block, len(kept)...]
    psum x1, waiting for transfers between devices: 37.6 us -> 21.5 us  [shards(): layer = lax.psum(layer, 'expert').astype(F32)]
    all_gather x1, waiting for transfers between devices: 0.02 us -> 14.2 us  [shards(): weights = lax.all_gather(packed, 'shard', axis=0, tiled=True)]
    all_to_all x7 -> x5, starting transfers between devices: 36.8 us -> 25.6 us  [exchange(): lax.all_to_all(array, 'expert', split_axis=0, concat_axis=0, tiled=True)]
    dot_general x8 -> x5, matrix products: 62.2 us -> 55 us  [dot(): return lax.dot_general(a, b, dims, preferred_element_type=F32)]
    unnamed x46 -> x56, local copies, waits for them, and re-layouts: 28.8 us -> 26.7 us
  transfers between devices with their start and end apart: 14 -> 13, of which waited for: 6 -> 9; matrix products, arithmetic and copies ran while one was open for 9% -> 12% of each run, Pallas kernels for 23% -> 23%
where the time goes in v2:
time: 660 us; the launch traced here: 652 us
  waiting for transfers between devices  248 us (38%)
  Pallas kernels  195 us (30%)
  blocking collectives  57.9 us (9%)
  matrix products  55 us (8%)
  local copies, waits for them, and re-layouts  41.5 us (6%)
  starting transfers between devices  27.6 us (4%)
  between operations  15 us (2%)
  other arithmetic  12.4 us (2%)
    all_to_all x5, waiting for transfers between devices, exchange(): lax.all_to_all(array, 'expert', split_axis=0, concat_axis=0, tiled=True)  166 us
    pallas_call x2, Pallas kernels, run_expert(): pl.pallas_call(functools.partial(expert_kernel, experts, block, len(kept)...  90.1 us
    all_to_all x1, blocking collectives, exchange(): lax.all_to_all(array, 'expert', split_axis=0, concat_axis=0, tiled=True)  57.9 us
    dot_general x5, matrix products, dot(): return lax.dot_general(a, b, dims, preferred_element_type=F32)  55 us
    pallas_call x1, Pallas kernels, attend_back(): call(attend_back_kernel, (images,), [image(padded, codes.shape[2])] + [wh...  50.1 us
    ppermute x1, waiting for transfers between devices, sum_shards(): total = total + lax.ppermute(part, 'shard', moves).astype(F32)  39.5 us
    unnamed x56, local copies, waits for them, and re-layouts  26.7 us
    all_to_all x5, starting transfers between devices, exchange(): lax.all_to_all(array, 'expert', split_axis=0, concat_axis=0, tiled=True)  25.6 us
  transfers between devices with their start and end apart: 13, of which 9 were waited for; matrix products, arithmetic and copies ran while one was open for 12% of the time, Pallas kernels for 23%

profile of v2, /device:TPU:0, one launch (start us, length us, event | category | flops | bytes accessed | tf_op | source)
XLA Modules:
  0.0 652.3 jit_solution(1327991621262119777)
XLA Ops:
  7.2 0.7 stack.12
  7.9 0.7 stack.13
  8.6 0.7 stack.14
  9.2 0.7 stack.15
  9.9 0.7 concatenate.25
  10.7 2.4 fusion.2
  15.4 1.1 copy.202
  16.5 1.1 copy.213
  17.6 1.1 add_select_fusion.1
  19.1 1.1 add_select_fusion
  20.8 8.6 %shard_map.221 = bf16[8,384,768]{2,1,0:T(8,128)(2,1)S(1)} custom-call(s32[2,1248]{1,0:T(2,128)S(1)} %bitcast.58, bf16[6,197,768]{2,1,0:T(8,128)(2,1)S(1)} %copy-done.5), custom_call_target="tpu_custom_call" | custom-call | tf_op jit(solution)/shard_map/pallas_call | solution.py:103
  29.5 2.1 copy-done
  31.6 7.5 %all-to-all-start.1 = ((bf16[8,384,768]{2,1,0:T(8,128)(2,1)}), bf16[8,384,768]{2,1,0:T(8,128)(2,1)}, u32[]{:S(2)}, u32[]{:S(2)}) async-start(bf16[8,384,768]{2,1,0:T(8,128)(2,1)} %copy-done), calls=%async_computation.1 | async-start | bytes 9437184 | tf_op jit(solution)/shard_map/all_to_all | solution.py:432
  39.1 0.7 all-gather.8.cloned.1.call-update
  40.4 14.2 %all-gather.6.cloned.1.call-done.qkv_weight_ref.out_weight_ref.router_ref.refs_7_.refs_8_ = bf16[768,3200]{1,0:T(8,128)(2,1)} async-done(((bf16[192,3200]{1,0:T(8,128)(2,1)}), bf16[768,3200]{1,0:T(8,128)(2,1)}) %all-gather.6.cloned.1.call-update) | async-done | bytes 4915216 | tf_op jit(solution)/shard_map/all_gather | solution.py:467
  54.6 1.0 slice.51
  55.8 1.5 copy-done.3
  57.3 22.9 %shard_map.222 = (bf16[6,208,2304]{2,1,0:T(8,128)(2,1)}, bf16[6,208,768]{2,1,0:T(8,128)(2,1)S(1)}, f32[6,208,768]{2,1,0:T(8,128)S(1)}, bf16[6,208,768]{2,1,0:T(8,128)(2,1)S(1)}, bf16[6,208,768]{2,1,0:T(8,128)(2,1)S(1)}) custom-call(bf16[6,197,768]{2,1,0:T(8,128)(2,1)S(1)} %copy-done.3, ...), custom_call_target="tpu_custom_call" | custom-call | tf_op jit(solution)/shard_map/pallas_call | solution.py:164
  80.2 2.1 copy-done.1
  82.3 1.3 copy-done.7
  83.5 1.3 copy-done.9
  84.8 5.8 shard_map.224
  90.7 52.9 %all-to-all-done.1.g_ref = bf16[8,384,768]{2,1,0:T(8,128)(2,1)} async-done(((bf16[8,384,768]{2,1,0:T(8,128)(2,1)}), bf16[8,384,768]{2,1,0:T(8,128)(2,1)}, u32[]{:S(2)}, u32[]{:S(2)}) %all-to-all-start.1) | async-done | bytes 4718624 | tf_op jit(solution)/shard_map/all_to_all | solution.py:432
  143.5 4.4 all-to-all-start.2
  148.0 0.7 all-gather.10.cloned.1.call-update
  148.7 5.9 shard_map.223
  154.6 46.8 %all-to-all-done.2.x_ref = bf16[8,192,768]{2,1,0:T(8,128)(2,1)} async-done(((bf16[8,192,768]{2,1,0:T(8,128)(2,1)}), bf16[8,192,768]{2,1,0:T(8,128)(2,1)}, u32[]{:S(2)}, u32[]{:S(2)}) %all-to-all-start.2) | async-done | bytes 2359328 | tf_op jit(solution)/shard_map/all_to_all | solution.py:432
  201.3 4.6 all-to-all-start
  206.0 0.6 iota.7.mine_ref
  206.6 44.9 %shard_map.225 = (bf16[2,1536,3072]{2,1,0:T(8,128)(2,1)}, bf16[2,1536,3072]{2,1,0:T(8,128)(2,1)}, bf16[2,1536,768]{2,1,0:T(8,128)(2,1)}, bf16[2,1536,768]{2,1,0:...) custom-call(f32[8,128]{1,0:T(8,128)} %iota.7.mine_ref, ...), custom_call_target="tpu_custom_call" | custom-call | tf_op jit(solution)/shard_map/pallas_call | solution.py:272
  251.4 7.9 %all-to-all-done.x_ref = bf16[8,192,768]{2,1,0:T(8,128)(2,1)} async-done(((bf16[8,192,768]{2,1,0:T(8,128)(2,1)}), bf16[8,192,768]{2,1,0:T(8,128)(2,1)}, u32[]{:S(2)}, u32[]{:S(2)}) %all-to-all-start) | async-done | bytes 2359328 | tf_op jit(solution)/shard_map/all_to_all | solution.py:432
  259.3 45.3 %shard_map.226 = (bf16[2,1536,3072]{2,1,0:T(8,128)(2,1)}, bf16[2,1536,3072]{2,1,0:T(8,128)(2,1)}, bf16[2,1536,768]{2,1,0:T(8,128)(2,1)}, bf16[2,1536,768]{2,1,0:...) custom-call(f32[8,128]{1,0:T(8,128)} %iota.7.mine_ref, ...), custom_call_target="tpu_custom_call", output_to_operand_aliasing={{0}: (6, {}), {1}: (7, {}), {2}: (8, {}), {3}: (9, {}), {4}... | custom-call | tf_op jit(solution)/shard_map/pallas_call | solution.py:272
  304.6 57.9 %all_to_all.30 = bf16[8,192,768]{2,1,0:T(8,128)(2,1)} all-to-all(bf16[8,192,768]{2,1,0:T(8,128)(2,1)} %get-tuple-element.58), channel_id=1, replica_groups=mesh['expert'=8,'shard'=4] {'expert'}, dimensions={0} | all-to-all | bytes 4718592 | tf_op jit(solution)/shard_map/all_to_all | solution.py:432
  362.5 4.4 all-to-all-start.3
  366.9 21.1 %bitcast_convert_fusion = bf16[3072,768]{1,0:T(8,128)(2,1)} fusion(bf16[2,1536,3072]{2,1,0:T(8,128)(2,1)} %get-tuple-element.63, bf16[2,1536,768]{2,1,0:T(8,128)(2,1)} %get-tuple-element.64), kind=kOutput, calls=%fused_computation | convolution fusion | flops 14497873920 | bytes 28311552 | tf_op jit(solution)/shard_map/dot_general | solution.py:23
  388.0 3.8 convolution_bitcast_fusion
  391.8 21.0 %bitcast_convert_fusion.1 = bf16[3072,768]{1,0:T(8,128)(2,1)} fusion(bf16[2,1536,3072]{2,1,0:T(8,128)(2,1)} %get-tuple-element.61, bf16[2,1536,768]{2,1,0:T(8,128)(2,1)} %get-tuple-element.62), kind=kOutput, calls=%fused_computation.1 | convolution fusion | flops 14497873920 | bytes 28311552 | tf_op jit(solution)/shard_map/dot_general | solution.py:23
  412.7 7.0 %all-to-all-done.3 = bf16[8,192,768]{2,1,0:T(8,128)(2,1)} async-done(((bf16[8,192,768]{2,1,0:T(8,128)(2,1)}), bf16[8,192,768]{2,1,0:T(8,128)(2,1)}, u32[]{:S(2)}, u32[]{:S(2)}) %all-to-all-start.3) | async-done | bytes 2359328 | tf_op jit(solution)/shard_map/all_to_all | solution.py:432
  420.4 0.9 copy-done.4
  421.3 1.5 copy-done.6
  422.8 50.1 %shard_map.228 = (bf16[6,197,768]{2,1,0:T(8,128)(2,1)}, bf16[6,208,768]{2,1,0:T(8,128)(2,1)}, bf16[6,208,2304]{2,1,0:T(8,128)(2,1)}, f32[8,768]{1,0:T(8,128)S(1)}) custom-call(s32[6,208,4]{2,1,0:T(8,128)S(1)} %pad.24.refs_0_, bf16[1536,768]{1,0:T(8,128)(2,1)} %bitcast.8.refs_1_, bf16[1536,768]{1,0:T(8,128)(2,1)} %bitcast.63, ...), custom_call_target="tpu_custom_call" | custom-call | tf_op jit(solution)/shard_map/pallas_call | solution.py:367
  473.0 4.8 all-to-all-start.5
  477.9 3.8 bitcast_convert_fusion.3
  481.7 0.8 copy-done.24
  482.5 5.4 bitcast_convert_fusion.2
  488.5 1.9 dynamic-slice_bitcast_fusion
  490.3 1.1 copy-done.11
  491.4 4.9 collective-permute-done
  496.3 2.2 convert_add_fusion
  498.5 2.2 copy-done.12
  500.9 1.7 collective-permute-start.1
  502.6 39.5 %collective-permute-done.1 = bf16[192,3200]{1,0:T(8,128)(2,1)S(1)} collective-permute-done((bf16[192,3200]{1,0:T(8,128)(2,1)S(1)}, bf16[192,3200]{1,0:T(8,128)(2,1)S(1)}, u32[]{:S(2)}, u32[]{:S(2)}) %collective-permute-start.1) | collective-permute-done | bytes 1228832 | tf_op jit(solution)/shard_map/ppermute | solution.py:427
  542.1 2.9 fusion
  545.1 51.5 %all-to-all-done.5 = bf16[8,384,768]{2,1,0:T(8,128)(2,1)} async-done(((bf16[8,384,768]{2,1,0:T(8,128)(2,1)}), bf16[8,384,768]{2,1,0:T(8,128)(2,1)}, u32[]{:S(2)}, u32[]{:S(2)}) %all-to-all-start.5) | async-done | bytes 4718624 | tf_op jit(solution)/shard_map/all_to_all | solution.py:432
  596.6 2.1 copy-done.2
  598.7 11.5 %shard_map.227 = bf16[6,197,768]{2,1,0:T(8,128)(2,1)} custom-call(s32[6,208,2]{2,1,0:T(8,128)S(1)} %pad.23.codes_ref, bf16[3072,768]{1,0:T(8,128)(2,1)} %bitcast.10.refs_0_, f32[6,208,768]{2,1,0:T(8,128)S(1)} %copy-done.2), custom_call_target="tpu_custom_call" | custom-call | tf_op jit(solution)/shard_map/pallas_call | solution.py:399
  610.5 3.8 copy.223
  614.4 3.8 copy.224
  618.2 21.5 %all-reduce.7.cloned.1.call-done = bf16[192,3200]{1,0:T(8,128)(2,1)} async-done(((bf16[192,3200]{1,0:T(8,128)(2,1)}), bf16[192,3200]{1,0:T(8,128)(2,1)}) %all-reduce.7.cloned.1.call-update) | async-done | bytes 1228816 | tf_op jit(solution)/shard_map/psum | solution.py:539
  639.7 1.5 convert_element_type.54
  641.3 0.9 slice_reduce_fusion
  642.2 0.7 copy.222
  642.9 1.3 slice.57
  644.2 0.9 slice.58
  (81 shorter events, 6.2 us)
Async XLA Ops:
  7.2 6.0 copy-start.21
  7.2 7.0 %copy-start.22 = (s32[6,197,2]{1,2,0:T(2,128)S(1)}, s32[6,197,2]{1,2,0:T(2,128)}, u32[]{:S(2)}) copy-start(s32[6,197,2]{1,2,0:T(2,128)} %param.24) | copy-start | bytes 28372
  7.2 47.4 %all-gather.6.cloned.1.call-start = ((), (), s32[]{:S(2)}) async-start(), calls=%async_computation.8 | async-start | bytes 6144000 | tf_op jit(solution)/shard_map/all_gather | solution.py:467
  10.7 3.7 copy-start.23
  17.6 1.1 copy-start.16
  17.6 1.5 copy-start.17
  19.1 1.7 copy-start.5
  29.5 2.1 copy-start
  31.6 8.2 %copy-start.14 = (s32[6,197,2]{2,1,0:T(8,128)S(1)}, s32[6,197,2]{2,1,0:T(8,128)}, u32[]{:S(2)}) copy-start(s32[6,197,2]{2,1,0:T(8,128)} %get-tuple-element.153) | copy-start | bytes 28372
  31.6 8.2 %copy-start.15 = (s32[6,197,2]{2,1,0:T(8,128)S(1)}, s32[6,197,2]{2,1,0:T(8,128)}, u32[]{:S(2)}) copy-start(s32[6,197,2]{2,1,0:T(8,128)} %get-tuple-element.155) | copy-start | bytes 28372
  31.6 111.9 %all-to-all-start.1 = ((bf16[8,384,768]{2,1,0:T(8,128)(2,1)}), bf16[8,384,768]{2,1,0:T(8,128)(2,1)}, u32[]{:S(2)}, u32[]{:S(2)}) async-start(bf16[8,384,768]{2,1,0:T(8,128)(2,1)} %copy-done), calls=%async_computation.1 | async-start | bytes 9437184 | tf_op jit(solution)/shard_map/all_to_all | solution.py:432
  39.1 166.9 %all-gather.8.cloned.1.call-start = ((), (), s32[]{:S(2)}) async-start(), calls=%async_computation.12 | async-start | bytes 5898240 | tf_op jit(solution)/shard_map/all_gather | solution.py:495
  55.8 1.5 copy-start.3
  80.2 2.1 copy-start.1
  82.3 1.3 copy-start.7
  83.5 1.3 copy-start.9
  143.5 57.8 %all-to-all-start.2 = ((bf16[8,192,768]{2,1,0:T(8,128)(2,1)}), bf16[8,192,768]{2,1,0:T(8,128)(2,1)}, u32[]{:S(2)}, u32[]{:S(2)}) async-start(bf16[8,192,768]{2,1,0:T(8,128)(2,1)} %shard_map.224), calls=%async_computation.2 | async-start | bytes 4718592 | tf_op jit(solution)/shard_map/all_to_all | solution.py:432
  148.0 58.0 %all-gather.10.cloned.1.call-start = ((), (), s32[]{:S(2)}) async-start(), calls=%async_computation.13 | async-start | bytes 5898240 | tf_op jit(solution)/shard_map/all_gather | solution.py:496
  201.3 58.0 %all-to-all-start = ((bf16[8,192,768]{2,1,0:T(8,128)(2,1)}), bf16[8,192,768]{2,1,0:T(8,128)(2,1)}, u32[]{:S(2)}, u32[]{:S(2)}) async-start(bf16[8,192,768]{2,1,0:T(8,128)(2,1)} %shard_map.223), calls=%async_computation | async-start | bytes 4718592 | tf_op jit(solution)/shard_map/all_to_all | solution.py:432
  362.5 57.3 %all-to-all-start.3 = ((bf16[8,192,768]{2,1,0:T(8,128)(2,1)}), bf16[8,192,768]{2,1,0:T(8,128)(2,1)}, u32[]{:S(2)}, u32[]{:S(2)}) async-start(bf16[8,192,768]{2,1,0:T(8,128)(2,1)} %get-tuple-element.57), calls=%async_computation.3 | async-start | bytes 4718592 | tf_op jit(solution)/shard_map/all_to_all | solution.py:432
  366.8 178.2 %reduce-scatter.3.cloned.1.call-start = ((), (), s32[]{:S(2)}) async-start(), calls=%async_computation.9 | async-start | bytes 5898240 | tf_op jit(solution)/shard_map/reduce_scatter | solution.py:525
  366.9 21.1 %copy-start.20 = (bf16[2,1536,128]{2,1,0:T(8,128)(2,1)S(1)}, bf16[2,1536,128]{2,1,0:T(8,128)(2,1)}, u32[]{:S(2)}) copy-start(bf16[2,1536,128]{2,1,0:T(8,128)(2,1)} %get-tuple-element.65) | copy-start | bytes 2359300
  419.8 1.5 copy-start.4
  419.8 125.3 %reduce-scatter.5.cloned.1.call-start = ((), (), s32[]{:S(2)}) async-start(), calls=%async_computation.10 | async-start | bytes 5898240 | tf_op jit(solution)/shard_map/reduce_scatter | solution.py:524
  421.3 1.5 copy-start.6
  473.0 4.8 copy-start.10
  473.0 123.5 %all-to-all-start.5 = ((bf16[8,384,768]{2,1,0:T(8,128)(2,1)}), bf16[8,384,768]{2,1,0:T(8,128)(2,1)}, u32[]{:S(2)}, u32[]{:S(2)}) async-start(bf16[8,384,768]{2,1,0:T(8,128)(2,1)} %get-tuple-element.59), calls=%async_computation.5 | async-start | bytes 9437184 | tf_op jit(solution)/shard_map/all_to_all | solution.py:432
  477.8 161.9 %all-reduce.7.cloned.1.call-start = ((), (), s32[]{:S(2)}) async-start(), calls=%async_computation.11 | async-start | bytes 2457600 | tf_op jit(solution)/shard_map/psum | solution.py:539
  477.9 3.8 copy-start.8
  477.9 4.6 copy-start.24
  488.5 3.0 copy-start.11
  491.4 4.9 collective-permute-start
  498.5 2.3 copy-start.12
  500.9 41.3 %collective-permute-start.1 = (bf16[192,3200]{1,0:T(8,128)(2,1)S(1)}, bf16[192,3200]{1,0:T(8,128)(2,1)S(1)}, u32[]{:S(2)}, u32[]{:S(2)}) collective-permute-start(bf16[192,3200]{1,0:T(8,128)(2,1)S(1)} %fusion.3), channel_id=1, source_target_pairs={{0,2},{1,3},{2,0},{3,1},{4,6},{5,7},{6,4},{7,5},{8,10},{9,11},{10,... | collective-permute-start | bytes 3686408 | tf_op jit(solution)/shard_map/ppermute | solution.py:427
  596.6 2.1 copy-start.2
  598.7 11.5 %copy-start.18 = (bf16[768,768]{1,0:T(8,128)(2,1)S(1)}, bf16[768,768]{1,0:T(8,128)(2,1)}, u32[]{:S(2)}) copy-start(bf16[768,768]{1,0:T(8,128)(2,1)} %reduce-scatter.3.cloned.1.call-done) | copy-start | bytes 3538948
  598.7 11.5 %copy-start.19 = (bf16[768,768]{1,0:T(8,128)(2,1)S(1)}, bf16[768,768]{1,0:T(8,128)(2,1)}, u32[]{:S(2)}) copy-start(bf16[768,768]{1,0:T(8,128)(2,1)} %reduce-scatter.5.cloned.1.call-done) | copy-start | bytes 3538948
  639.7 2.5 copy-start.13
Sparse Core Ops, SparseCore 0:
  13.3 41.2 all-gather.5
  56.1 37.4 all-gather.7
  150.3 38.8 all-gather.9
  419.9 46.9 reduce-scatter.2
  469.4 59.9 reduce-scatter.4
  545.2 94.4 all-reduce.6

commit v3 on v2

--- a/solution.py
+++ b/solution.py
@@ -27,7 +27,11 @@
     return pl.BlockSpec(shape, lambda *_: (0,) * len(shape), pipeline_mode=pl.Buffered(1))
 
 
-def call(kernel, grid, in_specs, out_specs, out_shape, scratch, limit):
+def cost(products, moved, powers=0):
+    return pl.CostEstimate(flops=2 * products, transcendentals=powers, bytes_accessed=moved)
+
+
+def call(kernel, grid, in_specs, out_specs, out_shape, scratch, limit, estimate):
     return pl.pallas_call(
         kernel,
         grid=grid,
@@ -35,6 +39,7 @@
         out_specs=out_specs,
         out_shape=out_shape,
         scratch_shapes=scratch,
+        cost_estimate=estimate,
         compiler_params=pltpu.CompilerParams(
             vmem_limit_bytes=limit * MIB,
             dimension_semantics=("arbitrary",) * len(grid),
@@ -62,10 +67,30 @@
 
 
 def padded_rows(source, buffer):
-    length = source.shape[1]
+    group, length, _ = source.shape
+    padded = buffer.shape[0] // group
     buffer[...] = jnp.zeros_like(buffer)
-    buffer[0:length, :] = source[0].astype(buffer.dtype)
+    for image in range(group):
+        buffer[image * padded : image * padded + length, :] = source[image].astype(buffer.dtype)
     return buffer[...]
+
+
+def group_of(images):
+    return 2 if images % 2 == 0 else 1
+
+
+def stacked(tile, lane, heads):
+    return jnp.concatenate(
+        [jnp.where(lane == head, tile, 0.0) for head in range(heads)], 0
+    ).astype(BF16)
+
+
+def unstacked(rows, lane, heads):
+    count = rows.shape[0] // heads
+    result = rows[0:count, :]
+    for head in range(1, heads):
+        result = jnp.where(lane == head, rows[head * count : (head + 1) * count, :], result)
+    return result
 
 
 def send_images_kernel(codes_ref, source_ref, out_ref, rows):
@@ -108,6 +133,7 @@
         jax.ShapeDtypeStruct((experts, count, width), BF16),
         scratch,
         40,
+        cost(experts * count * tokens * width, 2 * (tokens + experts * count) * width),
     )(codes, source)
 
 
@@ -126,46 +152,47 @@
     tokens_ref, qkv_weight_ref, out_weight_ref, vector_ref,
     qkv_ref, mixed_ref, attended_ref, first_ref, second_ref, buffer,
 ):
-    length = tokens_ref.shape[1]
-    padded, width = buffer.shape
+    group, length, width = tokens_ref.shape
+    padded = buffer.shape[0] // group
     value = padded_rows(tokens_ref, buffer)
     unit, _ = normal(value)
     first = (unit * vector_ref[0:1, :] + vector_ref[1:2, :]).astype(BF16)
-    first_ref[0] = first
-    qkv_ref[0] = dot(first, qkv_weight_ref[...]).astype(BF16)
+    first_ref[...] = first.reshape(group, padded, width)
+    qkv = dot(first, qkv_weight_ref[...]).astype(BF16)
+    qkv_ref[...] = qkv.reshape(group, padded, 3 * width)
     scale = (width // HEADS) ** (-0.5)
-    per_tile = LANES * HEADS // width
+    heads = LANES * HEADS // width
     lane = lax.broadcasted_iota(jnp.int32, (padded, LANES), 1) // (width // HEADS)
-    real = lax.broadcasted_iota(jnp.int32, (padded, padded), 1) < length
-    for tile in range(width // LANES):
-        at = tile * LANES
-        query = qkv_ref[0, :, at : at + LANES]
-        keys = qkv_ref[0, :, width + at : width + at + LANES]
-        values = qkv_ref[0, :, 2 * width + at : 2 * width + at + LANES]
-        result = None
-        for head in range(per_tile):
-            chosen = jnp.where(lane == head, query.astype(F32) * scale, 0.0).astype(BF16)
-            scores = jnp.where(real, dot(chosen, keys, NT), -1e30)
+    real = lax.broadcasted_iota(jnp.int32, (heads * padded, padded), 1) < length
+    for image in range(group):
+        for at in range(0, width, LANES):
+            query = qkv_ref[image, :, at : at + LANES].astype(F32) * scale
+            keys = qkv_ref[image, :, width + at : width + at + LANES]
+            values = qkv_ref[image, :, 2 * width + at : 2 * width + at + LANES]
+            scores = jnp.where(real, dot(stacked(query, lane, heads), keys, NT), -1e30)
             raised = jnp.exp(scores - jnp.max(scores, -1, keepdims=True))
             probs = raised * (1.0 / jnp.sum(raised, -1, keepdims=True))
-            part = dot(probs.astype(BF16), values)
-            result = part if result is None else jnp.where(lane == head, part, result)
-        mixed_ref[0, :, at : at + LANES] = result.astype(BF16)
-    attended = value + dot(mixed_ref[0], out_weight_ref[...])
-    attended_ref[0] = attended
+            result = unstacked(dot(probs.astype(BF16), values), lane, heads)
+            mixed_ref[image, :, at : at + LANES] = result.astype(BF16)
+    mixed = mixed_ref[...].reshape(group * padded, width)
+    attended = buffer[...] + dot(mixed, out_weight_ref[...])
+    attended_ref[...] = attended.reshape(group, padded, width)
     unit, _ = normal(attended)
-    second_ref[0] = (unit * vector_ref[2:3, :] + vector_ref[3:4, :]).astype(BF16)
+    second = (unit * vector_ref[2:3, :] + vector_ref[3:4, :]).astype(BF16)
+    second_ref[...] = second.reshape(group, padded, width)
 
 
 def attend(tokens, weights, vectors, padded):
     images, length, width = tokens.shape
-    image = lambda cols: pl.BlockSpec((1, padded, cols), lambda i: (i, 0, 0))
+    group = group_of(images)
+    rows = images * padded
+    image = lambda cols: pl.BlockSpec((group, padded, cols), lambda i: (i, 0, 0))
     shape = lambda cols, kind: jax.ShapeDtypeStruct((images, padded, cols), kind)
     return call(
         attend_kernel,
-        (images,),
+        (images // group,),
         [
-            pl.BlockSpec((1, length, width), lambda i: (i, 0, 0)),
+            pl.BlockSpec((group, length, width), lambda i: (i, 0, 0)),
             pl.BlockSpec((width, 3 * width), lambda i: (0, 0), pipeline_mode=pl.Buffered(1)),
             pl.BlockSpec((width, width), lambda i: (0, 3), pipeline_mode=pl.Buffered(1)),
             whole(vectors.shape),
@@ -175,8 +202,13 @@
             shape(3 * width, BF16), shape(width, BF16), shape(width, F32),
             shape(width, BF16), shape(width, BF16),
         ],
-        [pltpu.VMEM((padded, width), F32)],
-        40,
+        [pltpu.VMEM((group * padded, width), F32)],
+        44,
+        cost(
+            rows * width * (4 * width + 4 * padded),
+            rows * width * 18 + width * width * 8,
+            rows * padded * HEADS,
+        ),
     )(tokens, weights, weights, vectors)
 
 
@@ -287,6 +319,7 @@
         scratch_shapes=[
             pltpu.VMEM((rows, width), F32), pltpu.VMEM((rows, width), F32), pltpu.VMEM((rows, LANES), F32)
         ],
+        cost_estimate=cost(4 * rows * width * hidden, 8 * rows * hidden, rows * hidden),
         input_output_aliases={6 + index: index for index in range(len(kept))},
         compiler_params=pltpu.CompilerParams(
             vmem_limit_bytes=56 * MIB, dimension_semantics=("arbitrary",)
@@ -300,73 +333,79 @@
     (
         cotangent_ref, tokens_ref, attended_ref, qkv_ref,
         qkv_weight_ref, out_weight_ref, vector_ref,
-        tokens_grad_ref, branch_ref, rows_grad_ref, sums_ref, buffer,
+        tokens_grad_ref, branch_ref, rows_grad_ref, sums_ref, buffer, mixed_grad_ref,
     ) = refs
-    length = tokens_ref.shape[1]
-    padded, width = buffer.shape
+    group, length, width = tokens_ref.shape
+    padded = buffer.shape[0] // group
 
     @pl.when(pl.program_id(0) == 0)
     def _():
         sums_ref[...] = jnp.zeros_like(sums_ref)
 
-    second_grad = gather_rows(codes_ref[0], returned)
-    unit, inverse = normal(attended_ref[0])
+    codes = codes_ref[...].reshape(group * padded, codes_ref.shape[2])
+    second_grad = gather_rows(codes, returned)
+    unit, inverse = normal(attended_ref[...].reshape(group * padded, width))
     sums_ref[2:3, :] += jnp.sum(second_grad * unit, 0, keepdims=True)
     sums_ref[3:4, :] += jnp.sum(second_grad, 0, keepdims=True)
     attended_grad = padded_rows(cotangent_ref, buffer) + norm_back(
         second_grad, vector_ref[2:3, :], unit, inverse
     )
+    buffer[...] = attended_grad
     branch = attended_grad.astype(BF16)
-    branch_ref[0] = branch
-    mixed_grad = dot(branch, out_weight_ref[...], NT).astype(BF16)
+    branch_ref[...] = branch.reshape(group, padded, width)
+    mixed_grad_ref[...] = (
+        dot(branch, out_weight_ref[...], NT).astype(BF16).reshape(group, padded, width)
+    )
     scale = (width // HEADS) ** (-0.5)
-    per_tile = LANES * HEADS // width
+    heads = LANES * HEADS // width
     lane = lax.broadcasted_iota(jnp.int32, (padded, LANES), 1) // (width // HEADS)
-    real = lax.broadcasted_iota(jnp.int32, (padded, padded), 0) < length
-    for tile in range(width // LANES):
-        at = tile * LANES
-        query = qkv_ref[0, :, at : at + LANES].astype(F32) * scale
-        keys = qkv_ref[0, :, width + at : width + at + LANES]
-        values = qkv_ref[0, :, 2 * width + at : 2 * width + at + LANES]
-        keys_scaled = keys.astype(F32) * scale
-        result = mixed_grad[:, at : at + LANES].astype(F32)
-        grads = [None, None, None]
-        for head in range(per_tile):
-            own = lane == head
-            own_query = jnp.where(own, query, 0.0).astype(BF16)
-            own_keys = jnp.where(own, keys_scaled, 0.0).astype(BF16)
-            own_result = jnp.where(own, result, 0.0).astype(BF16)
-            scores = jnp.where(real, dot(keys, own_query, NT), -1e30)
+    real = lax.broadcasted_iota(jnp.int32, (padded, heads * padded), 0) < length
+    for image in range(group):
+        for at in range(0, width, LANES):
+            query = qkv_ref[image, :, at : at + LANES].astype(F32) * scale
+            keys = qkv_ref[image, :, width + at : width + at + LANES]
+            values = qkv_ref[image, :, 2 * width + at : 2 * width + at + LANES]
+            result = mixed_grad_ref[image, :, at : at + LANES].astype(F32)
+            queries = stacked(query, lane, heads)
+            results = stacked(result, lane, heads)
+            scores = jnp.where(real, dot(keys, queries, NT), -1e30)
+            prob_grad = dot(values, results, NT)
             raised = jnp.exp(scores - jnp.max(scores, 0, keepdims=True))
             probs = raised * (1.0 / jnp.sum(raised, 0, keepdims=True))
-            prob_grad = dot(values, own_result, NT)
             score_grad = (
                 probs * (prob_grad - jnp.sum(probs * prob_grad, 0, keepdims=True))
             ).astype(BF16)
-            parts = (
-                dot(score_grad, own_keys, TN),
-                dot(score_grad, own_query),
-                dot(probs.astype(BF16), own_result),
+            keys_scaled = (keys.astype(F32) * scale).astype(BF16)
+            grads = (
+                unstacked(dot(score_grad, keys_scaled, TN), lane, heads),
+                dot(score_grad, queries),
+                dot(probs.astype(BF16), results),
             )
-            grads = [part if old is None else old + part for old, part in zip(grads, parts)]
-        for index, grad in enumerate(grads):
-            start = index * width + at
-            rows_grad_ref[0, :, start : start + LANES] = grad.astype(BF16)
-    first_grad = dot(rows_grad_ref[0], qkv_weight_ref[...], NT)
+            for index, grad in enumerate(grads):
+                start = index * width + at
+                rows_grad_ref[image, :, start : start + LANES] = grad.astype(BF16)
+    rows_grad = rows_grad_ref[...].reshape(group * padded, 3 * width)
+    first_grad = dot(rows_grad, qkv_weight_ref[...], NT)
+    attended_grad = buffer[...]
     unit, inverse = normal(padded_rows(tokens_ref, buffer))
     sums_ref[0:1, :] += jnp.sum(first_grad * unit, 0, keepdims=True)
     sums_ref[1:2, :] += jnp.sum(first_grad, 0, keepdims=True)
     tokens_grad = attended_grad + norm_back(first_grad, vector_ref[0:1, :], unit, inverse)
-    tokens_grad_ref[0] = tokens_grad[0:length, :].astype(BF16)
+    for image in range(group):
+        tokens_grad_ref[image] = tokens_grad[
+            image * padded : image * padded + length, :
+        ].astype(BF16)
 
 
 def attend_back(codes, returned, cotangent, tokens, attended, qkv, weights, vectors):
     images, length, width = tokens.shape
     padded = attended.shape[1]
-    image = lambda rows, cols: pl.BlockSpec((1, rows, cols), lambda i: (i, 0, 0))
+    group = group_of(images)
+    rows = images * padded
+    image = lambda count, cols: pl.BlockSpec((group, count, cols), lambda i: (i, 0, 0))
     return call(
         attend_back_kernel,
-        (images,),
+        (images // group,),
         [image(padded, codes.shape[2])]
         + [whole(array.shape) for array in returned]
         + [
@@ -382,23 +421,33 @@
             jax.ShapeDtypeStruct((images, padded, 3 * width), BF16),
             jax.ShapeDtypeStruct((8, width), F32),
         ],
-        [pltpu.VMEM((padded, width), F32)],
-        48,
+        [pltpu.VMEM((group * padded, width), F32), pltpu.VMEM((group, padded, width), BF16)],
+        56,
+        cost(
+            rows * width * (4 * width + 10 * padded + CHUNKS * returned[0].shape[0]),
+            rows * width * 24 + width * (width * 8 + 4 * returned[0].shape[0]),
+            rows * padded * HEADS,
+        ),
     )(codes, *returned, cotangent, tokens, attended, qkv, weights, weights, vectors)
 
 
 def combine_kernel(codes_ref, *refs):
     *returned, attended_ref, out_ref = refs
-    total = attended_ref[0] + gather_rows(codes_ref[0], returned)
-    out_ref[0] = total[0 : out_ref.shape[1], :].astype(BF16)
+    group, padded, width = attended_ref.shape
+    codes = codes_ref[...].reshape(group * padded, codes_ref.shape[2])
+    total = attended_ref[...].reshape(group * padded, width) + gather_rows(codes, returned)
+    for image in range(group):
+        at = image * padded
+        out_ref[image] = total[at : at + out_ref.shape[1], :].astype(BF16)
 
 
 def combine(codes, returned, attended, length):
     images, padded, width = attended.shape
-    image = lambda rows, cols: pl.BlockSpec((1, rows, cols), lambda i: (i, 0, 0))
+    group = group_of(images)
+    image = lambda rows, cols: pl.BlockSpec((group, rows, cols), lambda i: (i, 0, 0))
     return call(
         combine_kernel,
-        (images,),
+        (images // group,),
         [image(padded, codes.shape[2])]
         + [whole(array.shape) for array in returned]
         + [image(padded, width)],
@@ -406,6 +455,10 @@
         jax.ShapeDtypeStruct((images, length, width), BF16),
         [],
         40,
+        cost(
+            images * padded * width * sum(array.shape[0] for array in returned),
+            images * padded * width * 8,
+        ),
     )(codes, *returned, attended)
 
 
@@ -426,6 +479,14 @@
         moves = [(s, (s // 2 + shift) % pairs * 2 + s % 2) for s in range(size)]
         total = total + lax.ppermute(part, "shard", moves).astype(F32)
     return total.astype(BF16)
+
+
+def sum_experts(array):
+    experts = lax.axis_size("expert")
+    rows, cols = array.shape
+    parts = exchange(array.reshape(experts, rows // experts, cols))
+    share = jnp.sum(parts.astype(F32), 0).astype(BF16)
+    return lax.all_gather(share, "expert", axis=0, tiled=True).astype(F32)
 
 
 def exchange(array):
@@ -535,8 +596,8 @@
         [qkv_full, out_full, jnp.pad(small_full, ((0, 0), (0, spare)))], 1
     ).astype(BF16)
     layer = sum_shards(layer)
-    layer, up_grad, down_grad = lax.optimization_barrier((layer, up_grad, down_grad))
-    layer = lax.psum(layer, "expert").astype(F32)
+    layer, out_returned = lax.optimization_barrier((layer, out_returned))
+    layer = sum_experts(layer)
     block_out = combine(all_codes, [out_returned], attended, length)
     tail = 4 * width + experts
     return (

time: 660 us -> 656 us (level)
  waiting for transfers between devices: 248 us -> 212 us
  blocking collectives: 57.9 us -> 91.4 us
  Pallas kernels: 195 us -> 187 us
    all_to_all x5, waiting for transfers between devices: 166 us -> 123 us  [exchange(): lax.all_to_all(array, 'expert', split_axis=0, concat_axis=0, tiled=True)]
    all_to_all x1 -> x2, blocking collectives: 57.9 us -> 91.4 us  [exchange(): lax.all_to_all(array, 'expert', split_axis=0, concat_axis=0, tiled=True)]
    psum x1 -> x0, waiting for transfers between devices: 21.5 us -> none  [shards(): layer = lax.psum(layer, 'expert').astype(F32)]
    all_gather x0 -> x1, waiting for transfers between devices: none -> 18.1 us  [sum_experts(): return lax.all_gather(share, 'expert', axis=0, tiled=True).astype(F32)]
    ppermute x1, waiting for transfers between devices: 39.5 us -> 52.1 us  [sum_shards(): total = total + lax.ppermute(part, 'shard', moves).astype(F32)]
    pallas_call x3, Pallas kernels: 84.5 us -> 76.5 us  [the longest x1 46 us: attend_back(): call(attend_back_kernel, (images // group,), [image(padded, codes.shape[2...]
    unnamed x56 -> x54, local copies, waits for them, and re-layouts: 26.7 us -> 25.5 us
  transfers between devices with their start and end apart: 13 -> 13, of which waited for: 9 -> 8; matrix products, arithmetic and copies ran while one was open for 12% -> 14% of each run, Pallas kernels for 23% -> 22%
where the time goes in v3:
time: 656 us; the launch traced here: 647 us
  waiting for transfers between devices  212 us (32%)
  Pallas kernels  187 us (29%)
  blocking collectives  91.4 us (14%)
  matrix products  58.5 us (9%)
  local copies, waits for them, and re-layouts  41.1 us (6%)
  starting transfers between devices  26.1 us (4%)
  other arithmetic  16.1 us (2%)
  between operations  14.7 us (2%)
    all_to_all x5, waiting for transfers between devices, exchange(): lax.all_to_all(array, 'expert', split_axis=0, concat_axis=0, tiled=True)  123 us
    all_to_all x2, blocking collectives, exchange(): lax.all_to_all(array, 'expert', split_axis=0, concat_axis=0, tiled=True)  91.4 us
    pallas_call x2, Pallas kernels, run_expert(): pl.pallas_call(functools.partial(expert_kernel, experts, block, len(kept)...  90.1 us
    dot_general x5, matrix products, dot(): return lax.dot_general(a, b, dims, preferred_element_type=F32)  58.5 us
    ppermute x1, waiting for transfers between devices, sum_shards(): total = total + lax.ppermute(part, 'shard', moves).astype(F32)  52.1 us
    pallas_call x1, Pallas kernels, attend_back(): call(attend_back_kernel, (images // group,), [image(padded, codes.shape[2...  46 us
    unnamed x54, local copies, waits for them, and re-layouts  25.5 us
    all_to_all x5, starting transfers between devices, exchange(): lax.all_to_all(array, 'expert', split_axis=0, concat_axis=0, tiled=True)  24.1 us
  transfers between devices with their start and end apart: 13, of which 8 were waited for; matrix products, arithmetic and copies ran while one was open for 14% of the time, Pallas kernels for 22%

profile of v3, /device:TPU:0, one launch (start us, length us, event | category | flops | bytes accessed | tf_op | source)
XLA Modules:
  0.0 647.2 jit_solution(7811006862781181539)
XLA Ops:
  7.2 0.7 stack.12
  9.9 0.7 concatenate.24
  10.7 2.4 fusion.2
  13.2 0.7 all-gather.11.cloned.1.call-update
  16.2 1.1 copy.200
  17.3 1.1 copy.214
  18.4 1.1 add_select_fusion.1
  19.9 1.1 add_select_fusion
  21.6 8.6 %shard_map.221 = bf16[8,384,768]{2,1,0:T(8,128)(2,1)S(1)} custom-call(s32[2,1248]{1,0:T(2,128)S(1)} %bitcast.56, bf16[6,197,768]{2,1,0:T(8,128)(2,1)S(1)} %copy-done.3), custom_call_target="tpu_custom_call" | custom-call | flops 5888802816 | bytes 6635520 | tf_op jit(solution)/shard_map/pallas_call | solution.py:128
  30.2 2.1 copy-done
  32.3 7.5 %all-to-all-start.1 = ((bf16[8,384,768]{2,1,0:T(8,128)(2,1)}), bf16[8,384,768]{2,1,0:T(8,128)(2,1)}, u32[]{:S(2)}, u32[]{:S(2)}) async-start(bf16[8,384,768]{2,1,0:T(8,128)(2,1)} %copy-done), calls=%async_computation.1 | async-start | bytes 9437184 | tf_op jit(solution)/shard_map/all_to_all | solution.py:493
  39.9 0.7 all-gather.13.cloned.1.call-update
  40.6 1.4 pad_add_fusion
  42.4 12.2 %all-gather.7.cloned.1.call-done.qkv_weight_ref.out_weight_ref.router_ref.refs_7_.refs_8_ = bf16[768,3200]{1,0:T(8,128)(2,1)} async-done(((bf16[192,3200]{1,0:T(8,128)(2,1)}), bf16[768,3200]{1,0:T(8,128)(2,1)}) %all-gather.7.cloned.1.call-update) | async-done | bytes 4915216 | tf_op jit(solution)/shard_map/all_gather | solution.py:528
  54.6 1.0 slice.50
  55.8 19.7 %shard_map.222 = (bf16[6,208,2304]{2,1,0:T(8,128)(2,1)}, bf16[6,208,768]{2,1,0:T(8,128)(2,1)S(1)}, f32[6,208,768]{2,1,0:T(8,128)}, bf16[6,208,768]{2,1,0:T(8,128)(2,1)S(1)}, bf16[6,208,768]{2,1,0:T(8,128)(2,1)S(1)}) custom-call(bf16[6,197,768]{2,1,0:T(8,128)(2,1)S(1)} %copy-done.2, ...), custom_call_target="tpu_custom_call" | custom-call | flops 7483686912 | bytes 21970944 | tf_op jit(solution)/shard_map/pallas_call | solution.py:191
  75.5 1.3 copy-done.6
  76.8 1.3 copy-done.9
  78.1 5.8 shard_map.224
  83.9 1.3 copy-done.4
  85.1 59.3 %all-to-all-done.1.g_ref = bf16[8,384,768]{2,1,0:T(8,128)(2,1)} async-done(((bf16[8,384,768]{2,1,0:T(8,128)(2,1)}), bf16[8,384,768]{2,1,0:T(8,128)(2,1)}, u32[]{:S(2)}, u32[]{:S(2)}) %all-to-all-start.1) | async-done | bytes 4718624 | tf_op jit(solution)/shard_map/all_to_all | solution.py:493
  144.4 4.5 all-to-all-start.2
  148.9 5.9 shard_map.223
  154.8 47.5 %all-to-all-done.2.x_ref = bf16[8,192,768]{2,1,0:T(8,128)(2,1)} async-done(((bf16[8,192,768]{2,1,0:T(8,128)(2,1)}), bf16[8,192,768]{2,1,0:T(8,128)(2,1)}, u32[]{:S(2)}, u32[]{:S(2)}) %all-to-all-start.2) | async-done | bytes 2359328 | tf_op jit(solution)/shard_map/all_to_all | solution.py:493
  202.3 3.9 all-to-all-start
  206.9 44.8 %shard_map.225 = (bf16[2,1536,3072]{2,1,0:T(8,128)(2,1)}, bf16[2,1536,3072]{2,1,0:T(8,128)(2,1)}, bf16[2,1536,768]{2,1,0:T(8,128)(2,1)}, bf16[2,1536,768]{2,1,0:...) custom-call(f32[8,128]{1,0:T(8,128)} %iota.7.mine_ref, ...), custom_call_target="tpu_custom_call" | custom-call | flops 28991029248 | bytes 37748736 | tf_op jit(solution)/shard_map/pallas_call | solution.py:304
  251.7 8.5 %all-to-all-done.x_ref = bf16[8,192,768]{2,1,0:T(8,128)(2,1)S(1)} async-done(((bf16[8,192,768]{2,1,0:T(8,128)(2,1)}), bf16[8,192,768]{2,1,0:T(8,128)(2,1)S(1)}, u32[]{:S(2)}, u32[]{:S(2)}) %all-to-all-start) | async-done | bytes 2359328 | tf_op jit(solution)/shard_map/all_to_all | solution.py:493
  260.2 1.4 copy-done.20
  261.6 45.2 %shard_map.226 = (bf16[2,1536,3072]{2,1,0:T(8,128)(2,1)}, bf16[2,1536,3072]{2,1,0:T(8,128)(2,1)}, bf16[2,1536,768]{2,1,0:T(8,128)(2,1)}, bf16[2,1536,768]{2,1,0:...) custom-call(f32[8,128]{1,0:T(8,128)} %iota.7.mine_ref, ...), custom_call_target="tpu_custom_call", output_to_operand_aliasing={{0}: (6, {}), {1}: (7, {}), {2}: (8, {}), {3}: (9, {}), {4}... | custom-call | flops 28991029248 | bytes 37748736 | tf_op jit(solution)/shard_map/pallas_call | solution.py:304
  306.8 57.9 %all_to_all.35 = bf16[8,192,768]{2,1,0:T(8,128)(2,1)} all-to-all(bf16[8,192,768]{2,1,0:T(8,128)(2,1)} %get-tuple-element.63), channel_id=1, replica_groups=mesh['expert'=8,'shard'=4] {'expert'}, dimensions={0} | all-to-all | bytes 4718592 | tf_op jit(solution)/shard_map/all_to_all | solution.py:493
  364.7 3.6 all-to-all-start.3
  368.4 21.1 %bitcast_convert_fusion = bf16[3072,768]{1,0:T(8,128)(2,1)} fusion(bf16[2,1536,3072]{2,1,0:T(8,128)(2,1)} %get-tuple-element.58, bf16[2,1536,768]{2,1,0:T(8,128)(2,1)} %get-tuple-element.59), kind=kOutput, calls=%fused_computation | convolution fusion | flops 14497873920 | bytes 28311552 | tf_op jit(solution)/shard_map/dot_general | solution.py:23
  389.5 4.0 convolution_bitcast_fusion
  393.4 20.9 %bitcast_convert_fusion.1 = bf16[3072,768]{1,0:T(8,128)(2,1)} fusion(bf16[2,1536,3072]{2,1,0:T(8,128)(2,1)} %get-tuple-element.56, bf16[2,1536,768]{2,1,0:T(8,128)(2,1)} %get-tuple-element.57), kind=kOutput, calls=%fused_computation.1 | convolution fusion | flops 14497873920 | bytes 28311552 | tf_op jit(solution)/shard_map/dot_general | solution.py:23
  414.4 7.2 %all-to-all-done.3 = bf16[8,192,768]{2,1,0:T(8,128)(2,1)S(1)} async-done(((bf16[8,192,768]{2,1,0:T(8,128)(2,1)}), bf16[8,192,768]{2,1,0:T(8,128)(2,1)S(1)}, u32[]{:S(2)}, u32[]{:S(2)}) %all-to-all-start.3) | async-done | bytes 2359328 | tf_op jit(solution)/shard_map/all_to_all | solution.py:493
  421.6 1.4 copy-done.19
  423.0 4.6 all-to-all-start.5
  427.7 46.0 %shard_map.227 = (bf16[6,197,768]{2,1,0:T(8,128)(2,1)}, bf16[6,208,768]{2,1,0:T(8,128)(2,1)}, bf16[6,208,2304]{2,1,0:T(8,128)(2,1)}, f32[8,768]{1,0:T(8,128)}) custom-call(s32[6,208,4]{2,1,0:T(8,128)} %copy-done.15, bf16[1536,768]{1,0:T(8,128)(2,1)} %bitcast.63, bf16[1536,768]{1,0:T(8,128)(2,1)} %bitcast.62, bf16[6,197,768]{2,1,0:T(8,128)(2,1)} %refs_3_.1, ...), custom_call_target="tpu_custom_call" | custom-call | flops 15764815872 | bytes 32440320 | tf_op jit(solution)/shard_map/pallas_call | solution.py:406
  473.7 9.1 %bitcast_convert_fusion.2 = bf16[768,2304]{1,0:T(8,128)(2,1)} fusion(bf16[6,208,768]{2,1,0:T(8,128)(2,1)S(1)} %copy-done.10, bf16[6,208,2304]{2,1,0:T(8,128)(2,1)} %get-tuple-element.70), kind=kOutput, calls=%fused_computation.2 | convolution fusion | flops 4418371584 | bytes 11206656 | tf_op jit(solution)/shard_map/dot_general | solution.py:23
  482.8 0.7 fusion.7
  483.9 1.3 copy-done.7
  485.2 3.4 bitcast_convert_fusion.3
  489.1 1.9 dynamic-slice_bitcast_fusion
  490.9 1.4 copy-done.11
  492.3 6.2 collective-permute-done
  498.5 2.3 convert_add_fusion
  500.9 2.2 copy-done.12
  503.2 1.8 collective-permute-start.1
  505.0 52.1 %collective-permute-done.1 = bf16[192,3200]{1,0:T(8,128)(2,1)S(1)} collective-permute-done((bf16[192,3200]{1,0:T(8,128)(2,1)S(1)}, bf16[192,3200]{1,0:T(8,128)(2,1)S(1)}, u32[]{:S(2)}, u32[]{:S(2)}) %collective-permute-start.1) | collective-permute-done | bytes 1228832 | tf_op jit(solution)/shard_map/ppermute | solution.py:480
  557.0 1.9 fusion
  558.9 33.5 %all_to_all.36 = bf16[8,24,3200]{2,1,0:T(8,128)(2,1)S(1)} all-to-all(bf16[8,24,3200]{2,1,0:T(8,128)(2,1)S(1)} %bitcast.59), channel_id=1, replica_groups=mesh['expert'=8,'shard'=4] {'expert'}, dimensions={0} | all-to-all | bytes 2457600 | tf_op jit(solution)/shard_map/all_to_all | solution.py:493
  592.4 0.9 reduce_sum.12
  593.3 2.1 copy-done.8
  595.4 10.8 %shard_map.228 = bf16[6,197,768]{2,1,0:T(8,128)(2,1)} custom-call(s32[6,208,2]{2,1,0:T(8,128)S(1)} %pad.23.codes_ref, bf16[3072,768]{1,0:T(8,128)(2,1)} %bitcast.23.refs_0_, f32[6,208,768]{2,1,0:T(8,128)S(1)} %copy-done.8), custom_call_target="tpu_custom_call" | custom-call | flops 5888802816 | bytes 7667712 | tf_op jit(solution)/shard_map/pallas_call | solution.py:448
  606.2 1.5 bitcast_convert_fusion.5
  607.7 3.8 copy.221
  611.5 1.4 bitcast_convert_fusion.4
  612.9 3.8 copy.222
  616.8 18.1 %all-gather.9.cloned.1.call-done = bf16[192,3200]{1,0:T(8,128)(2,1)} async-done(((bf16[24,3200]{1,0:T(8,128)(2,1)}), bf16[192,3200]{1,0:T(8,128)(2,1)}) %all-gather.9.cloned.1.call-update) | async-done | bytes 1228816 | tf_op jit(solution)/shard_map/all_gather | solution.py:489
  634.9 1.5 convert_element_type.56
  636.4 0.9 slice_reduce_fusion
  637.4 0.7 copy.220
  638.0 1.3 slice.57
  639.3 0.9 slice.58
  (82 shorter events, 7.7 us)
Async XLA Ops:
  7.2 47.4 %all-gather.7.cloned.1.call-start = ((), (), s32[]{:S(2)}) async-start(), calls=%async_computation.9 | async-start | bytes 6144000 | tf_op jit(solution)/shard_map/all_gather | solution.py:528
  10.6 3.3 copy-start.21
  10.7 4.2 copy-start.22
  13.1 2.1 copy-start.23
  13.1 193.1 %all-gather.11.cloned.1.call-start = ((), (), s32[]{:S(2)}) async-start(), calls=%async_computation.13 | async-start | bytes 5898240 | tf_op jit(solution)/shard_map/all_gather | solution.py:556
  18.4 1.1 copy-start.17
  18.4 1.5 copy-start.18
  19.8 1.7 copy-start.3
  30.2 2.1 copy-start
  32.3 8.3 %copy-start.16 = (s32[6,197,2]{2,1,0:T(8,128)S(1)}, s32[6,197,2]{2,1,0:T(8,128)}, u32[]{:S(2)}) copy-start(s32[6,197,2]{2,1,0:T(8,128)} %get-tuple-element.151) | copy-start | bytes 28372
  32.3 112.1 %all-to-all-start.1 = ((bf16[8,384,768]{2,1,0:T(8,128)(2,1)}), bf16[8,384,768]{2,1,0:T(8,128)(2,1)}, u32[]{:S(2)}, u32[]{:S(2)}) async-start(bf16[8,384,768]{2,1,0:T(8,128)(2,1)} %copy-done), calls=%async_computation.1 | async-start | bytes 9437184 | tf_op jit(solution)/shard_map/all_to_all | solution.py:493
  39.9 166.4 %all-gather.13.cloned.1.call-start = ((), (), s32[]{:S(2)}) async-start(), calls=%async_computation.14 | async-start | bytes 5898240 | tf_op jit(solution)/shard_map/all_gather | solution.py:557
  40.6 15.1 %copy-start.2 = (bf16[6,197,768]{2,1,0:T(8,128)(2,1)S(1)}, bf16[6,197,768]{2,1,0:T(8,128)(2,1)}, u32[]{:S(2)}) copy-start(bf16[6,197,768]{2,1,0:T(8,128)(2,1)} %refs_4_.1) | copy-start | bytes 5446660
  42.1 33.4 %copy-start.15 = (s32[6,208,4]{2,1,0:T(8,128)}, s32[6,208,4]{2,1,0:T(8,128)S(1)}, u32[]{:S(2)}) copy-start(s32[6,208,4]{2,1,0:T(8,128)S(1)} %pad.27.refs_0_) | copy-start | bytes 59908
  55.8 19.7 %copy-start.1 = (f32[8,768]{1,0:T(8,128)}, f32[8,768]{1,0:T(8,128)S(1)}, u32[]{:S(2)}) copy-start(f32[8,768]{1,0:T(8,128)S(1)} %pad_convert_fusion.vector_ref.refs_9_) | copy-start | bytes 73732
  75.5 1.3 copy-start.6
  76.8 1.3 copy-start.9
  83.9 1.3 copy-start.4
  144.4 4.5 copy-start.5
  144.4 57.9 %all-to-all-start.2 = ((bf16[8,192,768]{2,1,0:T(8,128)(2,1)}), bf16[8,192,768]{2,1,0:T(8,128)(2,1)}, u32[]{:S(2)}, u32[]{:S(2)}) async-start(bf16[8,192,768]{2,1,0:T(8,128)(2,1)} %shard_map.224), calls=%async_computation.2 | async-start | bytes 4718592 | tf_op jit(solution)/shard_map/all_to_all | solution.py:493
  202.3 57.9 %all-to-all-start = ((bf16[8,192,768]{2,1,0:T(8,128)(2,1)}), bf16[8,192,768]{2,1,0:T(8,128)(2,1)S(1)}, u32[]{:S(2)}, u32[]{:S(2)}) async-start(bf16[8,192,768]{2,1,0:T(8,128)(2,1)} %shard_map.223), calls=%async_computation | async-start | bytes 4718592 | tf_op jit(solution)/shard_map/all_to_all | solution.py:493
  260.2 1.4 copy-start.20
  364.7 56.9 %all-to-all-start.3 = ((bf16[8,192,768]{2,1,0:T(8,128)(2,1)}), bf16[8,192,768]{2,1,0:T(8,128)(2,1)S(1)}, u32[]{:S(2)}, u32[]{:S(2)}) async-start(bf16[8,192,768]{2,1,0:T(8,128)(2,1)} %get-tuple-element.62), calls=%async_computation.3 | async-start | bytes 4718592 | tf_op jit(solution)/shard_map/all_to_all | solution.py:493
  368.3 237.9 %reduce-scatter.3.cloned.1.call-start = ((), (), s32[]{:S(2)}) async-start(), calls=%async_computation.11 | async-start | bytes 5898240 | tf_op jit(solution)/shard_map/reduce_scatter | solution.py:586
  421.6 1.4 copy-start.19
  423.0 135.9 %all-to-all-start.5 = ((bf16[8,384,768]{2,1,0:T(8,128)(2,1)}), bf16[8,384,768]{2,1,0:T(8,128)(2,1)}, u32[]{:S(2)}, u32[]{:S(2)}) async-start(bf16[8,384,768]{2,1,0:T(8,128)(2,1)} %get-tuple-element.75), calls=%async_computation.5 | async-start | bytes 9437184 | tf_op jit(solution)/shard_map/all_to_all | solution.py:493
  427.6 183.9 %reduce-scatter.5.cloned.1.call-start = ((), (), s32[]{:S(2)}) async-start(), calls=%async_computation.12 | async-start | bytes 5898240 | tf_op jit(solution)/shard_map/reduce_scatter | solution.py:585
  427.7 46.0 %copy-start.10 = (bf16[6,208,768]{2,1,0:T(8,128)(2,1)S(1)}, bf16[6,208,768]{2,1,0:T(8,128)(2,1)}, u32[]{:S(2)}) copy-start(bf16[6,208,768]{2,1,0:T(8,128)(2,1)} %copy-done.9) | copy-start | bytes 5750788
  483.7 1.5 copy-start.7
  483.7 151.1 %all-gather.9.cloned.1.call-start = ((), (), s32[]{:S(2)}) async-start(), calls=%async_computation.10 | async-start | bytes 1382400 | tf_op jit(solution)/shard_map/all_gather | solution.py:489
  485.2 3.4 copy-start.14
  489.1 3.3 copy-start.11
  492.3 6.2 collective-permute-start
  500.8 2.2 copy-start.12
  503.2 53.8 %collective-permute-start.1 = (bf16[192,3200]{1,0:T(8,128)(2,1)S(1)}, bf16[192,3200]{1,0:T(8,128)(2,1)S(1)}, u32[]{:S(2)}, u32[]{:S(2)}) collective-permute-start(bf16[192,3200]{1,0:T(8,128)(2,1)S(1)} %fusion.3), channel_id=1, source_target_pairs={{0,2},{1,3},{2,0},{3,1},{4,6},{5,7},{6,4},{7,5},{8,10},{9,11},{10,... | collective-permute-start | bytes 3686408 | tf_op jit(solution)/shard_map/ppermute | solution.py:480
  593.3 2.1 copy-start.8
  634.8 2.5 copy-start.13
Sparse Core Ops, SparseCore 0:
  13.2 41.2 all-gather.6
  56.1 37.4 all-gather.10
  95.2 37.4 all-gather.12
  421.7 46.8 reduce-scatter.2
  483.8 75.3 reduce-scatter.4
  593.4 41.3 all-gather.8

commit v4 on v3

--- a/solution.py
+++ b/solution.py
@@ -132,7 +132,7 @@
         pl.BlockSpec((1, count, width), lambda e: (e, 0, 0)),
         jax.ShapeDtypeStruct((experts, count, width), BF16),
         scratch,
-        40,
+        58,
         cost(experts * count * tokens * width, 2 * (tokens + experts * count) * width),
     )(codes, source)
 
@@ -225,8 +225,8 @@
 
 def expert_kernel(experts, block, kept, mine_ref, x_ref, g_ref, up_ref, down_ref, router_ref, *refs):
     (
-        active_ref, before_ref, scaled_ref, x_all_ref, logit_ref, out_ref, back_ref,
-        out_sum, back_sum, probs_ref,
+        out_ref, active_ref, before_ref, scaled_ref, logit_ref, back_ref,
+        out_sum, back_sum, probs_ref, x_all_ref,
     ) = refs[kept:]
     step = pl.program_id(0)
     sources, count, width = x_ref.shape
@@ -241,7 +241,7 @@
         for source in range(sources):
             rows = slice(source * count, (source + 1) * count)
             x = x_ref[source]
-            x_all_ref[0, rows, :] = x
+            x_all_ref[rows, :] = x
             logits = dot(x, router_ref[...])
             column = lax.broadcasted_iota(jnp.int32, logits.shape, 1)
             logits = jnp.where(column < experts, logits, -1e30)
@@ -249,12 +249,12 @@
             probs = raised / jnp.sum(raised, -1, keepdims=True)
             probs_ref[rows, :] = probs
             gate = jnp.sum(probs * mine, -1, keepdims=True)
-            scaled_ref[0, rows, :] = (gate * g_ref[source].astype(F32)).astype(BF16)
+            scaled_ref[rows, :] = (gate * g_ref[source].astype(F32)).astype(BF16)
 
     def first_products(index):
         rows = slice(index * block, (index + 1) * block)
-        before = dot(x_all_ref[0, rows, :], up_ref[...], NT)
-        return before, dot(scaled_ref[0, rows, :], down_ref[...], NT)
+        before = dot(x_all_ref[rows, :], up_ref[...], NT)
+        return before, dot(scaled_ref[rows, :], down_ref[...], NT)
 
     ahead = first_products(0)
     for index in range(blocks):
@@ -265,8 +265,8 @@
         active, slope = gelu_pair(before)
         active = active.astype(BF16)
         before_grad = (active_grad * slope).astype(BF16)
-        active_ref[0, rows, :] = active
-        before_ref[0, rows, :] = before_grad
+        active_ref[rows, :] = active
+        before_ref[rows, :] = before_grad
         out_sum[rows, :] += dot(active, down_ref[...])
         back_sum[rows, :] += dot(before_grad, up_ref[...])
 
@@ -279,7 +279,7 @@
             gate = jnp.sum(probs * mine, -1, keepdims=True)
             gate_grad = jnp.sum(made * g_ref[source].astype(F32), -1, keepdims=True)
             logit = (gate_grad * gate * (mine - probs)).astype(BF16)
-            logit_ref[0, rows, :] = logit
+            logit_ref[rows, :] = logit
             out_ref[source] = (gate * made).astype(BF16)
             back_ref[source] = (
                 back_sum[rows, :] + dot(logit, router_ref[...], NT)
@@ -294,13 +294,10 @@
     block = 256
     last = weights.shape[1] // LANES - 1
     chunk_rows = (sources, count, width)
-    wide = pl.BlockSpec((1, rows, part), lambda f: (chunk, 0, f))
+    wide = pl.BlockSpec((rows, part), lambda f: (0, f))
     weight = pl.BlockSpec((part, width), lambda f: (f, 0))
     slots = pl.BlockSpec(chunk_rows, lambda f: (0, chunk, 0), pipeline_mode=pl.Buffered(1))
-    one = lambda cols: pl.BlockSpec(
-        (1, rows, cols), lambda f: (chunk, 0, 0), pipeline_mode=pl.Buffered(1)
-    )
-    made = lambda cols: jax.ShapeDtypeStruct((CHUNKS, rows, cols), BF16)
+    made = lambda cols: jax.ShapeDtypeStruct((rows, cols), BF16)
     return pl.pallas_call(
         functools.partial(expert_kernel, experts, block, len(kept)),
         grid=(hidden // part,),
@@ -313,11 +310,16 @@
             pl.BlockSpec((width, LANES), lambda f: (0, last), pipeline_mode=pl.Buffered(1)),
         ]
         + [pl.BlockSpec(memory_space=pl.ANY)] * len(kept),
-        out_specs=[wide, wide, one(width), one(width), one(LANES), slots, whole(chunk_rows)],
-        out_shape=[made(hidden), made(hidden), made(width), made(width), made(LANES)]
-        + [jax.ShapeDtypeStruct(g.shape, BF16), jax.ShapeDtypeStruct(chunk_rows, BF16)],
+        out_specs=[
+            slots, wide, wide, whole((rows, width)), whole((rows, LANES)), whole(chunk_rows)
+        ],
+        out_shape=[
+            jax.ShapeDtypeStruct(g.shape, BF16), made(hidden), made(hidden), made(width), made(LANES),
+            jax.ShapeDtypeStruct(chunk_rows, BF16),
+        ],
         scratch_shapes=[
-            pltpu.VMEM((rows, width), F32), pltpu.VMEM((rows, width), F32), pltpu.VMEM((rows, LANES), F32)
+            pltpu.VMEM((rows, width), F32), pltpu.VMEM((rows, width), F32),
+            pltpu.VMEM((rows, LANES), F32), pltpu.VMEM((rows, width), BF16),
         ],
         cost_estimate=cost(4 * rows * width * hidden, 8 * rows * hidden, rows * hidden),
         input_output_aliases={6 + index: index for index in range(len(kept))},
@@ -517,6 +519,18 @@
     count = -(-capacity // (16 * CHUNKS)) * 16
     padded = -(-length // 16) * 16
 
+    routes, slots, keep = (array.transpose(0, 2, 1) for array in (routes, slots, keep))
+    fill = ((0, 0), (0, 0), (0, padded - length))
+    flat_codes = lambda codes: (
+        jnp.pad(codes, fill, constant_values=-1).transpose(1, 0, 2).reshape(2, images * padded)
+    )
+    all_codes = jnp.where(keep > 0, routes * (CHUNKS * count) + slots, -1)
+    g_sent = send(cotangent, flat_codes(all_codes), experts, CHUNKS * count, width)
+    g_sent, tokens_in, qkv_weight, routes, slots, keep, all_codes = lax.optimization_barrier(
+        (g_sent, tokens, qkv_weight, routes, slots, keep, all_codes)
+    )
+    g_here = exchange(g_sent)
+
     columns = experts + 4
     spare = -columns % LANES
     small = jnp.concatenate(
@@ -535,23 +549,10 @@
         place = slots - chunk * count
         here = (keep > 0) & (place >= 0) & (place < count)
         chunk_codes.append(jnp.where(here, routes * count + place, -1))
-    codes = jnp.pad(
-        jnp.concatenate(chunk_codes, -1),
-        ((0, 0), (0, padded - length), (0, 0)),
-        constant_values=-1,
-    )
-    flat_codes = codes.reshape(images * padded, 2 * CHUNKS).T
-    row_codes = [flat_codes[2 * chunk : 2 * chunk + 2] for chunk in range(CHUNKS)]
-
-    all_codes = jnp.pad(
-        jnp.where(keep > 0, routes * (CHUNKS * count) + slots, -1),
-        ((0, 0), (0, padded - length), (0, 0)),
-        constant_values=-1,
-    )
-    g_codes = all_codes.reshape(images * padded, 2).T
-    g_sent = send(cotangent, g_codes, experts, CHUNKS * count, width)
-    g_sent, tokens_in = lax.optimization_barrier((g_sent, tokens))
-    g_here = exchange(g_sent)
+    row_codes = [flat_codes(codes) for codes in chunk_codes]
+    column_codes = lambda codes: jnp.pad(codes, fill, constant_values=-1).transpose(0, 2, 1)
+    codes = column_codes(jnp.concatenate(chunk_codes, 1))
+    all_codes = column_codes(all_codes)
 
     up = lax.all_gather(up_weight.reshape(-1, width), "shard", axis=0, tiled=True)
     down = lax.all_gather(down_weight.reshape(-1, width), "shard", axis=0, tiled=True)
@@ -562,32 +563,34 @@
         lax.broadcasted_iota(jnp.int32, (8, LANES), 1) == lax.axis_index("expert")
     ).astype(F32)
 
-    back_here, kept = [], []
+    back_here, wide, kept = [], [], []
     for chunk in range(CHUNKS):
         x = exchange(send(flat_second, row_codes[chunk], experts, count, width))
-        *kept, back = run_expert(chunk, kept, mine, x, g_here, up, down, weights, experts)
+        out_here, *made, back = run_expert(
+            chunk, kept, mine, x, g_here, up, down, weights, experts
+        )
+        kept = [out_here]
+        wide.append((*made, x.reshape(experts * count, width)))
         back_here.append(back)
-    *kept, out_here = kept
-    active, before_grad, scaled, x_all, logit = [
-        array.reshape(CHUNKS * experts * count, -1) for array in kept
-    ]
+    wide, back_here[-1] = lax.optimization_barrier((wide, back_here[-1]))
 
     returned = [exchange(array).reshape(experts * count, width) for array in back_here]
     out_here, returned = lax.optimization_barrier((out_here, returned))
     out_returned = exchange(out_here).reshape(experts * CHUNKS * count, width)
 
-    down_full = dot(active, scaled, TN).astype(BF16)
-    up_full = dot(before_grad, x_all, TN).astype(BF16)
-    router_full = dot(x_all, logit, TN)
-    down_full, up_full, router_full, returned = lax.optimization_barrier(
-        (down_full, up_full, router_full, returned)
-    )
+    down_full = sum(dot(active, scaled, TN) for active, _, scaled, _, _ in wide).astype(BF16)
+    up_full = sum(dot(before, x, TN) for _, before, _, _, x in wide).astype(BF16)
+    router_full = sum(dot(x, logit, TN) for _, _, _, logit, x in wide)
     down_grad = lax.psum_scatter(down_full, "shard", scatter_dimension=0, tiled=True)
     up_grad = lax.psum_scatter(up_full, "shard", scatter_dimension=0, tiled=True)
+    _, _, router_full, returned = lax.optimization_barrier(
+        (down_full, up_full, router_full, returned)
+    )
 
     tokens_grad, branch, rows_grad, sums = attend_back(
         codes, returned, cotangent, tokens, attended, qkv, weights, vectors
     )
+    rows_grad, down_grad, up_grad = lax.optimization_barrier((rows_grad, down_grad, up_grad))
     flat = lambda array: array.reshape(images * padded, -1)
     qkv_full = dot(flat(first), flat(rows_grad), TN)
     out_full = dot(flat(mixed), flat(branch), TN)

time: 656 us -> 689 us (1.050)
  waiting for transfers between devices: 212 us -> 296 us
  blocking collectives: 91.4 us -> 33.5 us
    all_to_all x5 -> x6, waiting for transfers between devices: 123 us -> 215 us  [exchange(): lax.all_to_all(array, 'expert', split_axis=0, concat_axis=0, tiled=True)]
    all_to_all x2 -> x1, blocking collectives: 91.4 us -> 33.5 us  [exchange(): lax.all_to_all(array, 'expert', split_axis=0, concat_axis=0, tiled=True)]
    ppermute x1, waiting for transfers between devices: 52.1 us -> 27.5 us  [sum_shards(): total = total + lax.ppermute(part, 'shard', moves).astype(F32)]
    all_gather x1, waiting for transfers between devices: 12.2 us -> 27.2 us  [shards(): weights = lax.all_gather(packed, 'shard', axis=0, tiled=True)]
    all_to_all x5 -> x6, starting transfers between devices: 24.1 us -> 28 us  [exchange(): lax.all_to_all(array, 'expert', split_axis=0, concat_axis=0, tiled=True)]
    dot_general x5 -> x8, matrix products: 58.5 us -> 61.6 us  [dot(): return lax.dot_general(a, b, dims, preferred_element_type=F32)]
    unnamed x54 -> x71, local copies, waits for them, and re-layouts: 25.5 us -> 23.4 us
  transfers between devices with their start and end apart: 13 -> 14, of which waited for: 8 -> 10; matrix products, arithmetic and copies ran while one was open for 14% -> 10% of each run, Pallas kernels for 22% -> 20%
where the time goes in v4:
time: 689 us; the launch traced here: 680 us
  waiting for transfers between devices  296 us (43%)
  Pallas kernels  189 us (27%)
  matrix products  61.6 us (9%)
  local copies, waits for them, and re-layouts  38.9 us (6%)
  blocking collectives  33.5 us (5%)
  starting transfers between devices  30.5 us (4%)
  other arithmetic  15.6 us (2%)
  between operations  14.9 us (2%)
    all_to_all x6, waiting for transfers between devices, exchange(): lax.all_to_all(array, 'expert', split_axis=0, concat_axis=0, tiled=True)  215 us
    pallas_call x2, Pallas kernels, run_expert(): pl.pallas_call(functools.partial(expert_kernel, experts, block, len(kept)...  88.8 us
    dot_general x8, matrix products, dot(): return lax.dot_general(a, b, dims, preferred_element_type=F32)  61.6 us
    pallas_call x1, Pallas kernels, attend_back(): call(attend_back_kernel, (images // group,), [image(padded, codes.shape[2...  44.2 us
    all_to_all x1, blocking collectives, exchange(): lax.all_to_all(array, 'expert', split_axis=0, concat_axis=0, tiled=True)  33.5 us
    all_to_all x6, starting transfers between devices, exchange(): lax.all_to_all(array, 'expert', split_axis=0, concat_axis=0, tiled=True)  28 us
    ppermute x1, waiting for transfers between devices, sum_shards(): total = total + lax.ppermute(part, 'shard', moves).astype(F32)  27.5 us
    all_gather x1, waiting for transfers between devices, shards(): weights = lax.all_gather(packed, 'shard', axis=0, tiled=True)  27.2 us
  transfers between devices with their start and end apart: 14, of which 10 were waited for; matrix products, arithmetic and copies ran while one was open for 10% of the time, Pallas kernels for 20%

profile of v4, /device:TPU:0, one launch (start us, length us, event | category | flops | bytes accessed | tf_op | source)
XLA Modules:
  0.0 680.0 jit_solution(157424138913625517)
XLA Ops:
  7.2 1.0 copy.99
  8.2 1.0 copy.98
  9.2 1.0 copy.97
  10.3 1.0 pad.32
  11.3 1.9 copy.100.codes_ref
  13.3 11.1 %shard_map.221 = bf16[8,384,768]{2,1,0:T(8,128)(2,1)} custom-call(s32[2,1248]{1,0:T(2,128)} %copy.100.codes_ref, bf16[6,197,768]{2,1,0:T(8,128)(2,1)} %refs_3_.1), custom_call_target="tpu_custom_call" | custom-call | flops 5888802816 | bytes 6635520 | tf_op jit(solution)/shard_map/pallas_call | solution.py:128
  24.6 2.3 fusion.2
  27.7 7.3 %all-to-all-start.1 = ((bf16[8,384,768]{2,1,0:T(8,128)(2,1)}), bf16[8,384,768]{2,1,0:T(8,128)(2,1)}, u32[]{:S(2)}, u32[]{:S(2)}) async-start(bf16[8,384,768]{2,1,0:T(8,128)(2,1)} %shard_map.221), calls=%async_computation.1 | async-start | bytes 9437184 | tf_op jit(solution)/shard_map/all_to_all | solution.py:495
  35.7 1.8 add_select_fusion.1
  37.5 0.8 copy-done.17
  38.3 0.9 pad.38
  39.2 2.0 copy.103.codes_ref
  41.2 27.2 %all-gather.7.cloned.1.call-done.qkv_weight_ref.out_weight_ref.router_ref.refs_7_.refs_8_ = bf16[768,3200]{1,0:T(8,128)(2,1)} async-done(((bf16[192,3200]{1,0:T(8,128)(2,1)}), bf16[768,3200]{1,0:T(8,128)(2,1)}) %all-gather.7.cloned.1.call-update) | async-done | bytes 4915216 | tf_op jit(solution)/shard_map/all_gather | solution.py:542
  68.3 1.0 slice.42
  69.5 19.7 %shard_map.222 = (bf16[6,208,2304]{2,1,0:T(8,128)(2,1)}, bf16[6,208,768]{2,1,0:T(8,128)(2,1)S(1)}, f32[6,208,768]{2,1,0:T(8,128)}, bf16[6,208,768]{2,1,0:T(8,128)(2,1)S(1)}, bf16[6,208,768]{2,1,0:T(8,128)(2,1)S(1)}) custom-call(bf16[6,197,768]{2,1,0:T(8,128)(2,1)S(1)} %copy-done.1, ...), custom_call_target="tpu_custom_call" | custom-call | flops 7483686912 | bytes 21970944 | tf_op jit(solution)/shard_map/pallas_call | solution.py:191
  89.2 1.3 copy-done.2
  90.5 1.3 copy-done.3
  91.8 1.2 copy-done.6
  93.0 7.3 %shard_map.223 = bf16[8,192,768]{2,1,0:T(8,128)(2,1)} custom-call(s32[2,1248]{1,0:T(2,128)} %copy.103.codes_ref, bf16[1248,768]{1,0:T(8,128)(2,1)} %bitcast.72), custom_call_target="tpu_custom_call" | custom-call | flops 2944401408 | bytes 4276224 | tf_op jit(solution)/shard_map/pallas_call | solution.py:128
  100.4 39.1 %all-to-all-done.1.g_ref = bf16[8,384,768]{2,1,0:T(8,128)(2,1)} async-done(((bf16[8,384,768]{2,1,0:T(8,128)(2,1)}), bf16[8,384,768]{2,1,0:T(8,128)(2,1)}, u32[]{:S(2)}, u32[]{:S(2)}) %all-to-all-start.1) | async-done | bytes 4718624 | tf_op jit(solution)/shard_map/all_to_all | solution.py:495
  139.4 3.6 all-to-all-start
  143.1 1.3 add_select_fusion
  146.1 7.3 %shard_map.225 = bf16[8,192,768]{2,1,0:T(8,128)(2,1)} custom-call(s32[2,1248]{1,0:T(2,128)} %copy.104.codes_ref, bf16[1248,768]{1,0:T(8,128)(2,1)} %bitcast.73), custom_call_target="tpu_custom_call" | custom-call | flops 2944401408 | bytes 4276224 | tf_op jit(solution)/shard_map/pallas_call | solution.py:128
  153.5 43.7 %all-to-all-done.x_ref = bf16[8,192,768]{2,1,0:T(8,128)(2,1)S(1)} async-done(((bf16[8,192,768]{2,1,0:T(8,128)(2,1)}), bf16[8,192,768]{2,1,0:T(8,128)(2,1)S(1)}, u32[]{:S(2)}, u32[]{:S(2)}) %all-to-all-start) | async-done | bytes 2359328 | tf_op jit(solution)/shard_map/all_to_all | solution.py:495
  197.1 1.4 copy-done.11
  198.5 3.6 all-to-all-start.2
  203.1 44.2 %shard_map.224 = (bf16[8,384,768]{2,1,0:T(8,128)(2,1)}, bf16[1536,3072]{1,0:T(8,128)(2,1)}, bf16[1536,3072]{1,0:T(8,128)(2,1)}, bf16[1536,768]{1,0:T(8,128)(2,1)...) custom-call(f32[8,128]{1,0:T(8,128)} %iota.7.mine_ref, bf16[8,192,768]{2,1,0:T(8,128)(2,1)} %copy-done.11, ...), custom_call_target="tpu_custom_call" | custom-call | flops 28991029248 | bytes 37748736 | tf_op jit(solution)/shard_map/pallas_call | solution.py:301
  247.3 8.9 %all-to-all-done.2.x_ref = bf16[8,192,768]{2,1,0:T(8,128)(2,1)S(1)} async-done(((bf16[8,192,768]{2,1,0:T(8,128)(2,1)}), bf16[8,192,768]{2,1,0:T(8,128)(2,1)S(1)}, u32[]{:S(2)}, u32[]{:S(2)}) %all-to-all-start.2) | async-done | bytes 2359328 | tf_op jit(solution)/shard_map/all_to_all | solution.py:495
  256.2 1.4 copy-done.9
  257.6 44.6 %shard_map.226 = (bf16[8,384,768]{2,1,0:T(8,128)(2,1)}, bf16[1536,3072]{1,0:T(8,128)(2,1)}, bf16[1536,3072]{1,0:T(8,128)(2,1)}, bf16[1536,768]{1,0:T(8,128)(2,1)...) custom-call(f32[8,128]{1,0:T(8,128)} %iota.7.mine_ref, ...), custom_call_target="tpu_custom_call", output_to_operand_aliasing={{0}: (6, {})} | custom-call | flops 28991029248 | bytes 37748736 | tf_op jit(solution)/shard_map/pallas_call | solution.py:301
  302.2 11.5 %fusion.8 = f32[3072,768]{1,0:T(8,128)S(1)} fusion(bf16[1536,3072]{1,0:T(8,128)(2,1)} %get-tuple-element.80, bf16[1536,768]{1,0:T(8,128)(2,1)} %get-tuple-element.81), kind=kOutput, calls=%fused_computation.37 | convolution fusion | flops 7247757312 | bytes 21233664 | tf_op jit(solution)/shard_map/dot_general | solution.py:23
  313.7 9.8 %add_convert_fusion.1 = bf16[3072,768]{1,0:T(8,128)(2,1)} fusion(f32[3072,768]{1,0:T(8,128)S(1)} %fusion.8, bf16[1536,3072]{1,0:T(8,128)(2,1)S(1)} %copy-done.30, bf16[1536,768]{1,0:T(8,128)(2,1)S(1)} %copy-done.31), kind=kOutput, calls=%fused_computation.1 | convolution fusion | flops 7252475904 | bytes 25952256 | tf_op jit(solution)/shard_map/dot_general | solution.py:23
  323.6 4.4 all-to-all-start.3
  328.0 12.5 %fusion.9 = f32[3072,768]{1,0:T(8,128)S(1)} fusion(bf16[1536,3072]{1,0:T(8,128)(2,1)} %get-tuple-element.84, bf16[1536,768]{1,0:T(8,128)(2,1)} %bitcast.76), kind=kOutput, calls=%fused_computation.38 | convolution fusion | flops 7247757312 | bytes 21233664 | tf_op jit(solution)/shard_map/dot_general | solution.py:23
  340.6 14.8 %add_convert_fusion = bf16[3072,768]{1,0:T(8,128)(2,1)} fusion(f32[3072,768]{1,0:T(8,128)S(1)} %fusion.9, bf16[1536,3072]{1,0:T(8,128)(2,1)} %get-tuple-element.86, bf16[1536,768]{1,0:T(8,128)(2,1)S(1)} %bitcast.74), kind=kOutput, calls=%fused_computation | convolution fusion | flops 7252475904 | bytes 25952256 | tf_op jit(solution)/shard_map/dot_general | solution.py:23
  355.4 25.9 %all-to-all-done.3 = bf16[8,192,768]{2,1,0:T(8,128)(2,1)} async-done(((bf16[8,192,768]{2,1,0:T(8,128)(2,1)}), bf16[8,192,768]{2,1,0:T(8,128)(2,1)}, u32[]{:S(2)}, u32[]{:S(2)}) %all-to-all-start.3) | async-done | bytes 2359328 | tf_op jit(solution)/shard_map/all_to_all | solution.py:495
  381.4 4.4 all-to-all-start.4
  385.8 1.4 pad_add_fusion
  387.3 0.9 pad_bitcast_fusion.refs_0_
  389.8 49.3 %all-to-all-done.4 = bf16[8,192,768]{2,1,0:T(8,128)(2,1)} async-done(((bf16[8,192,768]{2,1,0:T(8,128)(2,1)}), bf16[8,192,768]{2,1,0:T(8,128)(2,1)}, u32[]{:S(2)}, u32[]{:S(2)}) %all-to-all-start.4) | async-done | bytes 2359328 | tf_op jit(solution)/shard_map/all_to_all | solution.py:495
  439.1 44.2 %shard_map.227 = (bf16[6,197,768]{2,1,0:T(8,128)(2,1)}, bf16[6,208,768]{2,1,0:T(8,128)(2,1)}, bf16[6,208,2304]{2,1,0:T(8,128)(2,1)}, f32[8,768]{1,0:T(8,128)}) custom-call(s32[6,208,4]{2,1,0:T(8,128)} %pad_bitcast_fusion.refs_0_, bf16[1536,768]{1,0:T(8,128)(2,1)} %bitcast.17.refs_1_, bf16[1536,768]{1,0:T(8,128)(2,1)} %bitcast.18.refs_2_, ...), custom_call_target="tpu_custom_call" | custom-call | flops 15764815872 | bytes 32440320 | tf_op jit(solution)/shard_map/pallas_call | solution.py:408
  484.3 4.7 all-to-all-start.5
  489.7 3.3 bitcast_convert_fusion.1
  493.0 8.0 %bitcast_convert_fusion = bf16[768,2304]{1,0:T(8,128)(2,1)S(1)} fusion(bf16[6,208,768]{2,1,0:T(8,128)(2,1)} %copy-done.6, bf16[6,208,2304]{2,1,0:T(8,128)(2,1)} %get-tuple-element.100), kind=kOutput, calls=%fused_computation.2 | convolution fusion | flops 4418371584 | bytes 11206656 | tf_op jit(solution)/shard_map/dot_general | solution.py:23
  501.4 1.9 dynamic-slice_bitcast_fusion
  503.3 1.1 copy-done.7
  504.4 4.9 collective-permute-done
  509.3 2.2 convert_add_fusion
  511.5 2.2 copy-done.8
  513.8 1.6 collective-permute-start.1
  515.4 27.5 %collective-permute-done.1 = bf16[192,3200]{1,0:T(8,128)(2,1)S(1)} collective-permute-done((bf16[192,3200]{1,0:T(8,128)(2,1)S(1)}, bf16[192,3200]{1,0:T(8,128)(2,1)S(1)}, u32[]{:S(2)}, u32[]{:S(2)}) %collective-permute-start.1) | collective-permute-done | bytes 1228832 | tf_op jit(solution)/shard_map/ppermute | solution.py:482
  543.0 2.0 fusion
  544.9 47.8 %all-to-all-done.5 = bf16[8,384,768]{2,1,0:T(8,128)(2,1)} async-done(((bf16[8,384,768]{2,1,0:T(8,128)(2,1)}), bf16[8,384,768]{2,1,0:T(8,128)(2,1)}, u32[]{:S(2)}, u32[]{:S(2)}) %all-to-all-start.5) | async-done | bytes 4718624 | tf_op jit(solution)/shard_map/all_to_all | solution.py:495
  592.7 33.5 %all_to_all.35 = bf16[8,24,3200]{2,1,0:T(8,128)(2,1)S(1)} all-to-all(bf16[8,24,3200]{2,1,0:T(8,128)(2,1)S(1)} %bitcast.83), channel_id=1, replica_groups=mesh['expert'=8,'shard'=4] {'expert'}, dimensions={0} | all-to-all | bytes 2457600 | tf_op jit(solution)/shard_map/all_to_all | solution.py:495
  626.3 0.9 reduce_sum.12
  627.6 1.6 bitcast_convert_fusion.2
  629.2 3.8 copy.107
  633.0 3.8 copy.108
  636.8 10.8 %shard_map.228 = bf16[6,197,768]{2,1,0:T(8,128)(2,1)} custom-call(s32[6,208,2]{2,1,0:T(8,128)S(1)} %pad_bitcast_fusion.1.codes_ref, bf16[3072,768]{1,0:T(8,128)(2,1)} %bitcast.29.refs_0_, f32[6,208,768]{2,1,0:T(8,128)S(1)} %copy-done.5), custom_call_target="tpu_custom_call" | custom-call | flops 5888802816 | bytes 7667712 | tf_op jit(solution)/shard_map/pallas_call | solution.py:450
  647.7 20.0 %all-gather.9.cloned.1.call-done = bf16[192,3200]{1,0:T(8,128)(2,1)} async-done(((bf16[24,3200]{1,0:T(8,128)(2,1)}), bf16[192,3200]{1,0:T(8,128)(2,1)}) %all-gather.9.cloned.1.call-update) | async-done | bytes 1228816 | tf_op jit(solution)/shard_map/all_gather | solution.py:491
  667.6 1.5 convert_element_type.56
  669.2 0.9 slice_reduce_fusion
  670.8 1.3 slice.47
  672.1 0.9 slice.48
  (96 shorter events, 9.6 us)
Async XLA Ops:
  7.2 61.2 %all-gather.7.cloned.1.call-start = ((), (), s32[]{:S(2)}) async-start(), calls=%async_computation.9 | async-start | bytes 6144000 | tf_op jit(solution)/shard_map/all_gather | solution.py:542
  9.2 4.1 copy-start.14
  10.2 14.2 %copy-start.20 = (s32[6,197,2]{2,1,0:T(8,128)}, s32[6,197,2]{2,1,0:T(8,128)S(1)}, u32[]{:S(2)}) copy-start(s32[6,197,2]{2,1,0:T(8,128)S(1)} %copy.97) | copy-start | bytes 28372
  10.3 14.1 %copy-start.18 = (s32[6,2,197]{1,2,0:T(8,128)}, s32[6,2,197]{1,2,0:T(8,128)S(1)}, u32[]{:S(2)}) copy-start(s32[6,2,197]{1,2,0:T(8,128)S(1)} %add_select_fusion.2) | copy-start | bytes 28372
  13.2 11.1 %copy-start.26 = (bf16[192]{0:T(256)(128)(2,1)S(1)}, bf16[192]{0:T(256)(128)(2,1)}, u32[]{:S(2)}) copy-start(bf16[192]{0:T(256)(128)(2,1)} %param.15) | copy-start | bytes 1156
  13.2 11.1 %copy-start.27 = (bf16[192]{0:T(256)(128)(2,1)S(1)}, bf16[192]{0:T(256)(128)(2,1)}, u32[]{:S(2)}) copy-start(bf16[192]{0:T(256)(128)(2,1)} %param.16) | copy-start | bytes 1156
  13.2 11.2 %copy-start.28 = (bf16[192]{0:T(256)(128)(2,1)S(1)}, bf16[192]{0:T(256)(128)(2,1)}, u32[]{:S(2)}) copy-start(bf16[192]{0:T(256)(128)(2,1)} %param.19) | copy-start | bytes 1156
  13.2 11.2 %copy-start.29 = (bf16[192]{0:T(256)(128)(2,1)S(1)}, bf16[192]{0:T(256)(128)(2,1)}, u32[]{:S(2)}) copy-start(bf16[192]{0:T(256)(128)(2,1)} %param.20) | copy-start | bytes 1156
  13.3 11.2 %copy-start.25 = (bf16[192,8]{0,1:T(8,128)(2,1)S(1)}, bf16[192,8]{0,1:T(8,128)(2,1)}, u32[]{:S(2)}) copy-start(bf16[192,8]{0,1:T(8,128)(2,1)} %param.21) | copy-start | bytes 9220
  13.3 11.3 %copy-start.24 = (bf16[192,768]{1,0:T(8,128)(2,1)S(1)}, bf16[192,768]{1,0:T(8,128)(2,1)}, u32[]{:S(2)}) copy-start(bf16[192,768]{1,0:T(8,128)(2,1)} %param.18) | copy-start | bytes 884740
  26.9 175.6 %all-gather.11.cloned.1.call-start = ((), (), s32[]{:S(2)}) async-start(), calls=%async_computation.13 | async-start | bytes 5898240 | tf_op jit(solution)/shard_map/all_gather | solution.py:557
  27.7 111.8 %all-to-all-start.1 = ((bf16[8,384,768]{2,1,0:T(8,128)(2,1)}), bf16[8,384,768]{2,1,0:T(8,128)(2,1)}, u32[]{:S(2)}, u32[]{:S(2)}) async-start(bf16[8,384,768]{2,1,0:T(8,128)(2,1)} %shard_map.221), calls=%async_computation.1 | async-start | bytes 9437184 | tf_op jit(solution)/shard_map/all_to_all | solution.py:495
  34.9 167.6 %all-gather.13.cloned.1.call-start = ((), (), s32[]{:S(2)}) async-start(), calls=%async_computation.14 | async-start | bytes 5898240 | tf_op jit(solution)/shard_map/all_gather | solution.py:558
  35.7 33.9 %copy-start.1 = (bf16[6,197,768]{2,1,0:T(8,128)(2,1)S(1)}, bf16[6,197,768]{2,1,0:T(8,128)(2,1)}, u32[]{:S(2)}) copy-start(bf16[6,197,768]{2,1,0:T(8,128)(2,1)} %refs_4_.1) | copy-start | bytes 5446660
  37.5 0.9 copy-start.17
  69.5 19.7 %copy-start = (f32[8,768]{1,0:T(8,128)}, f32[8,768]{1,0:T(8,128)S(1)}, u32[]{:S(2)}) copy-start(f32[8,768]{1,0:T(8,128)S(1)} %pad_convert_fusion.vector_ref.refs_9_) | copy-start | bytes 73732
  89.2 1.3 copy-start.2
  90.5 1.3 copy-start.3
  91.8 1.2 copy-start.6
  139.4 57.7 %all-to-all-start = ((bf16[8,192,768]{2,1,0:T(8,128)(2,1)}), bf16[8,192,768]{2,1,0:T(8,128)(2,1)S(1)}, u32[]{:S(2)}, u32[]{:S(2)}) async-start(bf16[8,192,768]{2,1,0:T(8,128)(2,1)} %shard_map.223), calls=%async_computation | async-start | bytes 4718592 | tf_op jit(solution)/shard_map/all_to_all | solution.py:495
  144.4 0.8 copy-start.15
  197.1 1.4 copy-start.11
  198.5 57.7 %all-to-all-start.2 = ((bf16[8,192,768]{2,1,0:T(8,128)(2,1)}), bf16[8,192,768]{2,1,0:T(8,128)(2,1)S(1)}, u32[]{:S(2)}, u32[]{:S(2)}) async-start(bf16[8,192,768]{2,1,0:T(8,128)(2,1)} %shard_map.225), calls=%async_computation.2 | async-start | bytes 4718592 | tf_op jit(solution)/shard_map/all_to_all | solution.py:495
  202.2 290.8 %reduce-scatter.3.cloned.1.call-start = ((), (), s32[]{:S(2)}) async-start(), calls=%async_computation.10 | async-start | bytes 5898240 | tf_op jit(solution)/shard_map/reduce_scatter | solution.py:584
  256.2 1.4 copy-start.9
  302.2 11.5 %copy-start.30 = (bf16[1536,3072]{1,0:T(8,128)(2,1)S(1)}, bf16[1536,3072]{1,0:T(8,128)(2,1)}, u32[]{:S(2)}) copy-start(bf16[1536,3072]{1,0:T(8,128)(2,1)} %get-tuple-element.82) | copy-start | bytes 28311556
  302.2 11.5 %copy-start.31 = (bf16[1536,768]{1,0:T(8,128)(2,1)S(1)}, bf16[1536,768]{1,0:T(8,128)(2,1)}, u32[]{:S(2)}) copy-start(bf16[1536,768]{1,0:T(8,128)(2,1)} %get-tuple-element.83) | copy-start | bytes 7077892
  323.6 57.8 %all-to-all-start.3 = ((bf16[8,192,768]{2,1,0:T(8,128)(2,1)}), bf16[8,192,768]{2,1,0:T(8,128)(2,1)}, u32[]{:S(2)}, u32[]{:S(2)}) async-start(bf16[8,192,768]{2,1,0:T(8,128)(2,1)} %get-tuple-element.91), calls=%async_computation.3 | async-start | bytes 4718592 | tf_op jit(solution)/shard_map/all_to_all | solution.py:495
  327.9 12.6 %copy-start.10 = (bf16[8,192,768]{2,1,0:T(8,128)(2,1)S(1)}, bf16[8,192,768]{2,1,0:T(8,128)(2,1)}, u32[]{:S(2)}) copy-start(bf16[8,192,768]{2,1,0:T(8,128)(2,1)} %copy-done.9) | copy-start | bytes 7077892
  328.0 165.0 %reduce-scatter.5.cloned.1.call-start = ((), (), s32[]{:S(2)}) async-start(), calls=%async_computation.11 | async-start | bytes 5898240 | tf_op jit(solution)/shard_map/reduce_scatter | solution.py:585
  355.4 30.4 %copy-start.16 = (s32[6,2,197]{1,2,0:T(8,128)S(1)}, s32[6,2,197]{1,2,0:T(8,128)}, u32[]{:S(2)}) copy-start(s32[6,2,197]{1,2,0:T(8,128)} %copy-done.15) | copy-start | bytes 28372
  381.4 57.8 %all-to-all-start.4 = ((bf16[8,192,768]{2,1,0:T(8,128)(2,1)}), bf16[8,192,768]{2,1,0:T(8,128)(2,1)}, u32[]{:S(2)}, u32[]{:S(2)}) async-start(bf16[8,192,768]{2,1,0:T(8,128)(2,1)} %get-tuple-element.92), calls=%async_computation.4 | async-start | bytes 4718592 | tf_op jit(solution)/shard_map/all_to_all | solution.py:495
  385.8 2.4 copy-start.23
  385.8 2.4 copy-start.12
  387.3 1.7 copy-start.22
  484.2 5.4 copy-start.4
  484.3 108.5 %all-to-all-start.5 = ((bf16[8,384,768]{2,1,0:T(8,128)(2,1)}), bf16[8,384,768]{2,1,0:T(8,128)(2,1)}, u32[]{:S(2)}, u32[]{:S(2)}) async-start(bf16[8,384,768]{2,1,0:T(8,128)(2,1)} %get-tuple-element.105), calls=%async_computation.7 | async-start | bytes 9437184 | tf_op jit(solution)/shard_map/all_to_all | solution.py:495
  489.0 178.6 %all-gather.9.cloned.1.call-start = ((), (), s32[]{:S(2)}) async-start(), calls=%async_computation.12 | async-start | bytes 1382400 | tf_op jit(solution)/shard_map/all_gather | solution.py:491
  501.4 3.0 copy-start.7
  504.4 4.9 collective-permute-start
  511.5 2.2 copy-start.8
  513.8 29.1 %collective-permute-start.1 = (bf16[192,3200]{1,0:T(8,128)(2,1)S(1)}, bf16[192,3200]{1,0:T(8,128)(2,1)S(1)}, u32[]{:S(2)}, u32[]{:S(2)}) collective-permute-start(bf16[192,3200]{1,0:T(8,128)(2,1)S(1)} %fusion.3), channel_id=1, source_target_pairs={{0,2},{1,3},{2,0},{3,1},{4,6},{5,7},{6,4},{7,5},{8,10},{9,11},{10,... | collective-permute-start | bytes 3686408 | tf_op jit(solution)/shard_map/ppermute | solution.py:482
  544.9 82.2 %copy-start.19 = (s32[6,2,197]{1,2,0:T(8,128)S(1)}, s32[6,2,197]{1,2,0:T(8,128)}, u32[]{:S(2)}) copy-start(s32[6,2,197]{1,2,0:T(8,128)} %copy-done.18) | copy-start | bytes 28372
  626.3 1.3 copy-start.21
  633.0 3.8 copy-start.5
  667.6 2.5 copy-start.13
Sparse Core Ops, SparseCore 0:
  27.0 41.2 all-gather.6
  69.9 37.4 all-gather.10
  109.0 37.4 all-gather.12
  323.7 46.9 reduce-scatter.2
  373.2 47.8 reduce-scatter.4
  627.3 40.3 all-gather.8

commit v5 on v4

--- a/solution.py
+++ b/solution.py
@@ -488,7 +488,8 @@
     rows, cols = array.shape
     parts = exchange(array.reshape(experts, rows // experts, cols))
     share = jnp.sum(parts.astype(F32), 0).astype(BF16)
-    return lax.all_gather(share, "expert", axis=0, tiled=True).astype(F32)
+    shares = exchange(jnp.broadcast_to(share[None], parts.shape))
+    return shares.reshape(rows, cols).astype(F32)
 
 
 def exchange(array):
@@ -572,25 +573,26 @@
         kept = [out_here]
         wide.append((*made, x.reshape(experts * count, width)))
         back_here.append(back)
-    wide, back_here[-1] = lax.optimization_barrier((wide, back_here[-1]))
-
-    returned = [exchange(array).reshape(experts * count, width) for array in back_here]
+    returned = []
+    for chunk in range(CHUNKS):
+        back = back_here[chunk]
+        if chunk:
+            back, wide, returned = lax.optimization_barrier((back, wide, returned))
+        returned.append(exchange(back).reshape(experts * count, width))
     out_here, returned = lax.optimization_barrier((out_here, returned))
     out_returned = exchange(out_here).reshape(experts * CHUNKS * count, width)
 
     down_full = sum(dot(active, scaled, TN) for active, _, scaled, _, _ in wide).astype(BF16)
     up_full = sum(dot(before, x, TN) for _, before, _, _, x in wide).astype(BF16)
     router_full = sum(dot(x, logit, TN) for _, _, _, logit, x in wide)
+    down_full, up_full, router_full, returned = lax.optimization_barrier(
+        (down_full, up_full, router_full, returned)
+    )
     down_grad = lax.psum_scatter(down_full, "shard", scatter_dimension=0, tiled=True)
-    up_grad = lax.psum_scatter(up_full, "shard", scatter_dimension=0, tiled=True)
-    _, _, router_full, returned = lax.optimization_barrier(
-        (down_full, up_full, router_full, returned)
-    )
 
     tokens_grad, branch, rows_grad, sums = attend_back(
         codes, returned, cotangent, tokens, attended, qkv, weights, vectors
     )
-    rows_grad, down_grad, up_grad = lax.optimization_barrier((rows_grad, down_grad, up_grad))
     flat = lambda array: array.reshape(images * padded, -1)
     qkv_full = dot(flat(first), flat(rows_grad), TN)
     out_full = dot(flat(mixed), flat(branch), TN)
@@ -599,6 +601,8 @@
         [qkv_full, out_full, jnp.pad(small_full, ((0, 0), (0, spare)))], 1
     ).astype(BF16)
     layer = sum_shards(layer)
+    layer, up_full = lax.optimization_barrier((layer, up_full))
+    up_grad = lax.psum_scatter(up_full, "shard", scatter_dimension=0, tiled=True)
     layer, out_returned = lax.optimization_barrier((layer, out_returned))
     layer = sum_experts(layer)
     block_out = combine(all_codes, [out_returned], attended, length)

time: 689 us -> 647 us (0.939)
  waiting for transfers between devices: 296 us -> 250 us
    all_to_all x6 -> x7, waiting for transfers between devices: 215 us -> 193 us  [exchange(): lax.all_to_all(array, 'expert', split_axis=0, concat_axis=0, tiled=True)]
    all_gather x1 -> x0, waiting for transfers between devices: 20 us -> none  [sum_experts(): return lax.all_gather(share, 'expert', axis=0, tiled=True).astype(F32)]
    all_to_all x6 -> x7, starting transfers between devices: 28 us -> 33.2 us  [exchange(): lax.all_to_all(array, 'expert', split_axis=0, concat_axis=0, tiled=True)]
    unnamed x71 -> x79, local copies, waits for them, and re-layouts: 23.4 us -> 24.9 us
  transfers between devices with their start and end apart: 14 -> 14, of which waited for: 10 -> 10; matrix products, arithmetic and copies ran while one was open for 10% -> 12% of each run, Pallas kernels for 20% -> 28%
where the time goes in v5:
time: 647 us; the launch traced here: 638 us
  waiting for transfers between devices  250 us (39%)
  Pallas kernels  190 us (29%)
  matrix products  58.7 us (9%)
  local copies, waits for them, and re-layouts  41.2 us (6%)
  starting transfers between devices  34.9 us (5%)
  blocking collectives  33.4 us (5%)
  between operations  14.7 us (2%)
  other arithmetic  14.5 us (2%)
    all_to_all x7, waiting for transfers between devices, exchange(): lax.all_to_all(array, 'expert', split_axis=0, concat_axis=0, tiled=True)  193 us
    pallas_call x2, Pallas kernels, run_expert(): pl.pallas_call(functools.partial(expert_kernel, experts, block, len(kept)...  88.4 us
    dot_general x8, matrix products, dot(): return lax.dot_general(a, b, dims, preferred_element_type=F32)  58.7 us
    pallas_call x1, Pallas kernels, attend_back(): call(attend_back_kernel, (images // group,), [image(padded, codes.shape[2...  45.4 us
    all_to_all x1, blocking collectives, exchange(): lax.all_to_all(array, 'expert', split_axis=0, concat_axis=0, tiled=True)  33.4 us
    all_to_all x7, starting transfers between devices, exchange(): lax.all_to_all(array, 'expert', split_axis=0, concat_axis=0, tiled=True)  33.2 us
    ppermute x1, waiting for transfers between devices, sum_shards(): total = total + lax.ppermute(part, 'shard', moves).astype(F32)  27.8 us
    all_gather x1, waiting for transfers between devices, shards(): weights = lax.all_gather(packed, 'shard', axis=0, tiled=True)  27.4 us
  transfers between devices with their start and end apart: 14, of which 10 were waited for; matrix products, arithmetic and copies ran while one was open for 12% of the time, Pallas kernels for 28%

profile of v5, /device:TPU:0, one launch (start us, length us, event | category | flops | bytes accessed | tf_op | source)
XLA Modules:
  0.0 637.8 jit_solution(1943650774877350140)
XLA Ops:
  7.2 1.0 copy.135
  8.2 1.0 copy.134
  9.2 1.0 copy.133
  10.3 0.9 copy-done.18
  12.1 11.1 %shard_map.221 = bf16[8,384,768]{2,1,0:T(8,128)(2,1)} custom-call(s32[2,1248]{1,0:T(2,128)} %copy.136.codes_ref, bf16[6,197,768]{2,1,0:T(8,128)(2,1)} %refs_3_.1), custom_call_target="tpu_custom_call" | custom-call | flops 5888802816 | bytes 6635520 | tf_op jit(solution)/shard_map/pallas_call | solution.py:128
  23.5 1.1 fusion.2
  25.4 7.3 %all-to-all-start.1 = ((bf16[8,384,768]{2,1,0:T(8,128)(2,1)}), bf16[8,384,768]{2,1,0:T(8,128)(2,1)}, u32[]{:S(2)}, u32[]{:S(2)}) async-start(bf16[8,384,768]{2,1,0:T(8,128)(2,1)} %shard_map.221), calls=%async_computation.1 | async-start | bytes 9437184 | tf_op jit(solution)/shard_map/all_to_all | solution.py:496
  33.4 1.6 add_select_fusion.1
  35.8 0.9 pad.39
  36.7 2.0 copy.140.codes_ref
  38.6 27.4 %all-gather.6.cloned.1.call-done.qkv_weight_ref.out_weight_ref.router_ref.refs_7_.refs_8_ = bf16[768,3200]{1,0:T(8,128)(2,1)} async-done(((bf16[192,3200]{1,0:T(8,128)(2,1)}), bf16[768,3200]{1,0:T(8,128)(2,1)}) %all-gather.6.cloned.1.call-update) | async-done | bytes 4915216 | tf_op jit(solution)/shard_map/all_gather | solution.py:543
  66.0 1.0 slice.42
  67.2 19.6 %shard_map.222 = (bf16[6,208,2304]{2,1,0:T(8,128)(2,1)}, bf16[6,208,768]{2,1,0:T(8,128)(2,1)S(1)}, f32[6,208,768]{2,1,0:T(8,128)}, bf16[6,208,768]{2,1,0:T(8,128)(2,1)S(1)}, bf16[6,208,768]{2,1,0:T(8,128)(2,1)S(1)}) custom-call(bf16[6,197,768]{2,1,0:T(8,128)(2,1)S(1)} %copy-done.1, ...), custom_call_target="tpu_custom_call" | custom-call | flops 7483686912 | bytes 21970944 | tf_op jit(solution)/shard_map/pallas_call | solution.py:191
  86.9 1.3 copy-done.2
  88.1 1.3 copy-done.3
  89.4 1.2 copy-done.6
  90.7 7.4 %shard_map.224 = bf16[8,192,768]{2,1,0:T(8,128)(2,1)} custom-call(s32[2,1248]{1,0:T(2,128)} %copy.140.codes_ref, bf16[1248,768]{1,0:T(8,128)(2,1)} %bitcast.75), custom_call_target="tpu_custom_call" | custom-call | flops 2944401408 | bytes 4276224 | tf_op jit(solution)/shard_map/pallas_call | solution.py:128
  98.0 39.1 %all-to-all-done.1.g_ref = bf16[8,384,768]{2,1,0:T(8,128)(2,1)} async-done(((bf16[8,384,768]{2,1,0:T(8,128)(2,1)}), bf16[8,384,768]{2,1,0:T(8,128)(2,1)}, u32[]{:S(2)}, u32[]{:S(2)}) %all-to-all-start.1) | async-done | bytes 4718624 | tf_op jit(solution)/shard_map/all_to_all | solution.py:496
  137.1 3.6 all-to-all-start.2
  140.8 1.3 add_select_fusion
  142.9 0.9 pad.38
  143.8 1.9 copy.139.codes_ref
  145.7 7.3 %shard_map.223 = bf16[8,192,768]{2,1,0:T(8,128)(2,1)} custom-call(s32[2,1248]{1,0:T(2,128)} %copy.139.codes_ref, bf16[1248,768]{1,0:T(8,128)(2,1)} %bitcast.76), custom_call_target="tpu_custom_call" | custom-call | flops 2944401408 | bytes 4276224 | tf_op jit(solution)/shard_map/pallas_call | solution.py:128
  153.1 41.8 %all-to-all-done.2.x_ref = bf16[8,192,768]{2,1,0:T(8,128)(2,1)S(1)} async-done(((bf16[8,192,768]{2,1,0:T(8,128)(2,1)}), bf16[8,192,768]{2,1,0:T(8,128)(2,1)S(1)}, u32[]{:S(2)}, u32[]{:S(2)}) %all-to-all-start.2) | async-done | bytes 2359328 | tf_op jit(solution)/shard_map/all_to_all | solution.py:496
  194.8 1.4 copy-done.12
  196.2 3.9 all-to-all-start
  200.8 44.1 %shard_map.225 = (bf16[8,384,768]{2,1,0:T(8,128)(2,1)}, bf16[1536,3072]{1,0:T(8,128)(2,1)}, bf16[1536,3072]{1,0:T(8,128)(2,1)}, bf16[1536,768]{1,0:T(8,128)(2,1)...) custom-call(f32[8,128]{1,0:T(8,128)} %iota.7.mine_ref, bf16[8,192,768]{2,1,0:T(8,128)(2,1)} %copy-done.12, ...), custom_call_target="tpu_custom_call" | custom-call | flops 28991029248 | bytes 37748736 | tf_op jit(solution)/shard_map/pallas_call | solution.py:301
  244.9 9.2 %all-to-all-done.x_ref = bf16[8,192,768]{2,1,0:T(8,128)(2,1)S(1)} async-done(((bf16[8,192,768]{2,1,0:T(8,128)(2,1)}), bf16[8,192,768]{2,1,0:T(8,128)(2,1)S(1)}, u32[]{:S(2)}, u32[]{:S(2)}) %all-to-all-start) | async-done | bytes 2359328 | tf_op jit(solution)/shard_map/all_to_all | solution.py:496
  254.1 4.8 all-to-all-start.3
  259.0 1.3 pad_add_fusion
  260.3 0.9 pad_bitcast_fusion.refs_0_
  261.2 44.3 %shard_map.226 = (bf16[8,384,768]{2,1,0:T(8,128)(2,1)}, bf16[1536,3072]{1,0:T(8,128)(2,1)}, bf16[1536,3072]{1,0:T(8,128)(2,1)}, bf16[1536,768]{1,0:T(8,128)(2,1)...) custom-call(f32[8,128]{1,0:T(8,128)} %iota.7.mine_ref, ...), custom_call_target="tpu_custom_call", output_to_operand_aliasing={{0}: (6, {})} | custom-call | flops 28991029248 | bytes 37748736 | tf_op jit(solution)/shard_map/pallas_call | solution.py:301
  305.5 6.9 %all-to-all-done.3 = bf16[8,192,768]{2,1,0:T(8,128)(2,1)} async-done(((bf16[8,192,768]{2,1,0:T(8,128)(2,1)}), bf16[8,192,768]{2,1,0:T(8,128)(2,1)}, u32[]{:S(2)}, u32[]{:S(2)}) %all-to-all-start.3) | async-done | bytes 2359328 | tf_op jit(solution)/shard_map/all_to_all | solution.py:496
  312.4 12.5 %fusion.9 = f32[3072,768]{1,0:T(8,128)} fusion(bf16[1536,3072]{1,0:T(8,128)(2,1)} %get-tuple-element.87, bf16[1536,768]{1,0:T(8,128)(2,1)S(1)} %bitcast.79), kind=kOutput, calls=%fused_computation.39 | convolution fusion | flops 7247757312 | bytes 21233664 | tf_op jit(solution)/shard_map/dot_general | solution.py:23
  325.7 4.5 all-to-all-start.4
  330.3 14.6 %add_convert_fusion = bf16[3072,768]{1,0:T(8,128)(2,1)} fusion(f32[3072,768]{1,0:T(8,128)} %fusion.9, bf16[1536,3072]{1,0:T(8,128)(2,1)} %get-tuple-element.89, bf16[1536,768]{1,0:T(8,128)(2,1)S(1)} %bitcast.77), kind=kOutput, calls=%fused_computation | convolution fusion | flops 7252475904 | bytes 25952256 | tf_op jit(solution)/shard_map/dot_general | solution.py:23
  345.8 11.6 %fusion.8 = f32[3072,768]{1,0:T(8,128)S(1)} fusion(bf16[1536,3072]{1,0:T(8,128)(2,1)} %get-tuple-element.83, bf16[1536,768]{1,0:T(8,128)(2,1)} %get-tuple-element.84), kind=kOutput, calls=%fused_computation.38 | convolution fusion | flops 7247757312 | bytes 21233664 | tf_op jit(solution)/shard_map/dot_general | solution.py:23
  357.4 9.8 %add_convert_fusion.1 = bf16[3072,768]{1,0:T(8,128)(2,1)} fusion(f32[3072,768]{1,0:T(8,128)S(1)} %fusion.8, bf16[1536,3072]{1,0:T(8,128)(2,1)S(1)} %bitcast.102, bf16[1536,768]{1,0:T(8,128)(2,1)S(1)} %copy-done.30), kind=kOutput, calls=%fused_computation.1 | convolution fusion | flops 7252475904 | bytes 25952256 | tf_op jit(solution)/shard_map/dot_general | solution.py:23
  367.2 16.5 %all-to-all-done.4 = bf16[8,192,768]{2,1,0:T(8,128)(2,1)} async-done(((bf16[8,192,768]{2,1,0:T(8,128)(2,1)}), bf16[8,192,768]{2,1,0:T(8,128)(2,1)}, u32[]{:S(2)}, u32[]{:S(2)}) %all-to-all-start.4) | async-done | bytes 2359328 | tf_op jit(solution)/shard_map/all_to_all | solution.py:496
  383.7 45.4 %shard_map.227 = (bf16[6,197,768]{2,1,0:T(8,128)(2,1)}, bf16[6,208,768]{2,1,0:T(8,128)(2,1)}, bf16[6,208,2304]{2,1,0:T(8,128)(2,1)}, f32[8,768]{1,0:T(8,128)}) custom-call(s32[6,208,4]{2,1,0:T(8,128)} %pad_bitcast_fusion.refs_0_, bf16[1536,768]{1,0:T(8,128)(2,1)} %bitcast.17.refs_1_, bf16[1536,768]{1,0:T(8,128)(2,1)} %bitcast.18.refs_2_, ...), custom_call_target="tpu_custom_call" | custom-call | flops 15764815872 | bytes 32440320 | tf_op jit(solution)/shard_map/pallas_call | solution.py:408
  430.2 3.5 bitcast_convert_fusion.1
  433.9 5.1 bitcast_convert_fusion
  439.5 1.8 dynamic-slice_bitcast_fusion
  441.3 1.2 copy-done.8
  442.5 4.6 all-to-all-start.5
  447.3 2.2 convert_add_fusion
  449.5 2.2 copy-done.9
  451.9 1.5 collective-permute-start.1
  453.4 27.8 %collective-permute-done.1 = bf16[192,3200]{1,0:T(8,128)(2,1)S(1)} collective-permute-done((bf16[192,3200]{1,0:T(8,128)(2,1)S(1)}, bf16[192,3200]{1,0:T(8,128)(2,1)S(1)}, u32[]{:S(2)}, u32[]{:S(2)}) %collective-permute-start.1) | collective-permute-done | bytes 1228832 | tf_op jit(solution)/shard_map/ppermute | solution.py:482
  481.2 1.9 fusion
  483.1 69.3 %all-to-all-done.5 = bf16[8,384,768]{2,1,0:T(8,128)(2,1)} async-done(((bf16[8,384,768]{2,1,0:T(8,128)(2,1)}), bf16[8,384,768]{2,1,0:T(8,128)(2,1)}, u32[]{:S(2)}, u32[]{:S(2)}) %all-to-all-start.5) | async-done | bytes 4718624 | tf_op jit(solution)/shard_map/all_to_all | solution.py:496
  552.4 33.4 %all_to_all.40 = bf16[8,24,3200]{2,1,0:T(8,128)(2,1)S(1)} all-to-all(bf16[8,24,3200]{2,1,0:T(8,128)(2,1)S(1)} %bitcast.86), channel_id=1, replica_groups=mesh['expert'=8,'shard'=4] {'expert'}, dimensions={0} | all-to-all | bytes 2457600 | tf_op jit(solution)/shard_map/all_to_all | solution.py:496
  586.0 1.1 broadcast_in_dim.25
  587.1 4.4 all-to-all-start.7
  591.6 2.1 copy-done.5
  593.7 10.8 %shard_map.228 = bf16[6,197,768]{2,1,0:T(8,128)(2,1)} custom-call(s32[6,208,2]{2,1,0:T(8,128)S(1)} %pad_bitcast_fusion.1.codes_ref, bf16[3072,768]{1,0:T(8,128)(2,1)} %bitcast.29.refs_0_, f32[6,208,768]{2,1,0:T(8,128)S(1)} %copy-done.5), custom_call_target="tpu_custom_call" | custom-call | flops 5888802816 | bytes 7667712 | tf_op jit(solution)/shard_map/pallas_call | solution.py:450
  604.5 1.4 bitcast_convert_fusion.3
  606.0 3.8 copy.144
  609.8 10.7 %all-to-all-done.7 = bf16[8,24,3200]{2,1,0:T(8,128)(2,1)} async-done(((bf16[8,24,3200]{2,1,0:T(8,128)(2,1)}), bf16[8,24,3200]{2,1,0:T(8,128)(2,1)}, u32[]{:S(2)}, u32[]{:S(2)}) %all-to-all-start.7) | async-done | bytes 1228832 | tf_op jit(solution)/shard_map/all_to_all | solution.py:496
  620.5 1.4 bitcast_convert_fusion.2
  622.0 1.3 slice.47
  624.8 0.9 slice_reduce_fusion
  625.8 1.4 bitcast_convert_fusion.4
  627.2 3.8 copy.143
  (107 shorter events, 10.8 us)
Async XLA Ops:
  7.2 58.9 %all-gather.6.cloned.1.call-start = ((), (), s32[]{:S(2)}) async-start(), calls=%async_computation.10 | async-start | bytes 6144000 | tf_op jit(solution)/shard_map/all_gather | solution.py:543
  9.2 24.2 %copy-start.14 = (s32[6,197,2]{2,1,0:T(8,128)}, s32[6,197,2]{2,1,0:T(8,128)S(1)}, u32[]{:S(2)}) copy-start(s32[6,197,2]{2,1,0:T(8,128)S(1)} %copy.134) | copy-start | bytes 28372
  10.2 13.1 %copy-start.20 = (s32[6,197,2]{2,1,0:T(8,128)}, s32[6,197,2]{2,1,0:T(8,128)S(1)}, u32[]{:S(2)}) copy-start(s32[6,197,2]{2,1,0:T(8,128)S(1)} %copy.133) | copy-start | bytes 28372
  10.3 0.9 copy-start.18
  12.1 11.2 %copy-start.26 = (bf16[192]{0:T(256)(128)(2,1)S(1)}, bf16[192]{0:T(256)(128)(2,1)}, u32[]{:S(2)}) copy-start(bf16[192]{0:T(256)(128)(2,1)} %param.15) | copy-start | bytes 1156
  12.1 11.2 %copy-start.27 = (bf16[192]{0:T(256)(128)(2,1)S(1)}, bf16[192]{0:T(256)(128)(2,1)}, u32[]{:S(2)}) copy-start(bf16[192]{0:T(256)(128)(2,1)} %param.16) | copy-start | bytes 1156
  12.1 11.2 %copy-start.28 = (bf16[192]{0:T(256)(128)(2,1)S(1)}, bf16[192]{0:T(256)(128)(2,1)}, u32[]{:S(2)}) copy-start(bf16[192]{0:T(256)(128)(2,1)} %param.19) | copy-start | bytes 1156
  12.1 11.2 %copy-start.29 = (bf16[192]{0:T(256)(128)(2,1)S(1)}, bf16[192]{0:T(256)(128)(2,1)}, u32[]{:S(2)}) copy-start(bf16[192]{0:T(256)(128)(2,1)} %param.20) | copy-start | bytes 1156
  12.1 11.2 %copy-start.25 = (bf16[192,8]{0,1:T(8,128)(2,1)S(1)}, bf16[192,8]{0,1:T(8,128)(2,1)}, u32[]{:S(2)}) copy-start(bf16[192,8]{0,1:T(8,128)(2,1)} %param.21) | copy-start | bytes 9220
  12.1 11.4 %copy-start.21 = (bf16[192,2304]{1,0:T(8,128)(2,1)S(1)}, bf16[192,2304]{1,0:T(8,128)(2,1)}, u32[]{:S(2)}) copy-start(bf16[192,2304]{1,0:T(8,128)(2,1)} %param.17) | copy-start | bytes 2654212
  12.1 11.4 %copy-start.24 = (bf16[192,768]{1,0:T(8,128)(2,1)S(1)}, bf16[192,768]{1,0:T(8,128)(2,1)}, u32[]{:S(2)}) copy-start(bf16[192,768]{1,0:T(8,128)(2,1)} %param.18) | copy-start | bytes 884740
  24.6 175.5 %all-gather.8.cloned.1.call-start = ((), (), s32[]{:S(2)}) async-start(), calls=%async_computation.13 | async-start | bytes 5898240 | tf_op jit(solution)/shard_map/all_gather | solution.py:558
  25.4 111.8 %all-to-all-start.1 = ((bf16[8,384,768]{2,1,0:T(8,128)(2,1)}), bf16[8,384,768]{2,1,0:T(8,128)(2,1)}, u32[]{:S(2)}, u32[]{:S(2)}) async-start(bf16[8,384,768]{2,1,0:T(8,128)(2,1)} %shard_map.221), calls=%async_computation.1 | async-start | bytes 9437184 | tf_op jit(solution)/shard_map/all_to_all | solution.py:496
  32.6 167.6 %all-gather.10.cloned.1.call-start = ((), (), s32[]{:S(2)}) async-start(), calls=%async_computation.14 | async-start | bytes 5898240 | tf_op jit(solution)/shard_map/all_gather | solution.py:559
  33.4 33.9 %copy-start.1 = (bf16[6,197,768]{2,1,0:T(8,128)(2,1)S(1)}, bf16[6,197,768]{2,1,0:T(8,128)(2,1)}, u32[]{:S(2)}) copy-start(bf16[6,197,768]{2,1,0:T(8,128)(2,1)} %refs_4_.1) | copy-start | bytes 5446660
  34.9 0.8 copy-start.17
  67.2 19.6 %copy-start = (f32[8,768]{1,0:T(8,128)}, f32[8,768]{1,0:T(8,128)S(1)}, u32[]{:S(2)}) copy-start(f32[8,768]{1,0:T(8,128)S(1)} %pad_convert_fusion.vector_ref.refs_9_) | copy-start | bytes 73732
  86.9 1.3 copy-start.2
  88.1 1.3 copy-start.3
  89.4 1.2 copy-start.6
  137.1 57.7 %all-to-all-start.2 = ((bf16[8,192,768]{2,1,0:T(8,128)(2,1)}), bf16[8,192,768]{2,1,0:T(8,128)(2,1)S(1)}, u32[]{:S(2)}, u32[]{:S(2)}) async-start(bf16[8,192,768]{2,1,0:T(8,128)(2,1)} %shard_map.224), calls=%async_computation.2 | async-start | bytes 4718592 | tf_op jit(solution)/shard_map/all_to_all | solution.py:496
  142.1 0.8 copy-start.15
  194.8 1.4 copy-start.12
  196.2 57.9 %all-to-all-start = ((bf16[8,192,768]{2,1,0:T(8,128)(2,1)}), bf16[8,192,768]{2,1,0:T(8,128)(2,1)S(1)}, u32[]{:S(2)}, u32[]{:S(2)}) async-start(bf16[8,192,768]{2,1,0:T(8,128)(2,1)} %shard_map.223), calls=%async_computation | async-start | bytes 4718592 | tf_op jit(solution)/shard_map/all_to_all | solution.py:496
  244.9 14.1 %copy-start.16 = (s32[6,2,197]{1,2,0:T(8,128)S(1)}, s32[6,2,197]{1,2,0:T(8,128)}, u32[]{:S(2)}) copy-start(s32[6,2,197]{1,2,0:T(8,128)} %copy-done.15) | copy-start | bytes 28372
  254.1 6.2 copy-start.10
  254.1 58.3 %all-to-all-start.3 = ((bf16[8,192,768]{2,1,0:T(8,128)(2,1)}), bf16[8,192,768]{2,1,0:T(8,128)(2,1)}, u32[]{:S(2)}, u32[]{:S(2)}) async-start(bf16[8,192,768]{2,1,0:T(8,128)(2,1)} %get-tuple-element.82), calls=%async_computation.3 | async-start | bytes 4718592 | tf_op jit(solution)/shard_map/all_to_all | solution.py:496
  261.2 51.2 %copy-start.13 = (bf16[8,192,768]{2,1,0:T(8,128)(2,1)S(1)}, bf16[8,192,768]{2,1,0:T(8,128)(2,1)}, u32[]{:S(2)}) copy-start(bf16[8,192,768]{2,1,0:T(8,128)(2,1)} %copy-done.12) | copy-start | bytes 7077892
  312.4 12.5 %copy-start.23 = (bf16[1536,128]{1,0:T(8,128)(2,1)S(1)}, bf16[1536,128]{1,0:T(8,128)(2,1)}, u32[]{:S(2)}) copy-start(bf16[1536,128]{1,0:T(8,128)(2,1)} %get-tuple-element.91) | copy-start | bytes 1179652
  325.7 4.6 copy-start.11
  325.7 57.9 %all-to-all-start.4 = ((bf16[8,192,768]{2,1,0:T(8,128)(2,1)}), bf16[8,192,768]{2,1,0:T(8,128)(2,1)}, u32[]{:S(2)}, u32[]{:S(2)}) async-start(bf16[8,192,768]{2,1,0:T(8,128)(2,1)} %get-tuple-element.95), calls=%async_computation.4 | async-start | bytes 4718592 | tf_op jit(solution)/shard_map/all_to_all | solution.py:496
  330.2 14.7 %copy-start.22 = (bf16[1536,128]{1,0:T(8,128)(2,1)S(1)}, bf16[1536,128]{1,0:T(8,128)(2,1)}, u32[]{:S(2)}) copy-start(bf16[1536,128]{1,0:T(8,128)(2,1)} %get-tuple-element.92) | copy-start | bytes 1179652
  330.3 274.3 %reduce-scatter.5.cloned.1.call-start = ((), (), s32[]{:S(2)}) async-start(), calls=%async_computation.12 | async-start | bytes 5898240 | tf_op jit(solution)/shard_map/reduce_scatter | solution.py:591
  344.9 12.4 %slice-start.2 = ((s8[9437184]{0:T(1024)(128)(4,1)}), s8[4194304]{0:T(1024)(128)(4,1)S(1)}, s32[]{:S(2)}) async-start(s8[9437184]{0:T(1024)(128)(4,1)} %bitcast.101), calls=%async_computation.17 | async-start | bytes 8388608
  345.8 11.6 %slice-start.3 = ((s8[9437184]{0:T(1024)(128)(4,1)}), s8[4194304]{0:T(1024)(128)(4,1)S(1)}, s32[]{:S(2)}) async-start(s8[9437184]{0:T(1024)(128)(4,1)} %bitcast.101), calls=%async_computation.18 | async-start | bytes 8388608
  345.8 11.6 %slice-start.4 = ((s8[9437184]{0:T(1024)(128)(4,1)}), s8[1048576]{0:T(1024)(128)(4,1)S(1)}, s32[]{:S(2)}) async-start(s8[9437184]{0:T(1024)(128)(4,1)} %bitcast.101), calls=%async_computation.19 | async-start | bytes 2097152
  345.8 11.6 %copy-start.30 = (bf16[1536,768]{1,0:T(8,128)(2,1)S(1)}, bf16[1536,768]{1,0:T(8,128)(2,1)}, u32[]{:S(2)}) copy-start(bf16[1536,768]{1,0:T(8,128)(2,1)} %get-tuple-element.86) | copy-start | bytes 7077892
  383.7 46.5 %copy-start.4 = (bf16[6,208,768]{2,1,0:T(8,128)(2,1)S(1)}, bf16[6,208,768]{2,1,0:T(8,128)(2,1)}, u32[]{:S(2)}) copy-start(bf16[6,208,768]{2,1,0:T(8,128)(2,1)} %copy-done.3) | copy-start | bytes 5750788
  430.0 3.6 slice-start
  430.2 3.5 copy-start.7
  430.2 3.7 slice-start.1
  439.5 3.0 copy-start.8
  442.5 4.9 collective-permute-start
  442.5 110.0 %all-to-all-start.5 = ((bf16[8,384,768]{2,1,0:T(8,128)(2,1)}), bf16[8,384,768]{2,1,0:T(8,128)(2,1)}, u32[]{:S(2)}, u32[]{:S(2)}) async-start(bf16[8,384,768]{2,1,0:T(8,128)(2,1)} %get-tuple-element.109), calls=%async_computation.5 | async-start | bytes 9437184 | tf_op jit(solution)/shard_map/all_to_all | solution.py:496
  447.1 178.7 %reduce-scatter.3.cloned.1.call-start = ((), (), s32[]{:S(2)}) async-start(), calls=%async_computation.11 | async-start | bytes 5898240 | tf_op jit(solution)/shard_map/reduce_scatter | solution.py:605
  449.5 2.2 copy-start.9
  451.9 29.3 %collective-permute-start.1 = (bf16[192,3200]{1,0:T(8,128)(2,1)S(1)}, bf16[192,3200]{1,0:T(8,128)(2,1)S(1)}, u32[]{:S(2)}, u32[]{:S(2)}) collective-permute-start(bf16[192,3200]{1,0:T(8,128)(2,1)S(1)} %fusion.3), channel_id=1, source_target_pairs={{0,2},{1,3},{2,0},{3,1},{4,6},{5,7},{6,4},{7,5},{8,10},{9,11},{10,... | collective-permute-start | bytes 3686408 | tf_op jit(solution)/shard_map/ppermute | solution.py:482
  585.8 5.7 copy-start.19
  587.1 33.4 %all-to-all-start.7 = ((bf16[8,24,3200]{2,1,0:T(8,128)(2,1)}), bf16[8,24,3200]{2,1,0:T(8,128)(2,1)}, u32[]{:S(2)}, u32[]{:S(2)}) async-start(bf16[8,24,3200]{2,1,0:T(8,128)(2,1)} %broadcast_in_dim.25), calls=%async_computation.7 | async-start | bytes 2457600 | tf_op jit(solution)/shard_map/all_to_all | solution.py:496
  591.6 2.1 copy-start.5
Sparse Core Ops, SparseCore 0:
  24.7 41.2 all-gather.5
  67.6 37.4 all-gather.7
  106.7 37.4 all-gather.9
  383.8 46.9 reduce-scatter.4
  483.2 48.7 reduce-scatter.2

commit v6 on v5

--- a/solution.py
+++ b/solution.py
@@ -223,11 +223,11 @@
     return active, slope
 
 
-def expert_kernel(experts, block, kept, mine_ref, x_ref, g_ref, up_ref, down_ref, router_ref, *refs):
-    (
-        out_ref, active_ref, before_ref, scaled_ref, logit_ref, back_ref,
-        out_sum, back_sum, probs_ref, x_all_ref,
-    ) = refs[kept:]
+def expert_kernel(
+    experts, block, mine_ref, x_ref, g_ref, up_ref, down_ref, router_ref,
+    out_ref, active_ref, before_ref, scaled_ref, logit_ref, back_ref,
+    out_sum, back_sum, probs_ref, x_all_ref,
+):
     step = pl.program_id(0)
     sources, count, width = x_ref.shape
     total = sources * count
@@ -286,7 +286,7 @@
             ).astype(BF16)
 
 
-def run_expert(chunk, kept, mine, x, g, up, down, weights, experts):
+def run_expert(chunk, mine, x, g, up, down, weights, experts):
     sources, count, width = x.shape
     rows = sources * count
     hidden = up.shape[0]
@@ -299,7 +299,7 @@
     slots = pl.BlockSpec(chunk_rows, lambda f: (0, chunk, 0), pipeline_mode=pl.Buffered(1))
     made = lambda cols: jax.ShapeDtypeStruct((rows, cols), BF16)
     return pl.pallas_call(
-        functools.partial(expert_kernel, experts, block, len(kept)),
+        functools.partial(expert_kernel, experts, block),
         grid=(hidden // part,),
         in_specs=[
             whole(mine.shape),
@@ -308,13 +308,12 @@
             weight,
             weight,
             pl.BlockSpec((width, LANES), lambda f: (0, last), pipeline_mode=pl.Buffered(1)),
-        ]
-        + [pl.BlockSpec(memory_space=pl.ANY)] * len(kept),
+        ],
         out_specs=[
-            slots, wide, wide, whole((rows, width)), whole((rows, LANES)), whole(chunk_rows)
+            whole(chunk_rows), wide, wide, whole((rows, width)), whole((rows, LANES)), whole(chunk_rows)
         ],
         out_shape=[
-            jax.ShapeDtypeStruct(g.shape, BF16), made(hidden), made(hidden), made(width), made(LANES),
+            jax.ShapeDtypeStruct(chunk_rows, BF16), made(hidden), made(hidden), made(width), made(LANES),
             jax.ShapeDtypeStruct(chunk_rows, BF16),
         ],
         scratch_shapes=[
@@ -322,11 +321,10 @@
             pltpu.VMEM((rows, LANES), F32), pltpu.VMEM((rows, width), BF16),
         ],
         cost_estimate=cost(4 * rows * width * hidden, 8 * rows * hidden, rows * hidden),
-        input_output_aliases={6 + index: index for index in range(len(kept))},
         compiler_params=pltpu.CompilerParams(
             vmem_limit_bytes=56 * MIB, dimension_semantics=("arbitrary",)
         ),
-    )(mine, x, g, up, down, weights, *kept)
+    )(mine, x, g, up, down, weights)
 
 
 def attend_back_kernel(*refs):
@@ -527,8 +525,8 @@
     )
     all_codes = jnp.where(keep > 0, routes * (CHUNKS * count) + slots, -1)
     g_sent = send(cotangent, flat_codes(all_codes), experts, CHUNKS * count, width)
-    g_sent, tokens_in, qkv_weight, routes, slots, keep, all_codes = lax.optimization_barrier(
-        (g_sent, tokens, qkv_weight, routes, slots, keep, all_codes)
+    g_sent, tokens_in, qkv_weight, routes, slots, keep = lax.optimization_barrier(
+        (g_sent, tokens, qkv_weight, routes, slots, keep)
     )
     g_here = exchange(g_sent)
 
@@ -551,9 +549,9 @@
         here = (keep > 0) & (place >= 0) & (place < count)
         chunk_codes.append(jnp.where(here, routes * count + place, -1))
     row_codes = [flat_codes(codes) for codes in chunk_codes]
-    column_codes = lambda codes: jnp.pad(codes, fill, constant_values=-1).transpose(0, 2, 1)
-    codes = column_codes(jnp.concatenate(chunk_codes, 1))
-    all_codes = column_codes(all_codes)
+    codes = jnp.pad(
+        jnp.concatenate(chunk_codes, 1), fill, constant_values=-1
+    ).transpose(0, 2, 1)
 
     up = lax.all_gather(up_weight.reshape(-1, width), "shard", axis=0, tiled=True)
     down = lax.all_gather(down_weight.reshape(-1, width), "shard", axis=0, tiled=True)
@@ -564,26 +562,31 @@
         lax.broadcasted_iota(jnp.int32, (8, LANES), 1) == lax.axis_index("expert")
     ).astype(F32)
 
-    back_here, wide, kept = [], [], []
+    back_here, out_here, wide, up_parts = [], [], [], []
     for chunk in range(CHUNKS):
         x = exchange(send(flat_second, row_codes[chunk], experts, count, width))
-        out_here, *made, back = run_expert(
-            chunk, kept, mine, x, g_here, up, down, weights, experts
-        )
-        kept = [out_here]
+        if chunk:
+            x, up_parts = lax.optimization_barrier((x, up_parts))
+        out, *made, back = run_expert(chunk, mine, x, g_here, up, down, weights, experts)
+        out_here.append(out)
+        back_here.append(back)
         wide.append((*made, x.reshape(experts * count, width)))
-        back_here.append(back)
+        if chunk < CHUNKS - 1:
+            up_parts.append(dot(made[1], wide[chunk][4], TN))
     returned = []
     for chunk in range(CHUNKS):
         back = back_here[chunk]
         if chunk:
             back, wide, returned = lax.optimization_barrier((back, wide, returned))
         returned.append(exchange(back).reshape(experts * count, width))
-    out_here, returned = lax.optimization_barrier((out_here, returned))
-    out_returned = exchange(out_here).reshape(experts * CHUNKS * count, width)
+    out_returned = []
+    for out in out_here:
+        out, returned, out_returned = lax.optimization_barrier((out, returned, out_returned))
+        out_returned.append(exchange(out).reshape(experts * count, width))
 
     down_full = sum(dot(active, scaled, TN) for active, _, scaled, _, _ in wide).astype(BF16)
-    up_full = sum(dot(before, x, TN) for _, before, _, _, x in wide).astype(BF16)
+    _, before, _, _, x = wide[-1]
+    up_full = sum(up_parts, dot(before, x, TN)).astype(BF16)
     router_full = sum(dot(x, logit, TN) for _, _, _, logit, x in wide)
     down_full, up_full, router_full, returned = lax.optimization_barrier(
         (down_full, up_full, router_full, returned)
@@ -600,12 +603,13 @@
     layer = jnp.concatenate(
         [qkv_full, out_full, jnp.pad(small_full, ((0, 0), (0, spare)))], 1
     ).astype(BF16)
+    layer, out_returned[0] = lax.optimization_barrier((layer, out_returned[0]))
     layer = sum_shards(layer)
     layer, up_full = lax.optimization_barrier((layer, up_full))
     up_grad = lax.psum_scatter(up_full, "shard", scatter_dimension=0, tiled=True)
     layer, out_returned = lax.optimization_barrier((layer, out_returned))
     layer = sum_experts(layer)
-    block_out = combine(all_codes, [out_returned], attended, length)
+    block_out = combine(codes, out_returned, attended, length)
     tail = 4 * width + experts
     return (
         block_out,

time: 647 us -> 662 us (1.023)
  waiting for transfers between devices: 250 us -> 264 us
  local copies, waits for them, and re-layouts: 41.2 us -> 34.4 us
    all_to_all x7 -> x8, waiting for transfers between devices: 193 us -> 203 us  [exchange(): lax.all_to_all(array, 'expert', split_axis=0, concat_axis=0, tiled=True)]
    all_to_all x7 -> x8, starting transfers between devices: 33.2 us -> 38.6 us  [exchange(): lax.all_to_all(array, 'expert', split_axis=0, concat_axis=0, tiled=True)]
    unnamed x79 -> x62, local copies, waits for them, and re-layouts: 24.9 us -> 21.3 us
  transfers between devices with their start and end apart: 14 -> 15, of which waited for: 10 -> 10; matrix products, arithmetic and copies ran while one was open for 12% -> 14% of each run, Pallas kernels for 28% -> 27%
where the time goes in v6:
time: 662 us; the launch traced here: 654 us
  waiting for transfers between devices  264 us (40%)
  Pallas kernels  188 us (28%)
  matrix products  63.9 us (10%)
  starting transfers between devices  40.2 us (6%)
  local copies, waits for them, and re-layouts  34.4 us (5%)
  blocking collectives  33.7 us (5%)
  other arithmetic  14.6 us (2%)
  between operations  14.5 us (2%)
    all_to_all x8, waiting for transfers between devices, exchange(): lax.all_to_all(array, 'expert', split_axis=0, concat_axis=0, tiled=True)  203 us
    pallas_call x2, Pallas kernels, run_expert(): pl.pallas_call(functools.partial(expert_kernel, experts, block), grid=(hi...  88.3 us
    dot_general x8, matrix products, dot(): return lax.dot_general(a, b, dims, preferred_element_type=F32)  63.9 us
    pallas_call x1, Pallas kernels, attend_back(): call(attend_back_kernel, (images // group,), [image(padded, codes.shape[2...  45.3 us
    all_to_all x8, starting transfers between devices, exchange(): lax.all_to_all(array, 'expert', split_axis=0, concat_axis=0, tiled=True)  38.6 us
    all_to_all x1, blocking collectives, exchange(): lax.all_to_all(array, 'expert', split_axis=0, concat_axis=0, tiled=True)  33.7 us
    all_gather x1, waiting for transfers between devices, shards(): weights = lax.all_gather(packed, 'shard', axis=0, tiled=True)  31.7 us
    pallas_call x3, Pallas kernels, send(): call(kernel, (experts,), [whole(codes.shape), whole(source.shape)], pl.Bl...  25.8 us
  transfers between devices with their start and end apart: 15, of which 10 were waited for; matrix products, arithmetic and copies ran while one was open for 14% of the time, Pallas kernels for 27%

profile of v6, /device:TPU:0, one launch (start us, length us, event | category | flops | bytes accessed | tf_op | source)
XLA Modules:
  0.0 654.0 jit_solution(17019937965282837819)
XLA Ops:
  7.2 0.8 compare_select_fusion
  8.7 11.1 %shard_map.221 = bf16[8,384,768]{2,1,0:T(8,128)(2,1)} custom-call(s32[2,1248]{1,0:T(2,128)} %reshape.74.codes_ref, bf16[6,197,768]{2,1,0:T(8,128)(2,1)} %refs_3_.1), custom_call_target="tpu_custom_call" | custom-call | flops 5888802816 | bytes 6635520 | tf_op jit(solution)/shard_map/pallas_call | solution.py:128
  20.1 1.1 fusion.2
  21.3 0.7 all-gather.10.cloned.1.call-update
  22.0 7.4 %all-to-all-start.2 = ((bf16[8,384,768]{2,1,0:T(8,128)(2,1)}), bf16[8,384,768]{2,1,0:T(8,128)(2,1)}, u32[]{:S(2)}, u32[]{:S(2)}) async-start(bf16[8,384,768]{2,1,0:T(8,128)(2,1)} %shard_map.221), calls=%async_computation.2 | async-start | bytes 9437184 | tf_op jit(solution)/shard_map/all_to_all | solution.py:494
  31.0 31.7 %all-gather.6.cloned.1.call-done.qkv_weight_ref.out_weight_ref.router_ref.refs_7_.refs_8_ = bf16[768,3200]{1,0:T(8,128)(2,1)} async-done(((bf16[192,3200]{1,0:T(8,128)(2,1)}), bf16[768,3200]{1,0:T(8,128)(2,1)}) %all-gather.6.cloned.1.call-update) | async-done | bytes 4915216 | tf_op jit(solution)/shard_map/all_gather | solution.py:541
  62.7 1.0 slice.42
  63.9 19.6 %shard_map.222 = (bf16[6,208,2304]{2,1,0:T(8,128)(2,1)}, bf16[6,208,768]{2,1,0:T(8,128)(2,1)S(1)}, f32[6,208,768]{2,1,0:T(8,128)}, bf16[6,208,768]{2,1,0:T(8,128)(2,1)S(1)}, bf16[6,208,768]{2,1,0:T(8,128)(2,1)S(1)}) custom-call(bf16[6,197,768]{2,1,0:T(8,128)(2,1)S(1)} %copy-done.2, ...), custom_call_target="tpu_custom_call" | custom-call | flops 7483686912 | bytes 21970944 | tf_op jit(solution)/shard_map/pallas_call | solution.py:191
  83.5 1.3 copy-done.3
  84.8 1.3 copy-done.4
  86.1 1.3 copy-done.6
  87.3 7.3 %shard_map.224 = bf16[8,192,768]{2,1,0:T(8,128)(2,1)} custom-call(s32[2,1248]{1,0:T(2,128)} %reshape.77.codes_ref, bf16[1248,768]{1,0:T(8,128)(2,1)} %bitcast.70), custom_call_target="tpu_custom_call" | custom-call | flops 2944401408 | bytes 4276224 | tf_op jit(solution)/shard_map/pallas_call | solution.py:128
  94.7 39.3 %all-to-all-done.2.g_ref = bf16[8,384,768]{2,1,0:T(8,128)(2,1)} async-done(((bf16[8,384,768]{2,1,0:T(8,128)(2,1)}), bf16[8,384,768]{2,1,0:T(8,128)(2,1)}, u32[]{:S(2)}, u32[]{:S(2)}) %all-to-all-start.2) | async-done | bytes 4718624 | tf_op jit(solution)/shard_map/all_to_all | solution.py:494
  134.0 3.6 all-to-all-start.1
  138.3 7.4 %shard_map.223 = bf16[8,192,768]{2,1,0:T(8,128)(2,1)} custom-call(s32[2,1248]{1,0:T(2,128)} %reshape.75.codes_ref, bf16[1248,768]{1,0:T(8,128)(2,1)} %bitcast.71), custom_call_target="tpu_custom_call" | custom-call | flops 2944401408 | bytes 4276224 | tf_op jit(solution)/shard_map/pallas_call | solution.py:128
  145.6 46.0 %all-to-all-done.1.x_ref = bf16[8,192,768]{2,1,0:T(8,128)(2,1)S(1)} async-done(((bf16[8,192,768]{2,1,0:T(8,128)(2,1)}), bf16[8,192,768]{2,1,0:T(8,128)(2,1)S(1)}, u32[]{:S(2)}, u32[]{:S(2)}) %all-to-all-start.1) | async-done | bytes 2359328 | tf_op jit(solution)/shard_map/all_to_all | solution.py:494
  191.6 1.4 copy-done.12
  193.0 3.8 all-to-all-start
  197.5 44.2 %shard_map.225 = (bf16[8,192,768]{2,1,0:T(8,128)(2,1)}, bf16[1536,3072]{1,0:T(8,128)(2,1)}, bf16[1536,3072]{1,0:T(8,128)(2,1)}, bf16[1536,768]{1,0:T(8,128)(2,1)...) custom-call(f32[8,128]{1,0:T(8,128)} %iota.7.mine_ref, bf16[8,192,768]{2,1,0:T(8,128)(2,1)} %copy-done.12, ...), custom_call_target="tpu_custom_call" | custom-call | flops 28991029248 | bytes 37748736 | tf_op jit(solution)/shard_map/pallas_call | solution.py:301
  241.7 9.1 %all-to-all-done.x_ref = bf16[8,192,768]{2,1,0:T(8,128)(2,1)S(1)} async-done(((bf16[8,192,768]{2,1,0:T(8,128)(2,1)}), bf16[8,192,768]{2,1,0:T(8,128)(2,1)S(1)}, u32[]{:S(2)}, u32[]{:S(2)}) %all-to-all-start) | async-done | bytes 2359328 | tf_op jit(solution)/shard_map/all_to_all | solution.py:494
  250.9 1.5 copy-done.10
  252.4 4.8 all-to-all-start.3
  257.2 13.1 %fusion.8 = f32[3072,768]{1,0:T(8,128)} fusion(bf16[1536,3072]{1,0:T(8,128)(2,1)} %get-tuple-element.78, bf16[1536,768]{1,0:T(8,128)(2,1)} %bitcast.76), kind=kOutput, calls=%fused_computation.40 | convolution fusion | flops 7247757312 | bytes 21233664 | tf_op jit(solution)/shard_map/dot_general | solution.py:23
  270.3 44.1 %shard_map.226 = (bf16[8,192,768]{2,1,0:T(8,128)(2,1)}, bf16[1536,3072]{1,0:T(8,128)(2,1)}, bf16[1536,3072]{1,0:T(8,128)(2,1)}, bf16[1536,768]{1,0:T(8,128)(2,1)...) custom-call(f32[8,128]{1,0:T(8,128)} %iota.7.mine_ref, bf16[8,192,768]{2,1,0:T(8,128)(2,1)} %copy-done.10, ...), custom_call_target="tpu_custom_call" | custom-call | flops 28991029248 | bytes 37748736 | tf_op jit(solution)/shard_map/pallas_call | solution.py:301
  314.5 6.5 all-to-all-start.4
  321.3 0.9 pad_bitcast_fusion.refs_0_.codes_ref
  322.1 0.8 fusion.10
  323.2 0.8 convolution_add_fusion
  324.0 14.6 %add_convert_fusion = bf16[3072,768]{1,0:T(8,128)(2,1)} fusion(f32[3072,768]{1,0:T(8,128)} %fusion.8, bf16[1536,3072]{1,0:T(8,128)(2,1)} %get-tuple-element.93, bf16[1536,768]{1,0:T(8,128)(2,1)S(1)} %bitcast.75), kind=kOutput, calls=%fused_computation | convolution fusion | flops 7252475904 | bytes 25952256 | tf_op jit(solution)/shard_map/dot_general | solution.py:23
  338.6 35.2 %all-to-all-done.4 = bf16[8,192,768]{2,1,0:T(8,128)(2,1)} async-done(((bf16[8,192,768]{2,1,0:T(8,128)(2,1)}), bf16[8,192,768]{2,1,0:T(8,128)(2,1)}, u32[]{:S(2)}, u32[]{:S(2)}) %all-to-all-start.4) | async-done | bytes 2359328 | tf_op jit(solution)/shard_map/all_to_all | solution.py:494
  373.8 3.6 all-to-all-start.5
  377.5 11.3 %fusion.9 = f32[3072,768]{1,0:T(8,128)S(1)} fusion(bf16[1536,3072]{1,0:T(8,128)(2,1)} %get-tuple-element.89, bf16[1536,768]{1,0:T(8,128)(2,1)} %get-tuple-element.90), kind=kOutput, calls=%fused_computation.41 | convolution fusion | flops 7247757312 | bytes 21233664 | tf_op jit(solution)/shard_map/dot_general | solution.py:23
  388.8 14.0 %add_convert_fusion.1 = bf16[3072,768]{1,0:T(8,128)(2,1)} fusion(f32[3072,768]{1,0:T(8,128)S(1)} %fusion.9, bf16[1536,3072]{1,0:T(8,128)(2,1)} %get-tuple-element.91, bf16[1536,768]{1,0:T(8,128)(2,1)S(1)} %copy-done.26), kind=kOutput, calls=%fused_computation.1 | convolution fusion | flops 7252475904 | bytes 25952256 | tf_op jit(solution)/shard_map/dot_general | solution.py:23
  402.9 28.6 %all-to-all-done.5 = bf16[8,192,768]{2,1,0:T(8,128)(2,1)S(1)} async-done(((bf16[8,192,768]{2,1,0:T(8,128)(2,1)}), bf16[8,192,768]{2,1,0:T(8,128)(2,1)S(1)}, u32[]{:S(2)}, u32[]{:S(2)}) %all-to-all-start.5) | async-done | bytes 2359328 | tf_op jit(solution)/shard_map/all_to_all | solution.py:494
  431.5 45.3 %shard_map.227 = (bf16[6,197,768]{2,1,0:T(8,128)(2,1)}, bf16[6,208,768]{2,1,0:T(8,128)(2,1)}, bf16[6,208,2304]{2,1,0:T(8,128)(2,1)}, f32[8,768]{1,0:T(8,128)}) custom-call(s32[6,208,4]{2,1,0:T(8,128)} %pad_bitcast_fusion.refs_0_.codes_ref, bf16[1536,768]{1,0:T(8,128)(2,1)} %bitcast.13.refs_1_, bf16[1536,768]{1,0:T(8,128)(2,1)} %bitcast.14.refs_2_, ...), custom_call_target="tpu_custom_call" | custom-call | flops 15764815872 | bytes 32440320 | tf_op jit(solution)/shard_map/pallas_call | solution.py:406
  476.8 0.7 fusion.7
  477.9 4.0 bitcast_convert_fusion.1
  482.2 5.1 bitcast_convert_fusion
  487.8 1.7 dynamic-slice_bitcast_fusion
  489.5 1.2 copy-done.8
  490.7 5.0 collective-permute-done
  495.8 2.9 convert_add_fusion
  498.7 2.2 copy-done.9
  500.9 1.2 fusion.3
  502.1 1.5 collective-permute-start.1
  503.5 4.4 all-to-all-start.6
  508.0 23.5 %collective-permute-done.1 = bf16[192,3200]{1,0:T(8,128)(2,1)} collective-permute-done((bf16[192,3200]{1,0:T(8,128)(2,1)}, bf16[192,3200]{1,0:T(8,128)(2,1)}, u32[]{:S(2)}, u32[]{:S(2)}) %collective-permute-start.1) | collective-permute-done | bytes 1228832 | tf_op jit(solution)/shard_map/ppermute | solution.py:480
  531.4 3.3 fusion
  534.8 27.3 %all-to-all-done.6 = bf16[8,192,768]{2,1,0:T(8,128)(2,1)} async-done(((bf16[8,192,768]{2,1,0:T(8,128)(2,1)}), bf16[8,192,768]{2,1,0:T(8,128)(2,1)}, u32[]{:S(2)}, u32[]{:S(2)}) %all-to-all-start.6) | async-done | bytes 2359328 | tf_op jit(solution)/shard_map/all_to_all | solution.py:494
  562.1 33.7 %all_to_all.45 = bf16[8,24,3200]{2,1,0:T(8,128)(2,1)} all-to-all(bf16[8,24,3200]{2,1,0:T(8,128)(2,1)} %bitcast.78), channel_id=1, replica_groups=mesh['expert'=8,'shard'=4] {'expert'}, dimensions={0} | all-to-all | bytes 2457600 | tf_op jit(solution)/shard_map/all_to_all | solution.py:494
  595.8 1.5 reduce_sum.12
  597.3 1.1 broadcast_in_dim.25
  598.4 4.4 all-to-all-start.8
  602.9 2.1 copy-done.5
  604.9 9.3 %shard_map.228 = bf16[6,197,768]{2,1,0:T(8,128)(2,1)} custom-call(s32[6,208,4]{2,1,0:T(8,128)S(1)} %copy-done, bf16[1536,768]{1,0:T(8,128)(2,1)S(1)} %bitcast.69, bf16[1536,768]{1,0:T(8,128)(2,1)} %bitcast.24.refs_1_, f32[6,208,768]{2,1,0:T(8,128)S(1)} %copy-done.5), custom_call_target="tpu_custom_call" | custom-call | flops 5888802816 | bytes 7667712 | tf_op jit(solution)/shard_map/pallas_call | solution.py:448
  614.2 17.3 %all-to-all-done.8 = bf16[8,24,3200]{2,1,0:T(8,128)(2,1)} async-done(((bf16[8,24,3200]{2,1,0:T(8,128)(2,1)}), bf16[8,24,3200]{2,1,0:T(8,128)(2,1)}, u32[]{:S(2)}, u32[]{:S(2)}) %all-to-all-start.8) | async-done | bytes 1228832 | tf_op jit(solution)/shard_map/all_to_all | solution.py:494
  631.5 1.4 bitcast_convert_fusion.2
  632.9 1.3 slice.47
  634.3 0.9 slice.48
  635.8 0.9 slice_reduce_fusion
  636.7 1.4 bitcast_convert_fusion.3
  638.2 3.8 copy.133
  642.0 1.4 bitcast_convert_fusion.4
  643.4 3.8 copy.132
  (92 shorter events, 6.2 us)
Async XLA Ops:
  7.2 55.5 %all-gather.6.cloned.1.call-start = ((), (), s32[]{:S(2)}) async-start(), calls=%async_computation.11 | async-start | bytes 6144000 | tf_op jit(solution)/shard_map/all_gather | solution.py:541
  8.7 11.2 %copy-start.22 = (bf16[192]{0:T(256)(128)(2,1)S(1)}, bf16[192]{0:T(256)(128)(2,1)}, u32[]{:S(2)}) copy-start(bf16[192]{0:T(256)(128)(2,1)} %param.15) | copy-start | bytes 1156
  8.7 11.2 %copy-start.23 = (bf16[192]{0:T(256)(128)(2,1)S(1)}, bf16[192]{0:T(256)(128)(2,1)}, u32[]{:S(2)}) copy-start(bf16[192]{0:T(256)(128)(2,1)} %param.16) | copy-start | bytes 1156
  8.7 11.2 %copy-start.24 = (bf16[192]{0:T(256)(128)(2,1)S(1)}, bf16[192]{0:T(256)(128)(2,1)}, u32[]{:S(2)}) copy-start(bf16[192]{0:T(256)(128)(2,1)} %param.19) | copy-start | bytes 1156
  8.7 11.2 %copy-start.25 = (bf16[192]{0:T(256)(128)(2,1)S(1)}, bf16[192]{0:T(256)(128)(2,1)}, u32[]{:S(2)}) copy-start(bf16[192]{0:T(256)(128)(2,1)} %param.20) | copy-start | bytes 1156
  8.7 11.2 %copy-start.21 = (bf16[192,8]{0,1:T(8,128)(2,1)S(1)}, bf16[192,8]{0,1:T(8,128)(2,1)}, u32[]{:S(2)}) copy-start(bf16[192,8]{0,1:T(8,128)(2,1)} %param.21) | copy-start | bytes 9220
  8.7 11.4 %copy-start.14 = (bf16[192,2304]{1,0:T(8,128)(2,1)S(1)}, bf16[192,2304]{1,0:T(8,128)(2,1)}, u32[]{:S(2)}) copy-start(bf16[192,2304]{1,0:T(8,128)(2,1)} %param.17) | copy-start | bytes 2654212
  8.7 11.4 %copy-start.17 = (bf16[192,768]{1,0:T(8,128)(2,1)S(1)}, bf16[192,768]{1,0:T(8,128)(2,1)}, u32[]{:S(2)}) copy-start(bf16[192,768]{1,0:T(8,128)(2,1)} %param.18) | copy-start | bytes 884740
  21.2 175.7 %all-gather.10.cloned.1.call-start = ((), (), s32[]{:S(2)}) async-start(), calls=%async_computation.15 | async-start | bytes 5898240 | tf_op jit(solution)/shard_map/all_gather | solution.py:557
  22.0 8.2 %copy-start.18 = (s32[6,197,2]{1,2,0:T(2,128)S(1)}, s32[6,197,2]{1,2,0:T(2,128)}, u32[]{:S(2)}) copy-start(s32[6,197,2]{1,2,0:T(2,128)} %param.25) | copy-start | bytes 28372
  22.0 8.2 %copy-start.19 = (s32[6,197,2]{1,2,0:T(2,128)S(1)}, s32[6,197,2]{1,2,0:T(2,128)}, u32[]{:S(2)}) copy-start(s32[6,197,2]{1,2,0:T(2,128)} %param.24) | copy-start | bytes 28372
  22.0 8.2 %copy-start.20 = (s32[6,197,2]{1,2,0:T(2,128)S(1)}, s32[6,197,2]{1,2,0:T(2,128)}, u32[]{:S(2)}) copy-start(s32[6,197,2]{1,2,0:T(2,128)} %param.26) | copy-start | bytes 28372
  22.0 41.8 %copy-start.2 = (bf16[6,197,768]{2,1,0:T(8,128)(2,1)S(1)}, bf16[6,197,768]{2,1,0:T(8,128)(2,1)}, u32[]{:S(2)}) copy-start(bf16[6,197,768]{2,1,0:T(8,128)(2,1)} %refs_4_.1) | copy-start | bytes 5446660
  22.0 111.9 %all-to-all-start.2 = ((bf16[8,384,768]{2,1,0:T(8,128)(2,1)}), bf16[8,384,768]{2,1,0:T(8,128)(2,1)}, u32[]{:S(2)}, u32[]{:S(2)}) async-start(bf16[8,384,768]{2,1,0:T(8,128)(2,1)} %shard_map.221), calls=%async_computation.2 | async-start | bytes 9437184 | tf_op jit(solution)/shard_map/all_to_all | solution.py:494
  29.4 167.5 %all-gather.8.cloned.1.call-start = ((), (), s32[]{:S(2)}) async-start(), calls=%async_computation.14 | async-start | bytes 5898240 | tf_op jit(solution)/shard_map/all_gather | solution.py:556
  63.9 19.7 %copy-start.1 = (f32[8,768]{1,0:T(8,128)}, f32[8,768]{1,0:T(8,128)S(1)}, u32[]{:S(2)}) copy-start(f32[8,768]{1,0:T(8,128)S(1)} %pad_convert_fusion.vector_ref.refs_9_) | copy-start | bytes 73732
  83.5 1.3 copy-start.3
  84.8 1.3 copy-start.4
  86.1 1.3 copy-start.6
  134.0 57.7 %all-to-all-start.1 = ((bf16[8,192,768]{2,1,0:T(8,128)(2,1)}), bf16[8,192,768]{2,1,0:T(8,128)(2,1)S(1)}, u32[]{:S(2)}, u32[]{:S(2)}) async-start(bf16[8,192,768]{2,1,0:T(8,128)(2,1)} %shard_map.224), calls=%async_computation.1 | async-start | bytes 4718592 | tf_op jit(solution)/shard_map/all_to_all | solution.py:494
  191.6 1.4 copy-start.12
  193.0 57.8 %all-to-all-start = ((bf16[8,192,768]{2,1,0:T(8,128)(2,1)}), bf16[8,192,768]{2,1,0:T(8,128)(2,1)S(1)}, u32[]{:S(2)}, u32[]{:S(2)}) async-start(bf16[8,192,768]{2,1,0:T(8,128)(2,1)} %shard_map.223), calls=%async_computation | async-start | bytes 4718592 | tf_op jit(solution)/shard_map/all_to_all | solution.py:494
  250.9 1.5 copy-start.10
  252.4 62.0 %all-to-all-start.3 = ((bf16[8,192,768]{2,1,0:T(8,128)(2,1)}), bf16[8,192,768]{2,1,0:T(8,128)(2,1)}, u32[]{:S(2)}, u32[]{:S(2)}) async-start(bf16[8,192,768]{2,1,0:T(8,128)(2,1)} %get-tuple-element.88), calls=%async_computation.3 | async-start | bytes 4718592 | tf_op jit(solution)/shard_map/all_to_all | solution.py:494
  314.4 7.7 %copy-start.13 = (bf16[8,192,768]{2,1,0:T(8,128)(2,1)S(1)}, bf16[8,192,768]{2,1,0:T(8,128)(2,1)}, u32[]{:S(2)}) copy-start(bf16[8,192,768]{2,1,0:T(8,128)(2,1)} %copy-done.12) | copy-start | bytes 7077892
  314.4 7.7 %copy-start.16 = (bf16[1536,128]{1,0:T(8,128)(2,1)S(1)}, bf16[1536,128]{1,0:T(8,128)(2,1)}, u32[]{:S(2)}) copy-start(bf16[1536,128]{1,0:T(8,128)(2,1)} %get-tuple-element.97) | copy-start | bytes 1179652
  314.5 59.3 %all-to-all-start.4 = ((bf16[8,192,768]{2,1,0:T(8,128)(2,1)}), bf16[8,192,768]{2,1,0:T(8,128)(2,1)}, u32[]{:S(2)}, u32[]{:S(2)}) async-start(bf16[8,192,768]{2,1,0:T(8,128)(2,1)} %get-tuple-element.102), calls=%async_computation.4 | async-start | bytes 4718592 | tf_op jit(solution)/shard_map/all_to_all | solution.py:494
  321.2 1.9 copy-start.11
  321.2 1.9 copy-start.15
  373.8 57.7 %all-to-all-start.5 = ((bf16[8,192,768]{2,1,0:T(8,128)(2,1)}), bf16[8,192,768]{2,1,0:T(8,128)(2,1)S(1)}, u32[]{:S(2)}, u32[]{:S(2)}) async-start(bf16[8,192,768]{2,1,0:T(8,128)(2,1)} %get-tuple-element.105), calls=%async_computation.5 | async-start | bytes 4718592 | tf_op jit(solution)/shard_map/all_to_all | solution.py:494
  377.4 259.3 %reduce-scatter.5.cloned.1.call-start = ((), (), s32[]{:S(2)}) async-start(), calls=%async_computation.13 | async-start | bytes 5898240 | tf_op jit(solution)/shard_map/reduce_scatter | solution.py:594
  377.5 11.3 %copy-start.26 = (bf16[1536,768]{1,0:T(8,128)(2,1)S(1)}, bf16[1536,768]{1,0:T(8,128)(2,1)}, u32[]{:S(2)}) copy-start(bf16[1536,768]{1,0:T(8,128)(2,1)} %get-tuple-element.92) | copy-start | bytes 7077892
  477.7 4.2 slice-start
  477.9 4.1 copy-start.7
  477.9 4.3 slice-start.1
  487.8 3.0 copy-start.8
  490.7 5.0 collective-permute-start
  498.7 2.2 copy-start.9
  502.1 29.4 %collective-permute-start.1 = (bf16[192,3200]{1,0:T(8,128)(2,1)}, bf16[192,3200]{1,0:T(8,128)(2,1)}, u32[]{:S(2)}, u32[]{:S(2)}) collective-permute-start(bf16[192,3200]{1,0:T(8,128)(2,1)} %fusion.3), channel_id=1, source_target_pairs={{0,2},{1,3},{2,0},{3,1},{4,6},{5,7},{6,4},{7,5},{8,10},{9,11},{10,... | collective-permute-start | bytes 3686408 | tf_op jit(solution)/shard_map/ppermute | solution.py:480
  503.5 58.5 %all-to-all-start.6 = ((bf16[8,192,768]{2,1,0:T(8,128)(2,1)}), bf16[8,192,768]{2,1,0:T(8,128)(2,1)}, u32[]{:S(2)}, u32[]{:S(2)}) async-start(bf16[8,192,768]{2,1,0:T(8,128)(2,1)} %get-tuple-element.122), calls=%async_computation.6 | async-start | bytes 4718592 | tf_op jit(solution)/shard_map/all_to_all | solution.py:494
  507.9 134.1 %reduce-scatter.3.cloned.1.call-start = ((), (), s32[]{:S(2)}) async-start(), calls=%async_computation.12 | async-start | bytes 5898240 | tf_op jit(solution)/shard_map/reduce_scatter | solution.py:609
  595.8 7.1 %copy-start = (s32[6,208,4]{2,1,0:T(8,128)S(1)}, s32[6,208,4]{2,1,0:T(8,128)}, u32[]{:S(2)}) copy-start(s32[6,208,4]{2,1,0:T(8,128)} %pad_bitcast_fusion.refs_0_.codes_ref) | copy-start | bytes 59908
  598.4 33.1 %all-to-all-start.8 = ((bf16[8,24,3200]{2,1,0:T(8,128)(2,1)}), bf16[8,24,3200]{2,1,0:T(8,128)(2,1)}, u32[]{:S(2)}, u32[]{:S(2)}) async-start(bf16[8,24,3200]{2,1,0:T(8,128)(2,1)} %broadcast_in_dim.25), calls=%async_computation.8 | async-start | bytes 2457600 | tf_op jit(solution)/shard_map/all_to_all | solution.py:494
  602.9 2.1 copy-start.5
Sparse Core Ops, SparseCore 0:
  21.4 41.2 all-gather.5
  64.2 37.4 all-gather.9
  103.3 37.4 all-gather.7
  431.6 46.9 reduce-scatter.4
  534.9 46.1 reduce-scatter.2

commit v7 on v6

--- a/solution.py
+++ b/solution.py
@@ -579,10 +579,6 @@
         if chunk:
             back, wide, returned = lax.optimization_barrier((back, wide, returned))
         returned.append(exchange(back).reshape(experts * count, width))
-    out_returned = []
-    for out in out_here:
-        out, returned, out_returned = lax.optimization_barrier((out, returned, out_returned))
-        out_returned.append(exchange(out).reshape(experts * count, width))
 
     down_full = sum(dot(active, scaled, TN) for active, _, scaled, _, _ in wide).astype(BF16)
     _, before, _, _, x = wide[-1]
@@ -591,6 +587,10 @@
     down_full, up_full, router_full, returned = lax.optimization_barrier(
         (down_full, up_full, router_full, returned)
     )
+    out_returned = []
+    for out in out_here:
+        out, _, _ = lax.optimization_barrier((out, returned, out_returned))
+        out_returned.append(exchange(out).reshape(experts * count, width))
     down_grad = lax.psum_scatter(down_full, "shard", scatter_dimension=0, tiled=True)
 
     tokens_grad, branch, rows_grad, sums = attend_back(

time: 662 us -> 606 us (0.915)
  waiting for transfers between devices: 264 us -> 205 us
    all_to_all x8, waiting for transfers between devices: 203 us -> 145 us  [exchange(): lax.all_to_all(array, 'expert', split_axis=0, concat_axis=0, tiled=True)]
  transfers between devices with their start and end apart: 15 -> 15, of which waited for: 10 -> 9; matrix products, arithmetic and copies ran while one was open for 14% -> 16% of each run, Pallas kernels for 27% -> 30%
where the time goes in v7:
time: 606 us; the launch traced here: 598 us
  waiting for transfers between devices  205 us (34%)
  Pallas kernels  188 us (31%)
  matrix products  63.2 us (10%)
  starting transfers between devices  41.9 us (7%)
  local copies, waits for them, and re-layouts  35.2 us (6%)
  blocking collectives  33.7 us (6%)
  other arithmetic  16.6 us (3%)
  between operations  14.5 us (2%)
    all_to_all x8, waiting for transfers between devices, exchange(): lax.all_to_all(array, 'expert', split_axis=0, concat_axis=0, tiled=True)  145 us
    pallas_call x2, Pallas kernels, run_expert(): pl.pallas_call(functools.partial(expert_kernel, experts, block), grid=(hi...  88.3 us
    dot_general x8, matrix products, dot(): return lax.dot_general(a, b, dims, preferred_element_type=F32)  63.2 us
    pallas_call x1, Pallas kernels, attend_back(): call(attend_back_kernel, (images // group,), [image(padded, codes.shape[2...  44.5 us
    all_to_all x8, starting transfers between devices, exchange(): lax.all_to_all(array, 'expert', split_axis=0, concat_axis=0, tiled=True)  40.2 us
    all_to_all x1, blocking collectives, exchange(): lax.all_to_all(array, 'expert', split_axis=0, concat_axis=0, tiled=True)  33.7 us
    all_gather x1, waiting for transfers between devices, shards(): weights = lax.all_gather(packed, 'shard', axis=0, tiled=True)  31.7 us
    pallas_call x3, Pallas kernels, send(): call(kernel, (experts,), [whole(codes.shape), whole(source.shape)], pl.Bl...  25.8 us
  transfers between devices with their start and end apart: 15, of which 9 were waited for; matrix products, arithmetic and copies ran while one was open for 16% of the time, Pallas kernels for 30%

profile of v7, /device:TPU:0, one launch (start us, length us, event | category | flops | bytes accessed | tf_op | source)
XLA Modules:
  0.0 598.1 jit_solution(11021365193066529687)
XLA Ops:
  7.2 0.8 compare_select_fusion
  8.7 11.1 %shard_map.221 = bf16[8,384,768]{2,1,0:T(8,128)(2,1)} custom-call(s32[2,1248]{1,0:T(2,128)} %reshape.74.codes_ref, bf16[6,197,768]{2,1,0:T(8,128)(2,1)} %refs_3_.1), custom_call_target="tpu_custom_call" | custom-call | flops 5888802816 | bytes 6635520 | tf_op jit(solution)/shard_map/pallas_call | solution.py:128
  20.1 1.1 fusion.2
  21.3 0.7 all-gather.10.cloned.1.call-update
  22.0 7.4 %all-to-all-start.2 = ((bf16[8,384,768]{2,1,0:T(8,128)(2,1)}), bf16[8,384,768]{2,1,0:T(8,128)(2,1)}, u32[]{:S(2)}, u32[]{:S(2)}) async-start(bf16[8,384,768]{2,1,0:T(8,128)(2,1)} %shard_map.221), calls=%async_computation.2 | async-start | bytes 9437184 | tf_op jit(solution)/shard_map/all_to_all | solution.py:494
  31.0 31.7 %all-gather.6.cloned.1.call-done.qkv_weight_ref.out_weight_ref.router_ref.refs_7_.refs_8_ = bf16[768,3200]{1,0:T(8,128)(2,1)} async-done(((bf16[192,3200]{1,0:T(8,128)(2,1)}), bf16[768,3200]{1,0:T(8,128)(2,1)}) %all-gather.6.cloned.1.call-update) | async-done | bytes 4915216 | tf_op jit(solution)/shard_map/all_gather | solution.py:541
  62.7 1.0 slice.42
  63.9 19.6 %shard_map.222 = (bf16[6,208,2304]{2,1,0:T(8,128)(2,1)}, bf16[6,208,768]{2,1,0:T(8,128)(2,1)S(1)}, f32[6,208,768]{2,1,0:T(8,128)}, bf16[6,208,768]{2,1,0:T(8,128)(2,1)S(1)}, bf16[6,208,768]{2,1,0:T(8,128)(2,1)S(1)}) custom-call(bf16[6,197,768]{2,1,0:T(8,128)(2,1)S(1)} %copy-done.2, ...), custom_call_target="tpu_custom_call" | custom-call | flops 7483686912 | bytes 21970944 | tf_op jit(solution)/shard_map/pallas_call | solution.py:191
  83.5 1.3 copy-done.3
  84.8 1.3 copy-done.4
  86.1 1.3 copy-done.6
  87.3 7.3 %shard_map.224 = bf16[8,192,768]{2,1,0:T(8,128)(2,1)} custom-call(s32[2,1248]{1,0:T(2,128)} %reshape.77.codes_ref, bf16[1248,768]{1,0:T(8,128)(2,1)} %bitcast.70), custom_call_target="tpu_custom_call" | custom-call | flops 2944401408 | bytes 4276224 | tf_op jit(solution)/shard_map/pallas_call | solution.py:128
  94.7 39.3 %all-to-all-done.2.g_ref = bf16[8,384,768]{2,1,0:T(8,128)(2,1)} async-done(((bf16[8,384,768]{2,1,0:T(8,128)(2,1)}), bf16[8,384,768]{2,1,0:T(8,128)(2,1)}, u32[]{:S(2)}, u32[]{:S(2)}) %all-to-all-start.2) | async-done | bytes 4718624 | tf_op jit(solution)/shard_map/all_to_all | solution.py:494
  134.0 3.6 all-to-all-start.1
  138.3 7.4 %shard_map.223 = bf16[8,192,768]{2,1,0:T(8,128)(2,1)} custom-call(s32[2,1248]{1,0:T(2,128)} %reshape.75.codes_ref, bf16[1248,768]{1,0:T(8,128)(2,1)} %bitcast.71), custom_call_target="tpu_custom_call" | custom-call | flops 2944401408 | bytes 4276224 | tf_op jit(solution)/shard_map/pallas_call | solution.py:128
  145.6 46.0 %all-to-all-done.1.x_ref = bf16[8,192,768]{2,1,0:T(8,128)(2,1)S(1)} async-done(((bf16[8,192,768]{2,1,0:T(8,128)(2,1)}), bf16[8,192,768]{2,1,0:T(8,128)(2,1)S(1)}, u32[]{:S(2)}, u32[]{:S(2)}) %all-to-all-start.1) | async-done | bytes 2359328 | tf_op jit(solution)/shard_map/all_to_all | solution.py:494
  191.6 1.4 copy-done.11
  193.0 3.8 all-to-all-start
  197.2 0.9 pad_bitcast_fusion.refs_0_.codes_ref
  198.7 44.2 %shard_map.225 = (bf16[8,192,768]{2,1,0:T(8,128)(2,1)}, bf16[1536,3072]{1,0:T(8,128)(2,1)}, bf16[1536,3072]{1,0:T(8,128)(2,1)}, bf16[1536,768]{1,0:T(8,128)(2,1)...) custom-call(f32[8,128]{1,0:T(8,128)} %iota.7.mine_ref, bf16[8,192,768]{2,1,0:T(8,128)(2,1)} %copy-done.11, ...), custom_call_target="tpu_custom_call" | custom-call | flops 28991029248 | bytes 37748736 | tf_op jit(solution)/shard_map/pallas_call | solution.py:301
  242.9 8.0 %all-to-all-done.x_ref = bf16[8,192,768]{2,1,0:T(8,128)(2,1)S(1)} async-done(((bf16[8,192,768]{2,1,0:T(8,128)(2,1)}), bf16[8,192,768]{2,1,0:T(8,128)(2,1)S(1)}, u32[]{:S(2)}, u32[]{:S(2)}) %all-to-all-start) | async-done | bytes 2359328 | tf_op jit(solution)/shard_map/all_to_all | solution.py:494
  250.9 1.4 copy-done.9
  252.2 4.8 all-to-all-start.3
  257.0 13.1 %fusion.8 = f32[3072,768]{1,0:T(8,128)} fusion(bf16[1536,3072]{1,0:T(8,128)(2,1)} %get-tuple-element.73, bf16[1536,768]{1,0:T(8,128)(2,1)} %bitcast.76), kind=kOutput, calls=%fused_computation.40 | convolution fusion | flops 7247757312 | bytes 21233664 | tf_op jit(solution)/shard_map/dot_general | solution.py:23
  270.1 44.1 %shard_map.226 = (bf16[8,192,768]{2,1,0:T(8,128)(2,1)}, bf16[1536,3072]{1,0:T(8,128)(2,1)}, bf16[1536,3072]{1,0:T(8,128)(2,1)}, bf16[1536,768]{1,0:T(8,128)(2,1)...) custom-call(f32[8,128]{1,0:T(8,128)} %iota.7.mine_ref, bf16[8,192,768]{2,1,0:T(8,128)(2,1)} %copy-done.9, ...), custom_call_target="tpu_custom_call" | custom-call | flops 28991029248 | bytes 37748736 | tf_op jit(solution)/shard_map/pallas_call | solution.py:301
  314.3 6.5 %all-to-all-start.4 = ((bf16[8,192,768]{2,1,0:T(8,128)(2,1)}), bf16[8,192,768]{2,1,0:T(8,128)(2,1)}, u32[]{:S(2)}, u32[]{:S(2)}) async-start(bf16[8,192,768]{2,1,0:T(8,128)(2,1)} %get-tuple-element.95), calls=%async_computation.4 | async-start | bytes 4718592 | tf_op jit(solution)/shard_map/all_to_all | solution.py:494
  320.8 0.8 fusion.10
  321.6 0.8 copy-done.10
  322.5 0.8 convolution_add_fusion
  323.3 14.7 %add_convert_fusion = bf16[3072,768]{1,0:T(8,128)(2,1)} fusion(f32[3072,768]{1,0:T(8,128)} %fusion.8, bf16[1536,3072]{1,0:T(8,128)(2,1)} %get-tuple-element.88, bf16[1536,768]{1,0:T(8,128)(2,1)S(1)} %bitcast.75), kind=kOutput, calls=%fused_computation | convolution fusion | flops 7252475904 | bytes 25952256 | tf_op jit(solution)/shard_map/dot_general | solution.py:23
  338.1 10.6 %fusion.9 = f32[3072,768]{1,0:T(8,128)S(1)} fusion(bf16[1536,3072]{1,0:T(8,128)(2,1)} %get-tuple-element.84, bf16[1536,768]{1,0:T(8,128)(2,1)S(1)} %copy-done.25), kind=kOutput, calls=%fused_computation.41 | convolution fusion | flops 7247757312 | bytes 21233664 | tf_op jit(solution)/shard_map/dot_general | solution.py:23
  348.7 14.0 %add_convert_fusion.1 = bf16[3072,768]{1,0:T(8,128)(2,1)} fusion(f32[3072,768]{1,0:T(8,128)S(1)} %fusion.9, bf16[1536,3072]{1,0:T(8,128)(2,1)} %get-tuple-element.86, bf16[1536,768]{1,0:T(8,128)(2,1)S(1)} %copy-done.26), kind=kOutput, calls=%fused_computation.1 | convolution fusion | flops 7252475904 | bytes 25952256 | tf_op jit(solution)/shard_map/dot_general | solution.py:23
  362.7 10.9 %all-to-all-done.4 = bf16[8,192,768]{2,1,0:T(8,128)(2,1)} async-done(((bf16[8,192,768]{2,1,0:T(8,128)(2,1)}), bf16[8,192,768]{2,1,0:T(8,128)(2,1)}, u32[]{:S(2)}, u32[]{:S(2)}) %all-to-all-start.4) | async-done | bytes 2359328 | tf_op jit(solution)/shard_map/all_to_all | solution.py:494
  373.6 3.6 all-to-all-start.5
  377.9 44.5 %shard_map.227 = (bf16[6,197,768]{2,1,0:T(8,128)(2,1)}, bf16[6,208,768]{2,1,0:T(8,128)(2,1)}, bf16[6,208,2304]{2,1,0:T(8,128)(2,1)}, f32[8,768]{1,0:T(8,128)}) custom-call(s32[6,208,4]{2,1,0:T(8,128)} %pad_bitcast_fusion.refs_0_.codes_ref, bf16[1536,768]{1,0:T(8,128)(2,1)} %bitcast.13.refs_1_, bf16[1536,768]{1,0:T(8,128)(2,1)} %bitcast.14.refs_2_, ...), custom_call_target="tpu_custom_call" | custom-call | flops 15764815872 | bytes 32440320 | tf_op jit(solution)/shard_map/pallas_call | solution.py:406
  422.4 0.7 fusion.7
  423.5 4.0 bitcast_convert_fusion.1
  427.7 5.2 bitcast_convert_fusion
  432.9 2.4 pad_maximum_fusion
  435.3 3.3 dynamic-slice_bitcast_fusion
  438.6 5.0 collective-permute-done
  443.6 2.9 convert_add_fusion
  446.6 2.2 copy-done.8
  448.8 1.2 fusion.3
  449.9 1.5 collective-permute-start.1
  451.5 6.0 %all-to-all-start.6 = ((bf16[8,192,768]{2,1,0:T(8,128)(2,1)}), bf16[8,192,768]{2,1,0:T(8,128)(2,1)}, u32[]{:S(2)}, u32[]{:S(2)}) async-start(bf16[8,192,768]{2,1,0:T(8,128)(2,1)} %get-tuple-element.112), calls=%async_computation.6 | async-start | bytes 4718592 | tf_op jit(solution)/shard_map/all_to_all | solution.py:494
  457.5 21.8 %collective-permute-done.1 = bf16[192,3200]{1,0:T(8,128)(2,1)} collective-permute-done((bf16[192,3200]{1,0:T(8,128)(2,1)}, bf16[192,3200]{1,0:T(8,128)(2,1)}, u32[]{:S(2)}, u32[]{:S(2)}) %collective-permute-start.1) | collective-permute-done | bytes 1228832 | tf_op jit(solution)/shard_map/ppermute | solution.py:480
  479.3 3.3 fusion
  482.7 28.8 %all-to-all-done.6 = bf16[8,192,768]{2,1,0:T(8,128)(2,1)} async-done(((bf16[8,192,768]{2,1,0:T(8,128)(2,1)}), bf16[8,192,768]{2,1,0:T(8,128)(2,1)}, u32[]{:S(2)}, u32[]{:S(2)}) %all-to-all-start.6) | async-done | bytes 2359328 | tf_op jit(solution)/shard_map/all_to_all | solution.py:494
  511.4 33.7 %all_to_all.45 = bf16[8,24,3200]{2,1,0:T(8,128)(2,1)} all-to-all(bf16[8,24,3200]{2,1,0:T(8,128)(2,1)} %bitcast.78), channel_id=1, replica_groups=mesh['expert'=8,'shard'=4] {'expert'}, dimensions={0} | all-to-all | bytes 2457600 | tf_op jit(solution)/shard_map/all_to_all | solution.py:494
  545.2 1.5 reduce_sum.12
  546.7 1.1 broadcast_in_dim.25
  547.8 4.4 all-to-all-start.8
  552.3 2.1 copy-done.5
  554.3 9.3 %shard_map.228 = bf16[6,197,768]{2,1,0:T(8,128)(2,1)} custom-call(s32[6,208,4]{2,1,0:T(8,128)S(1)} %copy-done, bf16[1536,768]{1,0:T(8,128)(2,1)S(1)} %bitcast.69, bf16[1536,768]{1,0:T(8,128)(2,1)} %bitcast.24.refs_1_, f32[6,208,768]{2,1,0:T(8,128)S(1)} %copy-done.5), custom_call_target="tpu_custom_call" | custom-call | flops 5888802816 | bytes 7667712 | tf_op jit(solution)/shard_map/pallas_call | solution.py:448
  563.6 1.4 bitcast_convert_fusion.3
  565.1 3.8 copy.133
  568.9 12.0 %all-to-all-done.8 = bf16[8,24,3200]{2,1,0:T(8,128)(2,1)} async-done(((bf16[8,24,3200]{2,1,0:T(8,128)(2,1)}), bf16[8,24,3200]{2,1,0:T(8,128)(2,1)}, u32[]{:S(2)}, u32[]{:S(2)}) %all-to-all-start.8) | async-done | bytes 1228832 | tf_op jit(solution)/shard_map/all_to_all | solution.py:494
  580.9 1.4 bitcast_convert_fusion.2
  582.3 1.3 slice.47
  583.7 0.9 slice.48
  585.2 0.9 slice_reduce_fusion
  586.1 1.4 bitcast_convert_fusion.4
  587.6 3.8 copy.132
  (92 shorter events, 6.1 us)
Async XLA Ops:
  7.2 55.5 %all-gather.6.cloned.1.call-start = ((), (), s32[]{:S(2)}) async-start(), calls=%async_computation.11 | async-start | bytes 6144000 | tf_op jit(solution)/shard_map/all_gather | solution.py:541
  8.7 11.2 %copy-start.21 = (bf16[192]{0:T(256)(128)(2,1)S(1)}, bf16[192]{0:T(256)(128)(2,1)}, u32[]{:S(2)}) copy-start(bf16[192]{0:T(256)(128)(2,1)} %param.15) | copy-start | bytes 1156
  8.7 11.2 %copy-start.22 = (bf16[192]{0:T(256)(128)(2,1)S(1)}, bf16[192]{0:T(256)(128)(2,1)}, u32[]{:S(2)}) copy-start(bf16[192]{0:T(256)(128)(2,1)} %param.16) | copy-start | bytes 1156
  8.7 11.2 %copy-start.23 = (bf16[192]{0:T(256)(128)(2,1)S(1)}, bf16[192]{0:T(256)(128)(2,1)}, u32[]{:S(2)}) copy-start(bf16[192]{0:T(256)(128)(2,1)} %param.19) | copy-start | bytes 1156
  8.7 11.2 %copy-start.24 = (bf16[192]{0:T(256)(128)(2,1)S(1)}, bf16[192]{0:T(256)(128)(2,1)}, u32[]{:S(2)}) copy-start(bf16[192]{0:T(256)(128)(2,1)} %param.20) | copy-start | bytes 1156
  8.7 11.2 %copy-start.20 = (bf16[192,8]{0,1:T(8,128)(2,1)S(1)}, bf16[192,8]{0,1:T(8,128)(2,1)}, u32[]{:S(2)}) copy-start(bf16[192,8]{0,1:T(8,128)(2,1)} %param.21) | copy-start | bytes 9220
  8.7 11.4 %copy-start.13 = (bf16[192,2304]{1,0:T(8,128)(2,1)S(1)}, bf16[192,2304]{1,0:T(8,128)(2,1)}, u32[]{:S(2)}) copy-start(bf16[192,2304]{1,0:T(8,128)(2,1)} %param.17) | copy-start | bytes 2654212
  8.7 11.4 %copy-start.16 = (bf16[192,768]{1,0:T(8,128)(2,1)S(1)}, bf16[192,768]{1,0:T(8,128)(2,1)}, u32[]{:S(2)}) copy-start(bf16[192,768]{1,0:T(8,128)(2,1)} %param.18) | copy-start | bytes 884740
  21.2 176.9 %all-gather.10.cloned.1.call-start = ((), (), s32[]{:S(2)}) async-start(), calls=%async_computation.15 | async-start | bytes 5898240 | tf_op jit(solution)/shard_map/all_gather | solution.py:557
  22.0 8.2 %copy-start.17 = (s32[6,197,2]{1,2,0:T(2,128)S(1)}, s32[6,197,2]{1,2,0:T(2,128)}, u32[]{:S(2)}) copy-start(s32[6,197,2]{1,2,0:T(2,128)} %param.25) | copy-start | bytes 28372
  22.0 8.2 %copy-start.18 = (s32[6,197,2]{1,2,0:T(2,128)S(1)}, s32[6,197,2]{1,2,0:T(2,128)}, u32[]{:S(2)}) copy-start(s32[6,197,2]{1,2,0:T(2,128)} %param.24) | copy-start | bytes 28372
  22.0 8.2 %copy-start.19 = (s32[6,197,2]{1,2,0:T(2,128)S(1)}, s32[6,197,2]{1,2,0:T(2,128)}, u32[]{:S(2)}) copy-start(s32[6,197,2]{1,2,0:T(2,128)} %param.26) | copy-start | bytes 28372
  22.0 41.8 %copy-start.2 = (bf16[6,197,768]{2,1,0:T(8,128)(2,1)S(1)}, bf16[6,197,768]{2,1,0:T(8,128)(2,1)}, u32[]{:S(2)}) copy-start(bf16[6,197,768]{2,1,0:T(8,128)(2,1)} %refs_4_.1) | copy-start | bytes 5446660
  22.0 111.9 %all-to-all-start.2 = ((bf16[8,384,768]{2,1,0:T(8,128)(2,1)}), bf16[8,384,768]{2,1,0:T(8,128)(2,1)}, u32[]{:S(2)}, u32[]{:S(2)}) async-start(bf16[8,384,768]{2,1,0:T(8,128)(2,1)} %shard_map.221), calls=%async_computation.2 | async-start | bytes 9437184 | tf_op jit(solution)/shard_map/all_to_all | solution.py:494
  29.4 168.7 %all-gather.8.cloned.1.call-start = ((), (), s32[]{:S(2)}) async-start(), calls=%async_computation.14 | async-start | bytes 5898240 | tf_op jit(solution)/shard_map/all_gather | solution.py:556
  63.9 19.7 %copy-start.1 = (f32[8,768]{1,0:T(8,128)}, f32[8,768]{1,0:T(8,128)S(1)}, u32[]{:S(2)}) copy-start(f32[8,768]{1,0:T(8,128)S(1)} %pad_convert_fusion.vector_ref.refs_9_) | copy-start | bytes 73732
  83.5 1.3 copy-start.3
  84.8 1.3 copy-start.4
  86.1 1.3 copy-start.6
  134.0 57.7 %all-to-all-start.1 = ((bf16[8,192,768]{2,1,0:T(8,128)(2,1)}), bf16[8,192,768]{2,1,0:T(8,128)(2,1)S(1)}, u32[]{:S(2)}, u32[]{:S(2)}) async-start(bf16[8,192,768]{2,1,0:T(8,128)(2,1)} %shard_map.224), calls=%async_computation.1 | async-start | bytes 4718592 | tf_op jit(solution)/shard_map/all_to_all | solution.py:494
  191.6 1.4 copy-start.11
  193.0 57.8 %all-to-all-start = ((bf16[8,192,768]{2,1,0:T(8,128)(2,1)}), bf16[8,192,768]{2,1,0:T(8,128)(2,1)S(1)}, u32[]{:S(2)}, u32[]{:S(2)}) async-start(bf16[8,192,768]{2,1,0:T(8,128)(2,1)} %shard_map.223), calls=%async_computation | async-start | bytes 4718592 | tf_op jit(solution)/shard_map/all_to_all | solution.py:494
  250.9 1.4 copy-start.9
  252.2 62.0 %all-to-all-start.3 = ((bf16[8,192,768]{2,1,0:T(8,128)(2,1)}), bf16[8,192,768]{2,1,0:T(8,128)(2,1)}, u32[]{:S(2)}, u32[]{:S(2)}) async-start(bf16[8,192,768]{2,1,0:T(8,128)(2,1)} %get-tuple-element.83), calls=%async_computation.3 | async-start | bytes 4718592 | tf_op jit(solution)/shard_map/all_to_all | solution.py:494
  314.3 6.5 %copy-start.12 = (bf16[8,192,768]{2,1,0:T(8,128)(2,1)S(1)}, bf16[8,192,768]{2,1,0:T(8,128)(2,1)}, u32[]{:S(2)}) copy-start(bf16[8,192,768]{2,1,0:T(8,128)(2,1)} %copy-done.11) | copy-start | bytes 7077892
  314.3 6.5 %copy-start.15 = (bf16[1536,128]{1,0:T(8,128)(2,1)S(1)}, bf16[1536,128]{1,0:T(8,128)(2,1)}, u32[]{:S(2)}) copy-start(bf16[1536,128]{1,0:T(8,128)(2,1)} %get-tuple-element.92) | copy-start | bytes 1179652
  314.3 59.3 %all-to-all-start.4 = ((bf16[8,192,768]{2,1,0:T(8,128)(2,1)}), bf16[8,192,768]{2,1,0:T(8,128)(2,1)}, u32[]{:S(2)}, u32[]{:S(2)}) async-start(bf16[8,192,768]{2,1,0:T(8,128)(2,1)} %get-tuple-element.95), calls=%async_computation.4 | async-start | bytes 4718592 | tf_op jit(solution)/shard_map/all_to_all | solution.py:494
  320.8 1.7 copy-start.10
  320.8 1.7 copy-start.14
  323.3 14.7 %copy-start.25 = (bf16[1536,768]{1,0:T(8,128)(2,1)S(1)}, bf16[1536,768]{1,0:T(8,128)(2,1)}, u32[]{:S(2)}) copy-start(bf16[1536,768]{1,0:T(8,128)(2,1)} %get-tuple-element.85) | copy-start | bytes 7077892
  338.1 10.6 %copy-start.26 = (bf16[1536,768]{1,0:T(8,128)(2,1)S(1)}, bf16[1536,768]{1,0:T(8,128)(2,1)}, u32[]{:S(2)}) copy-start(bf16[1536,768]{1,0:T(8,128)(2,1)} %get-tuple-element.87) | copy-start | bytes 7077892
  373.6 61.7 %all-to-all-start.5 = ((bf16[8,192,768]{2,1,0:T(8,128)(2,1)}), bf16[8,192,768]{2,1,0:T(8,128)(2,1)S(1)}, u32[]{:S(2)}, u32[]{:S(2)}) async-start(bf16[8,192,768]{2,1,0:T(8,128)(2,1)} %get-tuple-element.106), calls=%async_computation.5 | async-start | bytes 4718592 | tf_op jit(solution)/shard_map/all_to_all | solution.py:494
  377.3 186.3 %reduce-scatter.5.cloned.1.call-start = ((), (), s32[]{:S(2)}) async-start(), calls=%async_computation.13 | async-start | bytes 5898240 | tf_op jit(solution)/shard_map/reduce_scatter | solution.py:594
  423.3 4.2 slice-start
  423.5 4.0 copy-start.7
  423.5 4.3 slice-start.1
  438.6 5.0 collective-permute-start
  446.6 2.2 copy-start.8
  449.9 29.4 %collective-permute-start.1 = (bf16[192,3200]{1,0:T(8,128)(2,1)}, bf16[192,3200]{1,0:T(8,128)(2,1)}, u32[]{:S(2)}, u32[]{:S(2)}) collective-permute-start(bf16[192,3200]{1,0:T(8,128)(2,1)} %fusion.3), channel_id=1, source_target_pairs={{0,2},{1,3},{2,0},{3,1},{4,6},{5,7},{6,4},{7,5},{8,10},{9,11},{10,... | collective-permute-start | bytes 3686408 | tf_op jit(solution)/shard_map/ppermute | solution.py:480
  451.5 60.0 %all-to-all-start.6 = ((bf16[8,192,768]{2,1,0:T(8,128)(2,1)}), bf16[8,192,768]{2,1,0:T(8,128)(2,1)}, u32[]{:S(2)}, u32[]{:S(2)}) async-start(bf16[8,192,768]{2,1,0:T(8,128)(2,1)} %get-tuple-element.112), calls=%async_computation.6 | async-start | bytes 4718592 | tf_op jit(solution)/shard_map/all_to_all | solution.py:494
  457.4 128.7 %reduce-scatter.3.cloned.1.call-start = ((), (), s32[]{:S(2)}) async-start(), calls=%async_computation.12 | async-start | bytes 5898240 | tf_op jit(solution)/shard_map/reduce_scatter | solution.py:609
  545.1 7.1 %copy-start = (s32[6,208,4]{2,1,0:T(8,128)S(1)}, s32[6,208,4]{2,1,0:T(8,128)}, u32[]{:S(2)}) copy-start(s32[6,208,4]{2,1,0:T(8,128)} %pad_bitcast_fusion.refs_0_.codes_ref) | copy-start | bytes 59908
  547.8 33.1 %all-to-all-start.8 = ((bf16[8,24,3200]{2,1,0:T(8,128)(2,1)}), bf16[8,24,3200]{2,1,0:T(8,128)(2,1)}, u32[]{:S(2)}, u32[]{:S(2)}) async-start(bf16[8,24,3200]{2,1,0:T(8,128)(2,1)} %broadcast_in_dim.25), calls=%async_computation.8 | async-start | bytes 2457600 | tf_op jit(solution)/shard_map/all_to_all | solution.py:494
  552.2 2.1 copy-start.5
Sparse Core Ops, SparseCore 0:
  21.4 41.2 all-gather.5
  64.2 37.4 all-gather.9
  103.3 37.4 all-gather.7
  380.3 49.2 reduce-scatter.4
  482.8 49.2 reduce-scatter.2
